TPU v7x, 512 devices: a whole 4x8x8 slice. The times are simulated.
512 devices in a mesh: tile: 32 (over y, x), chan: 16 (over z, core).
Axes of the slice: x: 4, y: 8, z: 8, core: 2. Of those that a mesh axis runs over, the one named last changes fastest.
Arguments:
- ensemble: bfloat16 [12288, 128, 256], P('tile', 'chan'), may hold values from -6 to 6
- jacobian: bfloat16 [5120, 512, 128], P('tile', 'chan'), may hold values from -1 to 1
- innovation: float32 [5120, 512], P('tile', 'chan'), may hold values from -6 to 6
- error_vectors: float32 [512, 32], replicated, may hold values from -1 to 1, as said below
- error_values: float32 [512], replicated, may hold values from 0.25 to 4
- ensemble_vectors: float32 [256, 256], replicated, may hold values from -1 to 1, as said below
- column_pick: int32 [32, 5, 40], P('tile'), may hold values from 0 to 383
- footprint_slot: int32 [5120], P('tile'), may hold values from 0 to 199, as said below
- footprint_count: int32 [32], P('tile'), may hold values from 20 to 160, as said below
Outputs:
- analysis: bfloat16 [12288, 128, 256], P('tile', 'chan')
Inputs may be any that keep to these rules, and one draw needn't show every extreme that they name: `footprint_slot`: the 160 entries of one pack are distinct; slot o * 40 + j is the j-th column that tile (pack + 2 - o) mod 32 sends to this pack. `footprint_count`: some pack has all 160 footprints live. `error_vectors`: each block of 32 rows is an orthogonal matrix. `ensemble_vectors`: an orthogonal matrix.
All inputs are finite; a program needn't handle non-finite values.
Results may differ from a plain program's by a relative error of at most 0.013.
Values may be sent and summed in bfloat16 or wider, within the bound.
No kernel may reach another device: no remote copies, remote signals or barrier semaphores. Data moves between devices by JAX's collectives and lax.ppermute only.
A program may use at most 64 MiB of HBM per device.

v0:
```python
import jax
import jax.numpy as jnp
from jax import lax
from jax.sharding import Mesh
from jax.sharding import PartitionSpec as P

TILE = ("tile_0", "tile_1")
CHAN = ("chan_0", "chan_1")


def from_behind(value, axis, steps):
    count = lax.axis_size(axis)
    pairs = [(source, (source + steps) % count) for source in range(count)]
    return lax.ppermute(value, axis, pairs)


def rows_for(lines, peers):
    spare = -lines.shape[0] % peers
    if not spare:
        return lines
    return jnp.concatenate([lines, jnp.zeros((spare, *lines.shape[1:]), lines.dtype)])


def from_everyone(x, axis):
    peers = lax.axis_size(axis)
    return lax.all_to_all(jnp.broadcast_to(x[None], (peers, *x.shape)), axis, 0, 0, tiled=True)


def laid_out(parts, dim):
    parts = jnp.moveaxis(parts, 0, dim)
    lengths = parts.shape
    return parts.reshape(*lengths[:dim], lengths[dim] * lengths[dim + 1], *lengths[dim + 2 :])


def gathered_by_axis(x, axes, dim):
    far, near = axes
    parts = from_everyone(from_everyone(x, far), near)
    return laid_out(parts.swapaxes(0, 1).reshape(-1, *x.shape), dim)


def in_blocks(x, dim, peers):
    lengths = x.shape
    parts = x.reshape(*lengths[:dim], peers, lengths[dim] // peers, *lengths[dim + 1 :])
    return jnp.moveaxis(parts, dim, 0)


def sent_and_summed(x, axis, dim):
    peers = lax.axis_size(axis)
    parts = lax.all_to_all(in_blocks(x, dim, peers), axis, 0, 0, tiled=True)
    return jnp.sum(parts, axis=0)


def sum_in_two_steps(x, axes, dim):
    far, near = axes
    parts = in_blocks(x, dim, lax.axis_size(far))
    nearer = sent_and_summed(parts, near, dim + 1)
    arrived = lax.all_to_all(nearer, far, split_axis=0, concat_axis=0, tiled=True)
    return arrived.sum(axis=0)


def nested_sum(x, axes):
    padded = rows_for(x, lax.axis_size(axes[0]) * lax.axis_size(axes[1]))
    whole = gathered_by_axis(sum_in_two_steps(padded, axes, 0), axes, 0)
    return lax.slice_in_dim(whole, 0, len(x)).reshape(x.shape)


def packed_total(arrays, axis):
    ends = [0]
    for a in arrays:
        ends.append(ends[-1] + a.size)
    running = nested_sum(jnp.concatenate([a.ravel() for a in arrays]), axis)
    return tuple((running[b:e].reshape(a.shape) for a, b, e in zip(arrays, ends, ends[1:])))


def turn_blocks(values, vectors):
    row_count, channels, members = values.shape
    group_width = vectors.shape[1]
    grouped = values.reshape(row_count, channels // group_width, group_width, members)
    basis_blocks = vectors.reshape(channels // group_width, group_width, group_width)
    turned = jnp.einsum("gce,fgck->fgek", basis_blocks, grouped, precision=lax.Precision.HIGHEST)
    return turned.reshape(row_count, channels, members)


def turn_rows(values, vectors):
    row_count, channels = values.shape
    group_width = vectors.shape[1]
    grouped = values.reshape(row_count, channels // group_width, group_width)
    basis_blocks = vectors.reshape(channels // group_width, group_width, group_width)
    turned = jnp.einsum("gce,fgc->fge", basis_blocks, grouped, precision=lax.Precision.HIGHEST)
    return turned.reshape(row_count, channels)


def local(
    ensemble,
    jacobian,
    innovation,
    error_vectors,
    error_values,
    ensemble_vectors,
    column_pick,
    footprint_slot,
    footprint_count,
):
    window = column_pick.shape[1]
    capacity = column_pick.shape[2]
    reach_tiles = window // 2
    level_part = ensemble.shape[1]
    members = ensemble.shape[2]
    chosen = jnp.take(ensemble, column_pick[0].reshape(-1), axis=0).reshape(
        window, capacity, level_part, members
    )
    blocks = []
    for slot_index in range(window):
        shift_by = slot_index - reach_tiles
        if shift_by == 0:
            blocks.append(chosen[slot_index])
        else:
            blocks.append(from_behind(chosen[slot_index], TILE, shift_by))
    arrived = jnp.stack(blocks, 0)
    slot_rows = arrived.reshape(window * capacity, level_part, members)
    columns = jnp.take(slot_rows, footprint_slot, axis=0)
    foot_rows = columns.shape[0]
    live_rows = (jnp.arange(foot_rows, dtype=jnp.int32) < footprint_count[0]).astype(jnp.float32)
    share_rows = foot_rows // lax.axis_size(CHAN)
    columns, sensitivity, misfit_rows = (
        lax.all_to_all(columns, CHAN, split_axis=0, concat_axis=1, tiled=True),
        lax.all_to_all(jacobian, CHAN, split_axis=0, concat_axis=1, tiled=True),
        lax.all_to_all(
            innovation.astype(jnp.bfloat16), CHAN, split_axis=0, concat_axis=1, tiled=True
        ).astype(innovation.dtype),
    )
    response = jnp.einsum("fcl,flk->fck", sensitivity, columns, preferred_element_type=jnp.float32)
    row_weights = lax.dynamic_slice_in_dim(
        live_rows, lax.axis_index(CHAN) * share_rows, share_rows, 0
    )
    scales = 1.0 / jnp.sqrt(error_values)
    whitened = (
        turn_blocks(response, error_vectors) * scales[None, :, None] * row_weights[:, None, None]
    )
    misfit = turn_rows(misfit_rows, error_vectors) * scales[None, :]
    pull_sum = jnp.einsum("fck,fc->k", whitened, misfit, precision=lax.Precision.HIGHEST)
    rounded = whitened.astype(jnp.bfloat16).reshape(-1, members)
    gram_sum = lax.dot_general(
        rounded, rounded, (((0,), (0,)), ((), ())), preferred_element_type=jnp.float32
    )
    gram_sum, pull_sum = packed_total(
        (gram_sum, pull_sum), ("tile_0", ("tile_1", "chan_0", "chan_1"))
    )
    system = gram_sum + (members - 1) * jnp.eye(members, dtype=jnp.float32)
    factor = jnp.linalg.cholesky(system)
    halfway = lax.linalg.triangular_solve(factor, pull_sum[:, None], left_side=True, lower=True)
    mean_weights = lax.linalg.triangular_solve(
        factor, halfway, left_side=True, lower=True, transpose_a=True
    )[:, 0]
    spread = jnp.sqrt(members - 1.0) * lax.linalg.triangular_solve(
        factor, ensemble_vectors, left_side=True, lower=True, transpose_a=True
    )
    transform = (spread + mean_weights[:, None]).astype(jnp.bfloat16)
    flat_rows = ensemble.reshape(-1, members)
    updated = jnp.dot(flat_rows, transform, preferred_element_type=jnp.float32).astype(jnp.bfloat16)
    return updated.reshape(ensemble.shape)


def solution(mesh):
    finer = Mesh(mesh.devices.reshape(8, 4, 8, 2), ("tile_0", "tile_1", "chan_0", "chan_1"))
    return jax.shard_map(
        local,
        mesh=finer,
        in_specs=(
            P(TILE, CHAN, None),
            P(TILE, CHAN, None),
            P(TILE, CHAN),
            P(),
            P(),
            P(),
            P(TILE, None, None),
            P(TILE),
            P(TILE),
        ),
        out_specs=P(TILE, CHAN, None),
        check_vma=False,
    )
```

profile of v0, /device:TPU:1, one launch (start us, length us, event | category | flops | bytes accessed | tf_op | source)
XLA Modules:
  0.0 243.2 jit_solution(3746167553359581715)
XLA Ops:
  0.0 0.9 convert_element_type.24
  1.0 0.7 reshape.210
  1.7 11.8 %all-to-all-start.2 = ((bf16[16,2,160]{2,1,0:T(2,128)(2,1)}), bf16[16,2,160]{2,1,0:T(2,128)(2,1)S(1)}, u32[]{:S(2)}, u32[]{:S(2)}) async-start(bf16[16,2,160]{2,1,0:T(2,128)(2,1)} %reshape.210), calls=%async_computation.2 | async-start | bytes 32768 | tf_op jit(solution)/shard_map/all_to_all | solution.py:128
  13.6 0.7 reduce.13
  14.5 1.7 gather_fusion
  16.2 4.7 %all-to-all-done.2 = bf16[16,2,160]{2,1,0:T(2,128)(2,1)S(1)} async-done(((bf16[16,2,160]{2,1,0:T(2,128)(2,1)}), bf16[16,2,160]{2,1,0:T(2,128)(2,1)S(1)}, u32[]{:S(2)}, u32[]{:S(2)}) %all-to-all-start.2) | async-done | bytes 10272 | tf_op jit(solution)/shard_map/all_to_all | solution.py:128
  20.9 3.9 %all-to-all-start.1 = ((bf16[160,32,128]{2,1,0:T(8,128)(2,1)}), bf16[160,32,128]{2,1,0:T(8,128)(2,1)S(1)}, u32[]{:S(2)}, u32[]{:S(2)}) async-start(bf16[160,32,128]{2,1,0:T(8,128)(2,1)} %param.10), calls=%async_computation.1 | async-start | bytes 2621440 | tf_op jit(solution)/shard_map/all_to_all | solution.py:127
  24.8 1.4 broadcast_select_fusion
  26.3 7.6 %collective-permute-start = (bf16[40,8,256]{2,1,0:T(8,128)(2,1)S(1)}, bf16[40,8,256]{2,1,0:T(8,128)(2,1)S(1)}, u32[]{:S(2)}, u32[]{:S(2)}) collective-permute-start(bf16[40,8,256]{2,1,0:T(8,128)(2,1)S(1)} %get-tuple-element.42), channel_id=1, source_target_pairs={{0,480},{16,496},{32,0},{48,16},{64,32},{80,48},{96,64},{112,80},{... | collective-permute-start | bytes 491528 | tf_op jit(solution)/shard_map/ppermute | solution.py:14
  33.8 2.8 %collective-permute-start.1 = (bf16[40,8,256]{2,1,0:T(8,128)(2,1)S(1)}, bf16[40,8,256]{2,1,0:T(8,128)(2,1)S(1)}, u32[]{:S(2)}, u32[]{:S(2)}) collective-permute-start(bf16[40,8,256]{2,1,0:T(8,128)(2,1)S(1)} %get-tuple-element.41), channel_id=1, source_target_pairs={{0,496},{16,0},{32,16},{48,32},{64,48},{80,64},{96,80},{112,96},{1... | collective-permute-start | bytes 491528 | tf_op jit(solution)/shard_map/ppermute | solution.py:14
  36.6 2.5 %collective-permute-start.2 = (bf16[40,8,256]{2,1,0:T(8,128)(2,1)S(1)}, bf16[40,8,256]{2,1,0:T(8,128)(2,1)S(1)}, u32[]{:S(2)}, u32[]{:S(2)}) collective-permute-start(bf16[40,8,256]{2,1,0:T(8,128)(2,1)S(1)} %get-tuple-element.40), channel_id=1, source_target_pairs={{0,16},{16,32},{32,48},{48,64},{64,80},{80,96},{96,112},{112,128},... | collective-permute-start | bytes 491528 | tf_op jit(solution)/shard_map/ppermute | solution.py:14
  39.1 2.6 %collective-permute-start.3 = (bf16[40,8,256]{2,1,0:T(8,128)(2,1)S(1)}, bf16[40,8,256]{2,1,0:T(8,128)(2,1)S(1)}, u32[]{:S(2)}, u32[]{:S(2)}) collective-permute-start(bf16[40,8,256]{2,1,0:T(8,128)(2,1)S(1)} %get-tuple-element.39), channel_id=1, source_target_pairs={{0,32},{16,48},{32,64},{48,80},{64,96},{80,112},{96,128},{112,144}... | collective-permute-start | bytes 491528 | tf_op jit(solution)/shard_map/ppermute | solution.py:14
  41.7 0.6 compare_and_fusion.1
  42.3 0.6 pad_clamp_fusion
  43.0 3.8 %collective-permute-done.2 = bf16[40,8,256]{2,1,0:T(8,128)(2,1)S(1)} collective-permute-done((bf16[40,8,256]{2,1,0:T(8,128)(2,1)S(1)}, bf16[40,8,256]{2,1,0:T(8,128)(2,1)S(1)}, u32[]{:S(2)}, u32[]{:S(2)}) %collective-permute-start.2) | collective-permute-done | bytes 163872 | tf_op jit(solution)/shard_map/ppermute | solution.py:14
  46.8 3.0 %collective-permute-done.3 = bf16[40,8,256]{2,1,0:T(8,128)(2,1)S(1)} collective-permute-done((bf16[40,8,256]{2,1,0:T(8,128)(2,1)S(1)}, bf16[40,8,256]{2,1,0:T(8,128)(2,1)S(1)}, u32[]{:S(2)}, u32[]{:S(2)}) %collective-permute-start.3) | collective-permute-done | bytes 163872 | tf_op jit(solution)/shard_map/ppermute | solution.py:14
  49.8 0.9 copy-done.3
  50.7 2.0 gather_fusion.1
  52.7 1.7 broadcast_select_fusion.1
  54.5 3.5 %all-to-all-done.1 = bf16[160,32,128]{2,1,0:T(8,128)(2,1)S(1)} async-done(((bf16[160,32,128]{2,1,0:T(8,128)(2,1)}), bf16[160,32,128]{2,1,0:T(8,128)(2,1)S(1)}, u32[]{:S(2)}, u32[]{:S(2)}) %all-to-all-start.1) | async-done | bytes 1310752 | tf_op jit(solution)/shard_map/all_to_all | solution.py:127
  58.0 5.7 %all-to-all-start = ((bf16[160,8,256]{2,1,0:T(8,128)(2,1)}), bf16[160,8,256]{2,1,0:T(8,128)(2,1)S(1)}, u32[]{:S(2)}, u32[]{:S(2)}) async-start(bf16[160,8,256]{2,1,0:T(8,128)(2,1)} %broadcast_select_fusion.1), calls=%async_computation | async-start | bytes 1310720 | tf_op jit(solution)/shard_map/all_to_all | solution.py:126
  64.3 1.3 sqrt.3
  65.6 1.3 mul.56
  67.0 1.7 reshape.150
  68.6 0.6 dynamic_slice.3
  69.2 0.7 reshape.211
  69.9 1.4 convolution_bitcast_fusion.1
  71.3 0.7 copy.74
  71.9 1.6 reshape.153
  73.5 1.4 multiply_bitcast_fusion
  74.9 1.6 copy.64
  76.5 7.2 %all-to-all-done = bf16[160,8,256]{2,1,0:T(8,128)(2,1)S(1)} async-done(((bf16[160,8,256]{2,1,0:T(8,128)(2,1)}), bf16[160,8,256]{2,1,0:T(8,128)(2,1)S(1)}, u32[]{:S(2)}, u32[]{:S(2)}) %all-to-all-start) | async-done | bytes 655392 | tf_op jit(solution)/shard_map/all_to_all | solution.py:126
  83.7 3.2 %convolution_bitcast_fusion = f32[10,512,256]{1,2,0:T(8,128)} fusion(bf16[10,512,128]{2,1,0:T(8,128)(2,1)S(1)} %bitcast.138, bf16[10,16,8,256]{3,2,0,1:T(8,128)(2,1)S(1)} %bitcast.140), kind=kOutput, calls=%fused_computation.14 | convolution fusion | flops 335544320 | bytes 7208960 | tf_op jit(solution)/shard_map/fcl,flk->fck/dot_general | solution.py:132
  86.9 5.9 %copy.66 = f32[10,512,256]{2,1,0:T(8,128)} copy(f32[10,512,256]{1,2,0:T(8,128)} %convolution_bitcast_fusion) | data formatting | bytes 10485760 | tf_op jit(solution)/shard_map/fcl,flk->fck/dot_general | solution.py:132
  92.9 7.1 %multiply_convert_fusion = (bf16[10,16,32,256]{3,2,0,1:T(8,128)(2,1)S(1)}, f32[10,16,32,256]{3,2,0,1:T(8,128)S(1)}) fusion(f32[10]{0:T(128)S(1)} %copy-done.8, f32[16,32]{1,0:T(8,128)S(1)} %copy-done.6, f32[16,32,32,1]{1,0,2,3:T(8,128)S(1)} %bitcast.141, f32[10,16,32,256]{3,2,1,0:T(8,128)} %bitcast.137), kind=kOutput, calls=%fused_computation.8 | convolution fusion | flops 507248640 | bytes 13174824 | tf_op jit(solution)/shard_map/gce,fgck->fgek/dot_general | solution.py:80
  100.0 0.8 copy.71
  100.8 1.0 fusion
  101.8 0.9 fusion.10
  102.9 2.6 %fusion.39 = f32[1,256,1]{1,0,2:T(1,128)S(1)} fusion(f32[10,512,256]{2,1,0:T(8,128)S(1)} %fusion, f32[10,512,1]{1,0,2:T(8,128)S(1)} %copy-done.5), kind=kOutput, calls=%fused_computation.72 | convolution fusion | flops 15728640 | bytes 5264384 | tf_op jit(solution)/shard_map/fck,fc->k/dot_general | solution.py:141
  105.6 0.6 reshape_reshape.6
  106.1 0.3 copy.75
  106.4 21.4 %all_to_all.77 = f32[64,8,129]{2,1,0:T(8,128)S(1)} all-to-all(f32[64,8,129]{2,1,0:T(8,128)S(1)} %copy.75), channel_id=1, replica_groups=mesh['tile_0'=8,'tile_1'=4,'chan_0'=8,'chan_1'=2] {'tile_1','chan_0','ch..., dimensions={0} | all-to-all | bytes 528384 | tf_op jit(solution)/shard_map/all_to_all | solution.py:49
  127.9 13.2 %all_to_all.78 = f32[8,1,129]{2,1,0:T(1,128)S(1)} all-to-all(f32[8,1,129]{2,1,0:T(1,128)S(1)} %all_to_all.66), channel_id=1, replica_groups=mesh['tile_0'=8,'tile_1'=4,'chan_0'=8,'chan_1'=2] {'tile_0'}, dimensions={0} | all-to-all | bytes 8256 | tf_op jit(solution)/shard_map/all_to_all | solution.py:57
  141.1 8.9 %all_to_all.79 = f32[8,1,129]{2,1,0:T(1,128)S(1)} all-to-all(f32[8,1,129]{2,1,0:T(1,128)S(1)} %broadcast_in_dim.51), channel_id=1, replica_groups=mesh['tile_0'=8,'tile_1'=4,'chan_0'=8,'chan_1'=2] {'tile_0'}, dimensions={0} | all-to-all | bytes 8256 | tf_op jit(solution)/shard_map/all_to_all | solution.py:26
  150.0 0.8 broadcast_in_dim.53
  150.9 9.1 %all-to-all-start.6 = ((f32[64,8,129]{2,1,0:T(8,128)}), f32[64,8,129]{2,1,0:T(8,128)S(1)}, u32[]{:S(2)}, u32[]{:S(2)}) async-start(f32[64,8,129]{2,1,0:T(8,128)} %broadcast_in_dim.53), calls=%async_computation.6 | async-start | bytes 1048576 | tf_op jit(solution)/shard_map/all_to_all | solution.py:26
  160.0 17.3 %all-to-all-done.6 = f32[64,8,129]{2,1,0:T(8,128)S(1)} async-done(((f32[64,8,129]{2,1,0:T(8,128)}), f32[64,8,129]{2,1,0:T(8,128)S(1)}, u32[]{:S(2)}, u32[]{:S(2)}) %all-to-all-start.6) | async-done | bytes 264224 | tf_op jit(solution)/shard_map/all_to_all | solution.py:26
  177.5 0.5 slice.104
  178.4 11.7 %cholesky.49 = f32[128,128]{1,0:T(8,128)S(1)} custom-call(f32[128,128]{1,0:T(8,128)S(1)} %cholesky.115), custom_call_target="Cholesky" | custom-call | tf_op jit(solution)/shard_map/jit(cholesky)/cholesky | solution.py:150
  190.1 9.8 %custom-call.18 = f32[1,128,128]{1,2,0:T(8,128)S(1)} custom-call(f32[1,128,128]{2,1,0:T(8,128)S(1)} %get-tuple-element.44), custom_call_target="InvertDiagBlocksLowerTriangular" | custom-call | tf_op jit(solution)/shard_map/jit(cholesky)/cholesky | solution.py:150
  200.2 0.3 convolution_subtract_fusion.1
  200.4 11.7 %cholesky.103 = f32[128,128]{1,0:T(8,128)S(1)} custom-call(f32[128,128]{1,0:T(8,128)S(1)} %convolution_subtract_fusion.1), custom_call_target="Cholesky" | custom-call | tf_op jit(solution)/shard_map/jit(cholesky)/cholesky | solution.py:150
  212.5 0.4 reshape_reshape.7
  212.9 0.6 compare_reduce_fusion
  214.9 4.0 %while.1 = (s32[]{:T(128)}, f32[256,256]{0,1:T(8,128)S(1)}, s32[2,2]{1,0:T(2,128)S(1)}, f32[2,128,128]{2,1,0:T(8,128)S(1)}, s32[]{:T(128)}) while((s32[]{:T(128)}, f32[256,256]{0,1:T(8,128)S(1)}, s32[2,2]{1,0:T(2,128)S(1)}, f32[2,128,128]{2,1,0:T(8,128)S(1)}, s32[]{:T(128)}) %tuple.29), condition=%wide.while_cond, body=%wide.while_body.sunk | while | flops 2 | bytes 393321 | solution.py:155
  214.9 0.6 fusion.57
  215.5 1.3 dynamic-slice.7
  216.9 0.6 fusion.57
  217.5 1.3 dynamic-slice.7
  219.0 19.9 %custom-call.19 = f32[2,128,128]{1,2,0:T(8,128)S(1)} custom-call(f32[2,128,128]{2,1,0:T(8,128)S(1)} %get-tuple-element.12), custom_call_target="InvertDiagBlocksLowerTriangular" | custom-call | tf_op jit(solution)/shard_map/triangular_solve | solution.py:155
  240.1 0.3 fusion.28
  240.6 0.3 fusion.35
  240.9 0.7 fusion.3
  241.6 1.6 copy.84
  (78 shorter events, 3.6 us)
Async XLA Ops:
  0.0 14.5 %copy-start = (bf16[384,8,256]{2,1,0:T(8,128)(2,1)S(1)}, bf16[384,8,256]{2,1,0:T(8,128)(2,1)}, u32[]{:S(2)}) copy-start(bf16[384,8,256]{2,1,0:T(8,128)(2,1)} %param.9) | copy-start | bytes 4718596
  0.0 41.7 %copy-start.9 = (s32[160]{0:T(256)S(1)}, s32[160]{0:T(256)}, u32[]{:S(2)}) copy-start(s32[160]{0:T(256)} %param.16) | copy-start | bytes 1924
  1.7 19.2 %all-to-all-start.2 = ((bf16[16,2,160]{2,1,0:T(2,128)(2,1)}), bf16[16,2,160]{2,1,0:T(2,128)(2,1)S(1)}, u32[]{:S(2)}, u32[]{:S(2)}) async-start(bf16[16,2,160]{2,1,0:T(2,128)(2,1)} %reshape.210), calls=%async_computation.2 | async-start | bytes 32768 | tf_op jit(solution)/shard_map/all_to_all | solution.py:128
  20.9 37.1 %all-to-all-start.1 = ((bf16[160,32,128]{2,1,0:T(8,128)(2,1)}), bf16[160,32,128]{2,1,0:T(8,128)(2,1)S(1)}, u32[]{:S(2)}, u32[]{:S(2)}) async-start(bf16[160,32,128]{2,1,0:T(8,128)(2,1)} %param.10), calls=%async_computation.1 | async-start | bytes 2621440 | tf_op jit(solution)/shard_map/all_to_all | solution.py:127
  26.3 16.6 %collective-permute-start = (bf16[40,8,256]{2,1,0:T(8,128)(2,1)S(1)}, bf16[40,8,256]{2,1,0:T(8,128)(2,1)S(1)}, u32[]{:S(2)}, u32[]{:S(2)}) collective-permute-start(bf16[40,8,256]{2,1,0:T(8,128)(2,1)S(1)} %get-tuple-element.42), channel_id=1, source_target_pairs={{0,480},{16,496},{32,0},{48,16},{64,32},{80,48},{96,64},{112,80},{... | collective-permute-start | bytes 491528 | tf_op jit(solution)/shard_map/ppermute | solution.py:14
  33.8 9.1 %collective-permute-start.1 = (bf16[40,8,256]{2,1,0:T(8,128)(2,1)S(1)}, bf16[40,8,256]{2,1,0:T(8,128)(2,1)S(1)}, u32[]{:S(2)}, u32[]{:S(2)}) collective-permute-start(bf16[40,8,256]{2,1,0:T(8,128)(2,1)S(1)} %get-tuple-element.41), channel_id=1, source_target_pairs={{0,496},{16,0},{32,16},{48,32},{64,48},{80,64},{96,80},{112,96},{1... | collective-permute-start | bytes 491528 | tf_op jit(solution)/shard_map/ppermute | solution.py:14
  36.6 10.2 %collective-permute-start.2 = (bf16[40,8,256]{2,1,0:T(8,128)(2,1)S(1)}, bf16[40,8,256]{2,1,0:T(8,128)(2,1)S(1)}, u32[]{:S(2)}, u32[]{:S(2)}) collective-permute-start(bf16[40,8,256]{2,1,0:T(8,128)(2,1)S(1)} %get-tuple-element.40), channel_id=1, source_target_pairs={{0,16},{16,32},{32,48},{48,64},{64,80},{80,96},{96,112},{112,128},... | collective-permute-start | bytes 491528 | tf_op jit(solution)/shard_map/ppermute | solution.py:14
  39.1 10.7 %collective-permute-start.3 = (bf16[40,8,256]{2,1,0:T(8,128)(2,1)S(1)}, bf16[40,8,256]{2,1,0:T(8,128)(2,1)S(1)}, u32[]{:S(2)}, u32[]{:S(2)}) collective-permute-start(bf16[40,8,256]{2,1,0:T(8,128)(2,1)S(1)} %get-tuple-element.39), channel_id=1, source_target_pairs={{0,32},{16,48},{32,64},{48,80},{64,96},{80,112},{96,128},{112,144}... | collective-permute-start | bytes 491528 | tf_op jit(solution)/shard_map/ppermute | solution.py:14
  49.8 0.9 copy-start.3
  58.0 16.8 %copy-start.1 = (bf16[160,32,128]{2,1,0:T(8,128)(2,1)}, bf16[160,32,128]{2,1,0:T(8,128)(2,1)S(1)}, u32[]{:S(2)}) copy-start(bf16[160,32,128]{2,1,0:T(8,128)(2,1)S(1)} %all-to-all-done.1) | copy-start | bytes 3932164
  58.0 25.7 %all-to-all-start = ((bf16[160,8,256]{2,1,0:T(8,128)(2,1)}), bf16[160,8,256]{2,1,0:T(8,128)(2,1)S(1)}, u32[]{:S(2)}, u32[]{:S(2)}) async-start(bf16[160,8,256]{2,1,0:T(8,128)(2,1)} %broadcast_select_fusion.1), calls=%async_computation | async-start | bytes 1310720 | tf_op jit(solution)/shard_map/all_to_all | solution.py:126
  86.9 6.0 %copy-start.2 = (f32[16,32,32]{1,0,2:T(8,128)S(1)}, f32[16,32,32]{1,0,2:T(8,128)}, u32[]{:S(2)}) copy-start(f32[16,32,32]{1,0,2:T(8,128)} %reshape.150) | copy-start | bytes 196612
  86.9 6.0 %copy-start.6 = (f32[16,32]{1,0:T(8,128)S(1)}, f32[16,32]{1,0:T(8,128)}, u32[]{:S(2)}) copy-start(f32[16,32]{1,0:T(8,128)} %mul.56) | copy-start | bytes 6148
  86.9 6.0 %copy-start.8 = (f32[10]{0:T(128)S(1)}, f32[10]{0:T(128)}, u32[]{:S(2)}) copy-start(f32[10]{0:T(128)} %dynamic_slice.3) | copy-start | bytes 124
  100.0 0.9 copy-start.7
  100.8 2.0 copy-start.5
  150.9 26.4 %all-to-all-start.6 = ((f32[64,8,129]{2,1,0:T(8,128)}), f32[64,8,129]{2,1,0:T(8,128)S(1)}, u32[]{:S(2)}, u32[]{:S(2)}) async-start(f32[64,8,129]{2,1,0:T(8,128)} %broadcast_in_dim.53), calls=%async_computation.6 | async-start | bytes 1048576 | tf_op jit(solution)/shard_map/all_to_all | solution.py:26
  160.0 80.1 %copy-start.4 = (f32[256,256]{1,0:T(8,128)S(1)}, f32[256,256]{1,0:T(8,128)}, u32[]{:S(2)}) copy-start(f32[256,256]{1,0:T(8,128)} %param.14) | copy-start | bytes 786436
where the time goes:
time: 244 us; the launch traced here: 243 us
  other arithmetic  62.4 us (26%)
  starting transfers between devices  45.8 us (19%)
  blocking collectives  43.5 us (18%)
  waiting for transfers between devices  39.6 us (16%)
  local copies, waits for them, and re-layouts  31.1 us (13%)
  matrix products  18.3 us (8%)
    another operation x6, other arithmetic, local(): factor = jnp.linalg.cholesky(system)  33.9 us
    all_to_all x1, blocking collectives, sent_and_summed(): parts = lax.all_to_all(in_blocks(x, dim, peers), axis, 0, 0, tiled=True)  21.4 us
    another operation x3, other arithmetic, local(): lax.linalg.triangular_solve(factor, ensemble_vectors, left_side=True, low...  20 us
    all_to_all x1, waiting for transfers between devices, from_everyone(): lax.all_to_all(jnp.broadcast_to(x[None], (peers, *x.shape)), axis, 0, 0,...  17.3 us
    ppermute x4, starting transfers between devices, from_behind(): return lax.ppermute(value, axis, pairs)  15.4 us
    all_to_all x1, blocking collectives, sum_in_two_steps(): lax.all_to_all(nearer, far, split_axis=0, concat_axis=0, tiled=True)  13.2 us
    all_to_all x1, starting transfers between devices, local(): lax.all_to_all(innovation.astype(jnp.bfloat16), CHAN, split_axis=0, conca...  11.8 us
    all_to_all x1, starting transfers between devices, from_everyone(): lax.all_to_all(jnp.broadcast_to(x[None], (peers, *x.shape)), axis, 0, 0,...  9.08 us
  transfers between devices with their start and end apart: 8, of which 6 were waited for; matrix products, arithmetic and copies ran while one was open for 9% of the time, Pallas kernels for 0%

commit v1 on v0

v1 whole, which is shorter than its diff:
```python
import jax
import jax.numpy as jnp
from jax import lax
from jax.experimental import pallas as pl
from jax.experimental.pallas import tpu as pltpu
from jax.sharding import Mesh
from jax.sharding import PartitionSpec as P

TILE = ("y", "x")
CHAN = ("z", "c")
NEAR = ("x", "z", "c")
FAR = "y"
MEM = 256
HI = lax.Precision.HIGHEST
F32 = jnp.float32
BF16 = jnp.bfloat16
VM = pl.BlockSpec(memory_space=pltpu.VMEM)
SM = pl.BlockSpec(memory_space=pltpu.SMEM)
PARAMS = pltpu.CompilerParams(vmem_limit_bytes=48 * 2**20)


def cost(flops, size):
    return pl.CostEstimate(flops=flops, bytes_accessed=size, transcendentals=0)


def iota2(rows, columns, dim):
    return lax.broadcasted_iota(jnp.int32, (rows, columns), dim)


def nt(a, b, precision=None):
    return lax.dot_general(
        a, b, (((1,), (1,)), ((), ())), precision=precision, preferred_element_type=F32
    )


def nn(a, b, precision=None):
    return lax.dot_general(
        a, b, (((1,), (0,)), ((), ())), precision=precision, preferred_element_type=F32
    )


def split(x):
    high = x.astype(BF16)
    return high, (x - high.astype(F32)).astype(BF16)


def pick_kernel(pick, ensemble, *sends):
    capacity = sends[0].shape[0]
    for o, out in enumerate(sends):

        def one(j, carry, o=o, out=out):
            out[j] = ensemble[pick[o * capacity + j]]
            return carry

        lax.fori_loop(0, capacity, one, 0, unroll=8)


def weights_kernel(place, innovation, vectors, inverses, jacobian, slabs, sums):
    group = place[0]
    width = vectors.shape[1]
    start = pl.multiple_of(group * width, width)
    basis = vectors[pl.ds(start, width), :]
    scaled = basis * inverses[pl.ds(group, 1), :]
    tiled = nt(scaled, jnp.concatenate([basis] * 8, axis=0), HI)
    weights = nn(innovation[...], tiled, HI)
    mine = iota2(8, 8 * width, 1) // width == iota2(8, 8 * width, 0)
    rows = innovation.shape[0]
    for k in range(rows // 8):
        high, low = split(jnp.where(mine, weights[8 * k : 8 * k + 8], 0.0))
        block = jacobian[8 * k : 8 * k + 8].reshape(8 * width, 128)
        sums[8 * k : 8 * k + 8, :] = nn(high, block) + nn(low, block)
    share = rows // slabs.shape[0]
    zero = jnp.zeros((8 - (share - 8), 128), F32)
    for i in range(slabs.shape[0]):
        left = sums[share * i : share * i + 8, :]
        right = jnp.concatenate([sums[share * i + 8 : share * i + share, :], zero], axis=0)
        slabs[i] = jnp.concatenate([left, right], axis=1).astype(BF16)


def slot_kernel(slot, a0, a1, a2, a3, a4, slabs, out, held):
    capacity = a0.shape[0]
    for o, part in enumerate((a0, a1, a2, a3, a4)):
        held[o * capacity : (o + 1) * capacity] = part[...]
    peers = slabs.shape[0]
    share = out.shape[0] // peers - 1

    def one(i, carry):
        for f in range(share):
            out[i * (share + 1) + f] = held[slot[i * share + f]]
        out[i * (share + 1) + share] = slabs[i]
        return carry

    lax.fori_loop(0, peers, one, 0)


def terms_kernel(place, vectors, scales, jacobian, arrived, out):
    peers = vectors.shape[0] // vectors.shape[1]
    share = jacobian.shape[0] // peers
    first = place[0] * share
    count = place[1]
    half = MEM
    same = iota2(half, half, 0) // 32 == iota2(half, half, 1) // 32
    turns = []
    for h in range(2):
        block = vectors[h * half : (h + 1) * half, :]
        wide = jnp.where(same, jnp.concatenate([block] * 8, axis=1), 0.0) * scales[h : h + 1, :]
        turns.append(split(wide.T))
    b = arrived[share].astype(F32)
    for source in range(1, peers):
        b = b + arrived[source * (share + 1) + share].astype(F32)
    gram = jnp.zeros((MEM, MEM), F32)
    pull = jnp.zeros((8, MEM), F32)
    for f in range(share):
        live = jnp.where(first + f < count, 1.0, 0.0).astype(F32)
        parts = []
        for h in range(2):
            block = jnp.concatenate(
                [jacobian[(h * 8 + s) * share + f] for s in range(8)], axis=0
            )
            high, low = turns[h]
            parts.append(((nn(high, block) + nn(low, block)) * live).astype(BF16))
        turned = jnp.concatenate(parts, axis=0)
        column = jnp.concatenate(
            [arrived[s * (share + 1) + f] for s in range(peers)], axis=0
        )
        flipped = column.astype(F32).T.astype(BF16)
        whitened = nt(flipped, turned).astype(BF16)
        gram = gram + nt(whitened, whitened)
        mine = iota2(8, 128, 0) == f % 8
        high, low = split(jnp.where(mine, b[:, 128 * (f // 8) : 128 * (f // 8) + 128] * live, 0.0))
        pull = pull + (nn(high, column) + nn(low, column))
    out[0:16] = gram[0:128, 0:128].reshape(16, 8, 128)
    out[16:32] = gram[128:256, 0:128].reshape(16, 8, 128)
    out[32:48] = gram[128:256, 128:256].reshape(16, 8, 128)
    total = jnp.sum(pull, axis=0, keepdims=True)
    last = jnp.concatenate(
        [total[:, 0:128], total[:, 128:256], jnp.zeros((6, 128), F32)], axis=0
    )
    out[48:64] = jnp.zeros((16, 8, 128), F32)
    out[48] = last


def lower_half(x):
    i, j = iota2(MEM, MEM, 0), iota2(MEM, MEM, 1)
    return jnp.where(i > j, x, jnp.where(i == j, 0.5 * x, 0.0))


def solve_kernel(summed, basis, out, system, inverse, rows):
    eye = (iota2(MEM, MEM, 0) == iota2(MEM, MEM, 1)).astype(F32)
    g00 = summed[0:16].reshape(128, 128)
    g10 = summed[16:32].reshape(128, 128)
    g11 = summed[32:48].reshape(128, 128)
    a = jnp.concatenate(
        [jnp.concatenate([g00, g10.T], axis=1), jnp.concatenate([g10, g11], axis=1)], axis=0
    ) + (MEM - 1.0) * eye
    system[...] = a
    across = lax.rsqrt(jnp.sum(a * eye, axis=0, keepdims=True))
    down = lax.rsqrt(jnp.sum(a * eye, axis=1, keepdims=True))
    x = across * (eye - lower_half(a * across * down - eye))
    residual = nt(nn(x, a), x) - eye
    inverse[...] = x - nn(lower_half(residual), x)

    def go_on(state):
        step, size = state
        return jnp.logical_and(step < 9, jnp.logical_and(size >= 1e-4, size < 1e6))

    def refine(state):
        step, _ = state
        x = inverse[...]
        residual = nt(nn(x, system[...], HI), x, HI) - eye
        inverse[...] = x - nn(lower_half(residual), x, HI)
        return step + 1, jnp.sum(residual * residual)

    _, size = lax.while_loop(go_on, refine, (jnp.int32(0), jnp.float32(1.0)))

    @pl.when(jnp.logical_not(size < 1e-4))
    def _():
        rows[:, 0:MEM] = system[...]
        rows[:, MEM : 2 * MEM] = eye
        lanes = iota2(1, 2 * MEM, 1)

        def eliminate(j, carry):
            row = rows[pl.ds(j, 1), :]
            pivot = jnp.sum(jnp.where(lanes == j, row, 0.0), axis=1, keepdims=True)
            old = rows[...]
            column = jnp.sum(jnp.where(lanes == j, old, 0.0), axis=1, keepdims=True)
            below = iota2(MEM, 1, 0) > j
            rows[...] = old - jnp.where(below, column / pivot, 0.0) * row
            rows[pl.ds(j, 1), :] = row * (1.0 / jnp.sqrt(pivot))
            return carry

        lax.fori_loop(0, MEM, eliminate, 0)
        inverse[...] = rows[:, MEM : 2 * MEM]

    x = inverse[...]
    last = summed[48]
    pull = jnp.concatenate([last[0:1, :], last[1:2, :]], axis=1)
    halfway = nt(x, jnp.broadcast_to(pull, (MEM, MEM)), HI)
    target = (MEM - 1.0) ** 0.5 * basis[...] + halfway
    out[...] = nn(x.T, target, HI).astype(BF16)


def send_by(value, axis, steps):
    count = lax.axis_size(axis)
    return lax.ppermute(value, axis, [(s, (s + steps) % count) for s in range(count)])


def swap(x, axis):
    return lax.all_to_all(x, axis, 0, 0, tiled=True)


def summed_everywhere(tiles):
    mine = jnp.sum(swap(tiles, NEAR), axis=0, keepdims=True)
    far = lax.axis_size(FAR)
    mine = jnp.sum(swap(jnp.broadcast_to(mine, (far, 8, 128)), FAR), axis=0, keepdims=True)
    return swap(jnp.broadcast_to(mine, (tiles.shape[0], 8, 128)), NEAR)


def local(
    ensemble,
    jacobian,
    innovation,
    error_vectors,
    error_values,
    ensemble_vectors,
    column_pick,
    footprint_slot,
    footprint_count,
):
    window, capacity = column_pick.shape[1:]
    levels, members = ensemble.shape[1:]
    width = error_vectors.shape[1]
    foot_rows = jacobian.shape[0]
    peers = lax.axis_size(CHAN)
    share = foot_rows // peers
    slab = (levels, members)

    sensitivity = swap(jacobian, CHAN)

    chosen = pl.pallas_call(
        pick_kernel,
        out_shape=[jax.ShapeDtypeStruct((capacity, *slab), BF16)] * window,
        in_specs=[SM, VM],
        out_specs=[VM] * window,
        compiler_params=PARAMS,
        cost_estimate=cost(0, 2 * ensemble.size),
        name="pick",
    )(column_pick.reshape(-1), ensemble)
    parts = []
    for o in range(window):
        steps = o - window // 2
        parts.append(send_by(chosen[o], TILE, steps) if steps else chosen[o])

    place = jnp.concatenate(
        [lax.axis_index(CHAN).astype(jnp.int32)[None], footprint_count.astype(jnp.int32)]
    )
    slabs = pl.pallas_call(
        weights_kernel,
        out_shape=jax.ShapeDtypeStruct((peers, *slab), BF16),
        in_specs=[SM, VM, VM, VM, VM],
        out_specs=VM,
        scratch_shapes=[pltpu.VMEM((foot_rows, 128), F32)],
        compiler_params=PARAMS,
        cost_estimate=cost(2 * foot_rows * 256 * 128, 2 * jacobian.size),
        name="weights",
    )(place, innovation, error_vectors, 1.0 / error_values.reshape(peers, width), jacobian)

    payload = pl.pallas_call(
        slot_kernel,
        out_shape=jax.ShapeDtypeStruct((foot_rows + peers, *slab), BF16),
        in_specs=[SM] + [VM] * (window + 1),
        out_specs=VM,
        scratch_shapes=[pltpu.VMEM((window * capacity, *slab), BF16)],
        compiler_params=PARAMS,
        cost_estimate=cost(0, 4 * foot_rows * levels * members),
        name="slots",
    )(footprint_slot, *parts, slabs)
    arrived = swap(payload, CHAN)

    tiles = pl.pallas_call(
        terms_kernel,
        out_shape=jax.ShapeDtypeStruct((64, 8, 128), F32),
        in_specs=[SM, VM, VM, VM, VM],
        out_specs=VM,
        compiler_params=PARAMS,
        cost_estimate=cost(4 * 512 * share * 256 * 384, 2 * jacobian.size),
        name="terms",
    )(place, error_vectors, 1.0 / jnp.sqrt(error_values).reshape(2, members), sensitivity, arrived)

    summed = summed_everywhere(tiles)

    transform = pl.pallas_call(
        solve_kernel,
        out_shape=jax.ShapeDtypeStruct((members, members), BF16),
        in_specs=[VM, VM],
        out_specs=VM,
        scratch_shapes=[
            pltpu.VMEM((members, members), F32),
            pltpu.VMEM((members, members), F32),
            pltpu.VMEM((members, 2 * members), F32),
        ],
        compiler_params=PARAMS,
        name="solve",
    )(summed, ensemble_vectors)

    updated = jnp.dot(
        ensemble.reshape(-1, members), transform, preferred_element_type=F32
    ).astype(BF16)
    return updated.reshape(ensemble.shape)


def solution(mesh):
    finer = Mesh(mesh.devices.reshape(8, 4, 8, 2), ("y", "x", "z", "c"))
    return jax.shard_map(
        local,
        mesh=finer,
        in_specs=(
            P(TILE, CHAN, None),
            P(TILE, CHAN, None),
            P(TILE, CHAN),
            P(),
            P(),
            P(),
            P(TILE, None, None),
            P(TILE),
            P(TILE),
        ),
        out_specs=P(TILE, CHAN, None),
        check_vma=False,
    )
```

time: 244 us -> 196 us (0.80)
  other arithmetic: 62.4 us -> 0.87 us
  Pallas kernels: 0 us -> 52.2 us
  blocking collectives: 43.5 us -> 80.5 us
  local copies, waits for them, and re-layouts: 31.1 us -> 3.41 us
  starting transfers between devices: 45.8 us -> 19.8 us
  matrix products: 18.3 us -> 0.63 us
  waiting for transfers between devices: 39.6 us -> 36.9 us
    another operation x10 -> x0, other arithmetic: 53.9 us -> none  [the longest x6 33.9 us: local(): factor = jnp.linalg.cholesky(system)]
    pallas_call x0 -> x5, Pallas kernels: none -> 52.2 us  [the longest x1 42.3 us: local(): pl.pallas_call(solve_kernel, out_shape=jax.ShapeDtypeStruct((members, mem...]
    all_to_all x3 -> x4, blocking collectives: 43.5 us -> 80.5 us  [swap(): return lax.all_to_all(x, axis, 0, 0, tiled=True)]
    all_to_all x4 -> x1, starting transfers between devices: 30.5 us -> 3.6 us  [swap(): return lax.all_to_all(x, axis, 0, 0, tiled=True)]
    dot_general x6 -> x1, matrix products: 15.9 us -> 0.63 us  [local(): jnp.dot(ensemble.reshape(-1, members), transform, preferred_element_type=...]
    dot_general x1 -> x0, local copies, waits for them, and re-layouts: 5.94 us -> none  [local(): jnp.einsum('fcl,flk->fck', sensitivity, columns, preferred_element_type=j...]
    another operation x23 -> x0, local copies, waits for them, and re-layouts: 5.48 us -> none
    gather x2 -> x0, local copies, waits for them, and re-layouts: 3.75 us -> none  [the longest x1 2.04 us: local(): columns = jnp.take(slot_rows, footprint_slot, axis=0)]
  transfers between devices with their start and end apart: 8 -> 5, of which waited for: 6 -> 3; matrix products, arithmetic and copies ran while one was open for 9% -> 0% of each run, Pallas kernels for 0% -> 1%
where the time goes in v1:
time: 196 us; the launch traced here: 195 us
  blocking collectives  80.5 us (41%)
  Pallas kernels  52.2 us (27%)
  waiting for transfers between devices  36.9 us (19%)
  starting transfers between devices  19.8 us (10%)
  local copies, waits for them, and re-layouts  3.41 us (2%)
    all_to_all x4, blocking collectives, swap(): return lax.all_to_all(x, axis, 0, 0, tiled=True)  80.5 us
    pallas_call x1, Pallas kernels, local(): pl.pallas_call(solve_kernel, out_shape=jax.ShapeDtypeStruct((members, mem...  42.3 us
    all_to_all x1, waiting for transfers between devices, swap(): return lax.all_to_all(x, axis, 0, 0, tiled=True)  32.5 us
    ppermute x4, starting transfers between devices, send_by(): lax.ppermute(value, axis, [(s, (s + steps) % count) for s in range(count)])  16.2 us
    pallas_call x1, Pallas kernels, local(): pl.pallas_call(terms_kernel, out_shape=jax.ShapeDtypeStruct((64, 8, 128),...  5.7 us
    ppermute x4, waiting for transfers between devices, send_by(): lax.ppermute(value, axis, [(s, (s + steps) % count) for s in range(count)])  4.4 us
  transfers between devices with their start and end apart: 5, of which 3 were waited for; matrix products, arithmetic and copies ran while one was open for 0% of the time, Pallas kernels for 1%

profile of v1, /device:TPU:1, one launch (start us, length us, event | category | flops | bytes accessed | tf_op | source)
XLA Modules:
  0.0 195.2 jit_solution(650815117058292435)
XLA Ops:
  0.0 0.0 copy-start.6
  0.0 0.7 reduce
  0.7 0.1 reshape.17.pick
  0.8 0.0 copy-start
  0.8 1.4 copy-done
  2.2 0.0 copy-start.4
  2.2 0.0 copy-start.5
  2.2 0.0 copy-start.3
  2.2 0.9 pick.1
  3.1 8.4 %collective-permute-start = (bf16[40,8,256]{2,1,0:T(8,128)(2,1)S(1)}, bf16[40,8,256]{2,1,0:T(8,128)(2,1)S(1)}, u32[]{:S(2)}, u32[]{:S(2)}) collective-permute-start(bf16[40,8,256]{2,1,0:T(8,128)(2,1)S(1)} %get-tuple-element.10), channel_id=1, source_target_pairs={{0,480},{16,496},{32,0},{48,16},{64,32},{80,48},{96,64},{112,80},{... | collective-permute-start | bytes 491528 | tf_op jit(solution)/shard_map/ppermute | solution.py:205
  11.5 2.8 %collective-permute-start.1 = (bf16[40,8,256]{2,1,0:T(8,128)(2,1)S(1)}, bf16[40,8,256]{2,1,0:T(8,128)(2,1)S(1)}, u32[]{:S(2)}, u32[]{:S(2)}) collective-permute-start(bf16[40,8,256]{2,1,0:T(8,128)(2,1)S(1)} %get-tuple-element.11), channel_id=1, source_target_pairs={{0,496},{16,0},{32,16},{48,32},{64,48},{80,64},{96,80},{112,96},{1... | collective-permute-start | bytes 491528 | tf_op jit(solution)/shard_map/ppermute | solution.py:205
  14.3 2.5 %collective-permute-start.2 = (bf16[40,8,256]{2,1,0:T(8,128)(2,1)S(1)}, bf16[40,8,256]{2,1,0:T(8,128)(2,1)S(1)}, u32[]{:S(2)}, u32[]{:S(2)}) collective-permute-start(bf16[40,8,256]{2,1,0:T(8,128)(2,1)S(1)} %get-tuple-element.13), channel_id=1, source_target_pairs={{0,16},{16,32},{32,48},{48,64},{64,80},{80,96},{96,112},{112,128},... | collective-permute-start | bytes 491528 | tf_op jit(solution)/shard_map/ppermute | solution.py:205
  16.8 2.6 %collective-permute-start.3 = (bf16[40,8,256]{2,1,0:T(8,128)(2,1)S(1)}, bf16[40,8,256]{2,1,0:T(8,128)(2,1)S(1)}, u32[]{:S(2)}, u32[]{:S(2)}) collective-permute-start(bf16[40,8,256]{2,1,0:T(8,128)(2,1)S(1)} %get-tuple-element.14), channel_id=1, source_target_pairs={{0,32},{16,48},{32,64},{48,80},{64,96},{80,112},{96,128},{112,144}... | collective-permute-start | bytes 491528 | tf_op jit(solution)/shard_map/ppermute | solution.py:205
  19.4 0.0 copy-done.6
  20.1 0.0 copy-done.4
  20.1 0.1 copy.20.vectors
  20.2 0.1 div.15.inverses
  20.3 0.0 copy-done.5
  20.3 0.1 copy.18.innovation
  20.4 0.1 pad_add_fusion.place
  20.5 2.4 %weights.1.slabs = bf16[16,8,256]{2,1,0:T(8,128)(2,1)S(1)} custom-call(s32[2]{0:T(128)S(1)} %pad_add_fusion.place, f32[160,32]{1,0:T(8,128)S(1)} %copy.18.innovation, f32[512,32]{1,0:T(8,128)S(1)} %copy.20.vectors, f32[16,32]{1,0:T(8,128)S(1)} %div.15.inverses, bf16[160,32,128]{2,1,0:T(8,128)(2,1)} %jacobian.1), custom_call_target="tpu_custom_call" | custom-call | flops 10485760 | bytes 1310720 | tf_op jit(solution)/shard_map/weights/pallas_call | solution.py:257
  22.9 0.0 collective-permute-done.a0
  22.9 0.0 collective-permute-done.1.a1
  22.9 0.7 collective-permute-done.2.a3
  23.7 3.7 %collective-permute-done.3.a4 = bf16[40,8,256]{2,1,0:T(8,128)(2,1)S(1)} collective-permute-done((bf16[40,8,256]{2,1,0:T(8,128)(2,1)S(1)}, bf16[40,8,256]{2,1,0:T(8,128)(2,1)S(1)}, u32[]{:S(2)}, u32[]{:S(2)}) %collective-permute-start.3) | collective-permute-done | bytes 163872 | tf_op jit(solution)/shard_map/ppermute | solution.py:205
  27.3 0.0 copy-done.3
  27.3 0.8 slots.1
  28.2 34.1 %all_to_all.25.arrived = bf16[176,8,256]{2,1,0:T(8,128)(2,1)S(1)} all-to-all(bf16[176,8,256]{2,1,0:T(8,128)(2,1)S(1)} %slots.1), channel_id=1, replica_groups=mesh['y'=8,'x'=4,'z'=8,'c'=2] {'z','c'}, dimensions={0} | all-to-all | bytes 1441792 | tf_op jit(solution)/shard_map/all_to_all | solution.py:209
  62.3 3.6 %all-to-all-start = ((bf16[160,32,128]{2,1,0:T(8,128)(2,1)}), bf16[160,32,128]{2,1,0:T(8,128)(2,1)S(1)}, u32[]{:S(2)}, u32[]{:S(2)}) async-start(bf16[160,32,128]{2,1,0:T(8,128)(2,1)} %jacobian.1), calls=%async_computation | async-start | bytes 2621440 | tf_op jit(solution)/shard_map/all_to_all | solution.py:209
  65.9 32.5 %all-to-all-done.jacobian = bf16[160,32,128]{2,1,0:T(8,128)(2,1)S(1)} async-done(((bf16[160,32,128]{2,1,0:T(8,128)(2,1)}), bf16[160,32,128]{2,1,0:T(8,128)(2,1)S(1)}, u32[]{:S(2)}, u32[]{:S(2)}) %all-to-all-start) | async-done | bytes 1310752 | tf_op jit(solution)/shard_map/all_to_all | solution.py:209
  98.4 0.0 copy-start.2
  98.4 5.7 %terms.1 = f32[64,8,128]{2,1,0:T(8,128)S(1)} custom-call(s32[2]{0:T(128)S(1)} %pad_add_fusion.place, f32[512,32]{1,0:T(8,128)S(1)} %copy.20.vectors, f32[2,256]{1,0:T(2,128)S(1)} %div.12.scales, bf16[160,32,128]{2,1,0:T(8,128)(2,1)S(1)} %all-to-all-done.jacobian, bf16[176,8,256]{2,1,0:T(8,128)(2,1)S(1)} %all_to_all.25.arrived), custom_call_target="tpu_custom_call" | custom-call | flops 2013265920 | bytes 1310720 | tf_op jit(solution)/shard_map/terms/pallas_call | solution.py:280
  104.1 0.0 copy-start.1
  104.2 16.7 %all_to_all.26 = f32[64,8,128]{2,1,0:T(8,128)S(1)} all-to-all(f32[64,8,128]{2,1,0:T(8,128)S(1)} %terms.1), channel_id=1, replica_groups=mesh['y'=8,'x'=4,'z'=8,'c'=2] {'x','z','c'}, dimensions={0} | all-to-all | bytes 524288 | tf_op jit(solution)/shard_map/all_to_all | solution.py:209
  120.8 0.1 reduce_sum.18
  120.9 10.5 %all_to_all.27 = f32[8,8,128]{2,1,0:T(8,128)S(1)} all-to-all(f32[8,8,128]{2,1,0:T(8,128)S(1)} %broadcast_in_dim.7), channel_id=1, replica_groups=mesh['y'=8,'x'=4,'z'=8,'c'=2] {'y'}, dimensions={0} | all-to-all | bytes 65536 | tf_op jit(solution)/shard_map/all_to_all | solution.py:209
  131.4 19.3 %all_to_all.28.summed = f32[64,8,128]{2,1,0:T(8,128)S(1)} all-to-all(f32[64,8,128]{2,1,0:T(8,128)S(1)} %broadcast_in_dim.8), channel_id=1, replica_groups=mesh['y'=8,'x'=4,'z'=8,'c'=2] {'x','z','c'}, dimensions={0} | all-to-all | bytes 524288 | tf_op jit(solution)/shard_map/all_to_all | solution.py:209
  150.7 0.0 copy-done.2
  150.7 42.3 %solve.1 = bf16[256,256]{1,0:T(8,128)(2,1)S(1)} custom-call(f32[64,8,128]{2,1,0:T(8,128)S(1)} %all_to_all.28.summed, f32[256,256]{1,0:T(8,128)S(1)} %copy-done.2), custom_call_target="tpu_custom_call" | custom-call | tf_op jit(solution)/shard_map/solve/pallas_call | solution.py:292
  193.0 0.0 copy-done.1
  193.0 0.6 fusion
  193.6 1.6 copy.21
  (5 shorter events, 0.1 us)
Async XLA Ops:
  0.0 19.4 %copy-start.6 = (f32[512]{0:T(512)S(1)}, f32[512]{0:T(512)}, u32[]{:S(2)}) copy-start(f32[512]{0:T(512)} %param.13) | copy-start | bytes 6148
  0.8 1.4 copy-start
  2.2 17.9 %copy-start.4 = (f32[512,32]{0,1:T(8,128)S(1)}, f32[512,32]{0,1:T(8,128)}, u32[]{:S(2)}) copy-start(f32[512,32]{0,1:T(8,128)} %param.12) | copy-start | bytes 196612
  2.2 18.1 %copy-start.5 = (f32[160,32]{0,1:T(8,128)S(1)}, f32[160,32]{0,1:T(8,128)}, u32[]{:S(2)}) copy-start(f32[160,32]{0,1:T(8,128)} %param.11) | copy-start | bytes 61444
  2.2 25.1 %copy-start.3 = (s32[160]{0:T(256)S(1)}, s32[160]{0:T(256)}, u32[]{:S(2)}) copy-start(s32[160]{0:T(256)} %slot.1) | copy-start | bytes 1924
  3.1 19.8 %collective-permute-start = (bf16[40,8,256]{2,1,0:T(8,128)(2,1)S(1)}, bf16[40,8,256]{2,1,0:T(8,128)(2,1)S(1)}, u32[]{:S(2)}, u32[]{:S(2)}) collective-permute-start(bf16[40,8,256]{2,1,0:T(8,128)(2,1)S(1)} %get-tuple-element.10), channel_id=1, source_target_pairs={{0,480},{16,496},{32,0},{48,16},{64,32},{80,48},{96,64},{112,80},{... | collective-permute-start | bytes 491528 | tf_op jit(solution)/shard_map/ppermute | solution.py:205
  11.5 11.4 %collective-permute-start.1 = (bf16[40,8,256]{2,1,0:T(8,128)(2,1)S(1)}, bf16[40,8,256]{2,1,0:T(8,128)(2,1)S(1)}, u32[]{:S(2)}, u32[]{:S(2)}) collective-permute-start(bf16[40,8,256]{2,1,0:T(8,128)(2,1)S(1)} %get-tuple-element.11), channel_id=1, source_target_pairs={{0,496},{16,0},{32,16},{48,32},{64,48},{80,64},{96,80},{112,96},{1... | collective-permute-start | bytes 491528 | tf_op jit(solution)/shard_map/ppermute | solution.py:205
  14.3 9.4 %collective-permute-start.2 = (bf16[40,8,256]{2,1,0:T(8,128)(2,1)S(1)}, bf16[40,8,256]{2,1,0:T(8,128)(2,1)S(1)}, u32[]{:S(2)}, u32[]{:S(2)}) collective-permute-start(bf16[40,8,256]{2,1,0:T(8,128)(2,1)S(1)} %get-tuple-element.13), channel_id=1, source_target_pairs={{0,16},{16,32},{32,48},{48,64},{64,80},{80,96},{96,112},{112,128},... | collective-permute-start | bytes 491528 | tf_op jit(solution)/shard_map/ppermute | solution.py:205
  16.8 10.5 %collective-permute-start.3 = (bf16[40,8,256]{2,1,0:T(8,128)(2,1)S(1)}, bf16[40,8,256]{2,1,0:T(8,128)(2,1)S(1)}, u32[]{:S(2)}, u32[]{:S(2)}) collective-permute-start(bf16[40,8,256]{2,1,0:T(8,128)(2,1)S(1)} %get-tuple-element.14), channel_id=1, source_target_pairs={{0,32},{16,48},{32,64},{48,80},{64,96},{80,112},{96,128},{112,144}... | collective-permute-start | bytes 491528 | tf_op jit(solution)/shard_map/ppermute | solution.py:205
  62.3 36.1 %all-to-all-start = ((bf16[160,32,128]{2,1,0:T(8,128)(2,1)}), bf16[160,32,128]{2,1,0:T(8,128)(2,1)S(1)}, u32[]{:S(2)}, u32[]{:S(2)}) async-start(bf16[160,32,128]{2,1,0:T(8,128)(2,1)} %jacobian.1), calls=%async_computation | async-start | bytes 2621440 | tf_op jit(solution)/shard_map/all_to_all | solution.py:209
  98.4 52.2 %copy-start.2 = (f32[256,256]{1,0:T(8,128)S(1)}, f32[256,256]{1,0:T(8,128)}, u32[]{:S(2)}) copy-start(f32[256,256]{1,0:T(8,128)} %basis.1) | copy-start | bytes 786436
  104.1 88.8 %copy-start.1 = (bf16[384,8,256]{2,1,0:T(8,128)(2,1)S(1)}, bf16[384,8,256]{2,1,0:T(8,128)(2,1)}, u32[]{:S(2)}) copy-start(bf16[384,8,256]{2,1,0:T(8,128)(2,1)} %ensemble.1) | copy-start | bytes 4718596

commit v2 on v1

--- a/solution.py
+++ b/solution.py
@@ -145,7 +145,7 @@
     return jnp.where(i > j, x, jnp.where(i == j, 0.5 * x, 0.0))
 
 
-def solve_kernel(summed, basis, out, system, inverse, rows):
+def solve_kernel(summed, basis, ensemble, out, system, inverse, rows, held, sems):
     eye = (iota2(MEM, MEM, 0) == iota2(MEM, MEM, 1)).astype(F32)
     g00 = summed[0:16].reshape(128, 128)
     g10 = summed[16:32].reshape(128, 128)
@@ -197,7 +197,17 @@
     pull = jnp.concatenate([last[0:1, :], last[1:2, :]], axis=1)
     halfway = nt(x, jnp.broadcast_to(pull, (MEM, MEM)), HI)
     target = (MEM - 1.0) ** 0.5 * basis[...] + halfway
-    out[...] = nn(x.T, target, HI).astype(BF16)
+    transform = nn(x.T, target, HI).astype(BF16)
+    copies = []
+    for i in range(held.shape[0]):
+        size = held.shape[1]
+        held[i] = nn(ensemble[i * size : (i + 1) * size, :], transform).astype(BF16)
+        copies.append(
+            pltpu.make_async_copy(held.at[i], out.at[i * size : (i + 1) * size], sems.at[i])
+        )
+        copies[-1].start()
+    for copy in copies:
+        copy.wait()
 
 
 def send_by(value, axis, steps):
@@ -275,6 +285,7 @@
         cost_estimate=cost(0, 4 * foot_rows * levels * members),
         name="slots",
     )(footprint_slot, *parts, slabs)
+    payload, sensitivity = lax.optimization_barrier((payload, sensitivity))
     arrived = swap(payload, CHAN)
 
     tiles = pl.pallas_call(
@@ -289,23 +300,23 @@
 
     summed = summed_everywhere(tiles)
 
-    transform = pl.pallas_call(
+    chunks = 6
+    flat_rows = ensemble.reshape(-1, members)
+    updated = pl.pallas_call(
         solve_kernel,
-        out_shape=jax.ShapeDtypeStruct((members, members), BF16),
-        in_specs=[VM, VM],
-        out_specs=VM,
+        out_shape=jax.ShapeDtypeStruct(flat_rows.shape, BF16),
+        in_specs=[VM, VM, VM],
+        out_specs=pl.BlockSpec(memory_space=pl.ANY),
         scratch_shapes=[
             pltpu.VMEM((members, members), F32),
             pltpu.VMEM((members, members), F32),
             pltpu.VMEM((members, 2 * members), F32),
+            pltpu.VMEM((chunks, flat_rows.shape[0] // chunks, members), BF16),
+            pltpu.SemaphoreType.DMA((chunks,)),
         ],
         compiler_params=PARAMS,
         name="solve",
-    )(summed, ensemble_vectors)
-
-    updated = jnp.dot(
-        ensemble.reshape(-1, members), transform, preferred_element_type=F32
-    ).astype(BF16)
+    )(summed, ensemble_vectors, flat_rows)
     return updated.reshape(ensemble.shape)
 
 

time: 196 us -> 172 us (0.88)
  blocking collectives: 80.5 us -> 50.8 us
  starting transfers between devices: 19.8 us -> 31.2 us
  waiting for transfers between devices: 36.9 us -> 29 us
  Pallas kernels: 52.2 us -> 55.9 us
    all_to_all x4 -> x3, blocking collectives: 80.5 us -> 50.8 us  [swap(): return lax.all_to_all(x, axis, 0, 0, tiled=True)]
    all_to_all x1 -> x2, starting transfers between devices: 3.6 us -> 15.9 us  [swap(): return lax.all_to_all(x, axis, 0, 0, tiled=True)]
    all_to_all x1 -> x2, waiting for transfers between devices: 32.5 us -> 26.6 us  [swap(): return lax.all_to_all(x, axis, 0, 0, tiled=True)]
    ppermute x4, waiting for transfers between devices: 4.4 us -> 2.42 us  [send_by(): lax.ppermute(value, axis, [(s, (s + steps) % count) for s in range(count)])]
  transfers between devices with their start and end apart: 5 -> 6, of which waited for: 3 -> 3; matrix products, arithmetic and copies ran while one was open for 0% -> 2% of each run, Pallas kernels for 1% -> 3%
where the time goes in v2:
time: 172 us
  Pallas kernels  55.9 us (32%)
  blocking collectives  50.8 us (30%)
  starting transfers between devices  31.2 us (18%)
  waiting for transfers between devices  29 us (17%)
  local copies, waits for them, and re-layouts  3.15 us (2%)
    all_to_all x3, blocking collectives, swap(): return lax.all_to_all(x, axis, 0, 0, tiled=True)  50.8 us
    pallas_call x1, Pallas kernels, local(): pl.pallas_call(solve_kernel, out_shape=jax.ShapeDtypeStruct(flat_rows.sha...  43.8 us
    all_to_all x2, waiting for transfers between devices, swap(): return lax.all_to_all(x, axis, 0, 0, tiled=True)  26.6 us
    all_to_all x2, starting transfers between devices, swap(): return lax.all_to_all(x, axis, 0, 0, tiled=True)  15.9 us
    ppermute x4, starting transfers between devices, send_by(): lax.ppermute(value, axis, [(s, (s + steps) % count) for s in range(count)])  15.4 us
    pallas_call x1, Pallas kernels, local(): pl.pallas_call(terms_kernel, out_shape=jax.ShapeDtypeStruct((64, 8, 128),...  6.49 us
  transfers between devices with their start and end apart: 6, of which 3 were waited for; matrix products, arithmetic and copies ran while one was open for 2% of the time, Pallas kernels for 3%

profile of v2, /device:TPU:1, one launch (start us, length us, event | category | flops | bytes accessed | tf_op | source)
XLA Modules:
  0.0 171.7 jit_solution(16051613786981108438)
XLA Ops:
  0.0 0.0 copy-start.9
  0.0 0.0 copy-start
  0.0 0.0 copy-start.10
  0.0 0.0 copy-start.7
  0.0 12.0 %all-to-all-start = ((bf16[160,32,128]{2,1,0:T(8,128)(2,1)}), bf16[160,32,128]{2,1,0:T(8,128)(2,1)}, u32[]{:S(2)}, u32[]{:S(2)}) async-start(bf16[160,32,128]{2,1,0:T(8,128)(2,1)} %jacobian.1), calls=%async_computation | async-start | bytes 2621440 | tf_op jit(solution)/shard_map/all_to_all | solution.py:219
  12.0 0.0 copy-done.9
  12.0 0.0 copy-start.1
  12.0 0.1 reshape.17.pick
  12.1 0.0 copy-done
  12.1 1.7 %pick.1 = (bf16[40,8,256]{2,1,0:T(8,128)(2,1)}, bf16[40,8,256]{2,1,0:T(8,128)(2,1)}, bf16[40,8,256]{2,1,0:T(8,128)(2,1)S(1)}, bf16[40,8,256]{2,1,0:T(8,128)(2,1)}, bf16[40,8,256]{2,1,0:T(8,128)(2,1)}) custom-call(s32[200]{0:T(256)S(1)} %reshape.17.pick, bf16[384,8,256]{2,1,0:T(8,128)(2,1)S(1)} %copy-done), custom_call_target="tpu_custom_call" | custom-call | bytes 1572864 | tf_op jit(solution)/shard_map/pick/pallas_call | solution.py:250
  13.9 7.5 %collective-permute-start = (bf16[40,8,256]{2,1,0:T(8,128)(2,1)}, bf16[40,8,256]{2,1,0:T(8,128)(2,1)S(1)}, u32[]{:S(2)}, u32[]{:S(2)}) collective-permute-start(bf16[40,8,256]{2,1,0:T(8,128)(2,1)} %get-tuple-element.12), channel_id=1, source_target_pairs={{0,480},{16,496},{32,0},{48,16},{64,32},{80,48},{96,64},{112,80},{... | collective-permute-start | bytes 491528 | tf_op jit(solution)/shard_map/ppermute | solution.py:215
  21.4 2.8 %collective-permute-start.1 = (bf16[40,8,256]{2,1,0:T(8,128)(2,1)}, bf16[40,8,256]{2,1,0:T(8,128)(2,1)}, u32[]{:S(2)}, u32[]{:S(2)}) collective-permute-start(bf16[40,8,256]{2,1,0:T(8,128)(2,1)} %get-tuple-element.13), channel_id=1, source_target_pairs={{0,496},{16,0},{32,16},{48,32},{64,48},{80,64},{96,80},{112,96},{1... | collective-permute-start | bytes 491528 | tf_op jit(solution)/shard_map/ppermute | solution.py:215
  24.2 2.5 %collective-permute-start.2 = (bf16[40,8,256]{2,1,0:T(8,128)(2,1)}, bf16[40,8,256]{2,1,0:T(8,128)(2,1)}, u32[]{:S(2)}, u32[]{:S(2)}) collective-permute-start(bf16[40,8,256]{2,1,0:T(8,128)(2,1)} %get-tuple-element.15), channel_id=1, source_target_pairs={{0,16},{16,32},{32,48},{48,64},{64,80},{80,96},{96,112},{112,128},... | collective-permute-start | bytes 491528 | tf_op jit(solution)/shard_map/ppermute | solution.py:215
  26.7 2.6 %collective-permute-start.3 = (bf16[40,8,256]{2,1,0:T(8,128)(2,1)}, bf16[40,8,256]{2,1,0:T(8,128)(2,1)}, u32[]{:S(2)}, u32[]{:S(2)}) collective-permute-start(bf16[40,8,256]{2,1,0:T(8,128)(2,1)} %get-tuple-element.16), channel_id=1, source_target_pairs={{0,32},{16,48},{32,64},{48,80},{64,96},{80,112},{96,128},{112,144}... | collective-permute-start | bytes 491528 | tf_op jit(solution)/shard_map/ppermute | solution.py:215
  29.3 0.0 copy-done.10
  29.3 0.6 broadcast_divide_fusion
  30.5 0.0 copy-done.7
  30.5 0.1 copy.15.vectors
  30.7 0.9 copy.13.innovation
  31.5 1.3 div.15.inverses
  32.8 0.0 copy-start.4
  32.8 0.1 pad_add_fusion.place
  32.9 0.0 copy-done.1
  32.9 0.0 copy-start.3
  32.9 0.7 copy-done.3
  33.6 0.0 copy-start.5
  33.6 1.7 weights.1.slabs
  35.3 0.0 copy-start.8
  35.3 0.0 collective-permute-done.a0
  35.3 0.0 copy-done.5
  35.3 0.0 collective-permute-done.1.a1
  35.3 0.0 copy-start.6
  35.3 0.0 collective-permute-done.2.a3
  35.3 2.4 %collective-permute-done.3.a4 = bf16[40,8,256]{2,1,0:T(8,128)(2,1)} collective-permute-done((bf16[40,8,256]{2,1,0:T(8,128)(2,1)}, bf16[40,8,256]{2,1,0:T(8,128)(2,1)}, u32[]{:S(2)}, u32[]{:S(2)}) %collective-permute-start.3) | collective-permute-done | bytes 163872 | tf_op jit(solution)/shard_map/ppermute | solution.py:215
  37.7 0.0 copy-done.4
  37.7 2.2 %slots.1 = bf16[176,8,256]{2,1,0:T(8,128)(2,1)} custom-call(s32[160]{0:T(256)S(1)} %copy-done.4, bf16[40,8,256]{2,1,0:T(8,128)(2,1)S(1)} %collective-permute-done.a0, bf16[40,8,256]{2,1,0:T(8,128)(2,1)} %collective-permute-done.1.a1, bf16[40,8,256]{2,1,0:T(8,128)(2,1)S(1)} %get-tuple-element.14.a2, bf16[40,8,256]{2,1,0:T(8,128)(2,1)} %collective-permute-done.2.a3, ...), custom_call_target="tpu_custom_call" | custom-call | bytes 1310720 | tf_op jit(solution)/shard_map/slots/pallas_call | solution.py:278
  40.0 5.3 %all-to-all-done.jacobian = bf16[160,32,128]{2,1,0:T(8,128)(2,1)} async-done(((bf16[160,32,128]{2,1,0:T(8,128)(2,1)}), bf16[160,32,128]{2,1,0:T(8,128)(2,1)}, u32[]{:S(2)}, u32[]{:S(2)}) %all-to-all-start) | async-done | bytes 1310752 | tf_op jit(solution)/shard_map/all_to_all | solution.py:219
  45.3 3.9 %all-to-all-start.1 = ((bf16[176,8,256]{2,1,0:T(8,128)(2,1)}), bf16[176,8,256]{2,1,0:T(8,128)(2,1)S(1)}, u32[]{:S(2)}, u32[]{:S(2)}) async-start(bf16[176,8,256]{2,1,0:T(8,128)(2,1)} %slots.1), calls=%async_computation.1 | async-start | bytes 1441792 | tf_op jit(solution)/shard_map/all_to_all | solution.py:219
  49.2 0.0 copy-done.8
  49.2 21.3 %all-to-all-done.1.arrived = bf16[176,8,256]{2,1,0:T(8,128)(2,1)S(1)} async-done(((bf16[176,8,256]{2,1,0:T(8,128)(2,1)}), bf16[176,8,256]{2,1,0:T(8,128)(2,1)S(1)}, u32[]{:S(2)}, u32[]{:S(2)}) %all-to-all-start.1) | async-done | bytes 720928 | tf_op jit(solution)/shard_map/all_to_all | solution.py:219
  70.5 0.0 copy-done.6
  70.5 6.5 %terms.1 = f32[64,8,128]{2,1,0:T(8,128)S(1)} custom-call(s32[2]{0:T(128)S(1)} %copy-done.6, f32[512,32]{1,0:T(8,128)S(1)} %copy.15.vectors, f32[2,256]{1,0:T(2,128)S(1)} %div.12.scales, bf16[160,32,128]{2,1,0:T(8,128)(2,1)} %all-to-all-done.jacobian, bf16[176,8,256]{2,1,0:T(8,128)(2,1)S(1)} %all-to-all-done.1.arrived), custom_call_target="tpu_custom_call" | custom-call | flops 2013265920 | bytes 1310720 | tf_op jit(solution)/shard_map/terms/pallas_call | solution.py:291
  77.0 0.0 copy-start.2
  77.0 18.0 %all_to_all.25 = f32[64,8,128]{2,1,0:T(8,128)S(1)} all-to-all(f32[64,8,128]{2,1,0:T(8,128)S(1)} %terms.1), channel_id=1, replica_groups=mesh['y'=8,'x'=4,'z'=8,'c'=2] {'x','z','c'}, dimensions={0} | all-to-all | bytes 524288 | tf_op jit(solution)/shard_map/all_to_all | solution.py:219
  95.1 0.1 reduce_sum.18
  95.1 13.5 %all_to_all.26 = f32[8,8,128]{2,1,0:T(8,128)S(1)} all-to-all(f32[8,8,128]{2,1,0:T(8,128)S(1)} %broadcast_in_dim.7), channel_id=1, replica_groups=mesh['y'=8,'x'=4,'z'=8,'c'=2] {'y'}, dimensions={0} | all-to-all | bytes 65536 | tf_op jit(solution)/shard_map/all_to_all | solution.py:219
  108.7 19.3 %all_to_all.27.summed = f32[64,8,128]{2,1,0:T(8,128)S(1)} all-to-all(f32[64,8,128]{2,1,0:T(8,128)S(1)} %broadcast_in_dim.8), channel_id=1, replica_groups=mesh['y'=8,'x'=4,'z'=8,'c'=2] {'x','z','c'}, dimensions={0} | all-to-all | bytes 524288 | tf_op jit(solution)/shard_map/all_to_all | solution.py:219
  127.9 0.0 copy-done.2
  127.9 43.8 %solve.1 = bf16[3072,256]{1,0:T(8,128)(2,1)} custom-call(f32[64,8,128]{2,1,0:T(8,128)S(1)} %all_to_all.27.summed, f32[256,256]{1,0:T(8,128)S(1)} %copy-done.2, bf16[3072,256]{1,0:T(8,128)(2,1)S(1)} %bitcast.3), custom_call_target="tpu_custom_call" | custom-call | tf_op jit(solution)/shard_map/solve/pallas_call | solution.py:305
  (5 shorter events, 0.1 us)
Async XLA Ops:
  0.0 12.0 %copy-start.9 = (s32[1,5,40]{2,0,1:T(1,128)S(1)}, s32[1,5,40]{2,0,1:T(1,128)}, u32[]{:S(2)}) copy-start(s32[1,5,40]{2,0,1:T(1,128)} %param.15) | copy-start | bytes 2404
  0.0 12.1 %copy-start = (bf16[384,8,256]{2,1,0:T(8,128)(2,1)S(1)}, bf16[384,8,256]{2,1,0:T(8,128)(2,1)}, u32[]{:S(2)}) copy-start(bf16[384,8,256]{2,1,0:T(8,128)(2,1)} %ensemble.1) | copy-start | bytes 4718596
  0.0 29.3 %copy-start.10 = (f32[512]{0:T(512)S(1)}, f32[512]{0:T(512)}, u32[]{:S(2)}) copy-start(f32[512]{0:T(512)} %param.13) | copy-start | bytes 6148
  0.0 30.5 %copy-start.7 = (f32[512,32]{0,1:T(8,128)S(1)}, f32[512,32]{0,1:T(8,128)}, u32[]{:S(2)}) copy-start(f32[512,32]{0,1:T(8,128)} %param.12) | copy-start | bytes 196612
  0.0 45.3 %all-to-all-start = ((bf16[160,32,128]{2,1,0:T(8,128)(2,1)}), bf16[160,32,128]{2,1,0:T(8,128)(2,1)}, u32[]{:S(2)}, u32[]{:S(2)}) async-start(bf16[160,32,128]{2,1,0:T(8,128)(2,1)} %jacobian.1), calls=%async_computation | async-start | bytes 2621440 | tf_op jit(solution)/shard_map/all_to_all | solution.py:219
  12.0 20.9 %copy-start.1 = (bf16[160,32,128]{2,1,0:T(8,128)(2,1)S(1)}, bf16[160,32,128]{2,1,0:T(8,128)(2,1)}, u32[]{:S(2)}) copy-start(bf16[160,32,128]{2,1,0:T(8,128)(2,1)} %jacobian.1) | copy-start | bytes 3932164
  13.9 21.4 %collective-permute-start = (bf16[40,8,256]{2,1,0:T(8,128)(2,1)}, bf16[40,8,256]{2,1,0:T(8,128)(2,1)S(1)}, u32[]{:S(2)}, u32[]{:S(2)}) collective-permute-start(bf16[40,8,256]{2,1,0:T(8,128)(2,1)} %get-tuple-element.12), channel_id=1, source_target_pairs={{0,480},{16,496},{32,0},{48,16},{64,32},{80,48},{96,64},{112,80},{... | collective-permute-start | bytes 491528 | tf_op jit(solution)/shard_map/ppermute | solution.py:215
  21.4 13.9 %collective-permute-start.1 = (bf16[40,8,256]{2,1,0:T(8,128)(2,1)}, bf16[40,8,256]{2,1,0:T(8,128)(2,1)}, u32[]{:S(2)}, u32[]{:S(2)}) collective-permute-start(bf16[40,8,256]{2,1,0:T(8,128)(2,1)} %get-tuple-element.13), channel_id=1, source_target_pairs={{0,496},{16,0},{32,16},{48,32},{64,48},{80,64},{96,80},{112,96},{1... | collective-permute-start | bytes 491528 | tf_op jit(solution)/shard_map/ppermute | solution.py:215
  24.2 11.1 %collective-permute-start.2 = (bf16[40,8,256]{2,1,0:T(8,128)(2,1)}, bf16[40,8,256]{2,1,0:T(8,128)(2,1)}, u32[]{:S(2)}, u32[]{:S(2)}) collective-permute-start(bf16[40,8,256]{2,1,0:T(8,128)(2,1)} %get-tuple-element.15), channel_id=1, source_target_pairs={{0,16},{16,32},{32,48},{48,64},{64,80},{80,96},{96,112},{112,128},... | collective-permute-start | bytes 491528 | tf_op jit(solution)/shard_map/ppermute | solution.py:215
  26.7 11.0 %collective-permute-start.3 = (bf16[40,8,256]{2,1,0:T(8,128)(2,1)}, bf16[40,8,256]{2,1,0:T(8,128)(2,1)}, u32[]{:S(2)}, u32[]{:S(2)}) collective-permute-start(bf16[40,8,256]{2,1,0:T(8,128)(2,1)} %get-tuple-element.16), channel_id=1, source_target_pairs={{0,32},{16,48},{32,64},{48,80},{64,96},{80,112},{96,128},{112,144}... | collective-permute-start | bytes 491528 | tf_op jit(solution)/shard_map/ppermute | solution.py:215
  32.8 4.9 %copy-start.4 = (s32[160]{0:T(256)S(1)}, s32[160]{0:T(256)}, u32[]{:S(2)}) copy-start(s32[160]{0:T(256)} %slot.1) | copy-start | bytes 1924
  32.9 0.7 copy-start.3
  33.6 1.7 copy-start.5
  35.3 13.9 %copy-start.8 = (f32[512]{0:T(512)S(1)}, f32[512]{0:T(512)}, u32[]{:S(2)}) copy-start(f32[512]{0:T(512)} %get-tuple-element.20) | copy-start | bytes 6148
  35.3 35.2 %copy-start.6 = (s32[2]{0:T(128)S(1)}, s32[2]{0:T(128)}, u32[]{:S(2)}) copy-start(s32[2]{0:T(128)} %copy-done.5) | copy-start | bytes 28
  45.3 25.2 %all-to-all-start.1 = ((bf16[176,8,256]{2,1,0:T(8,128)(2,1)}), bf16[176,8,256]{2,1,0:T(8,128)(2,1)S(1)}, u32[]{:S(2)}, u32[]{:S(2)}) async-start(bf16[176,8,256]{2,1,0:T(8,128)(2,1)} %slots.1), calls=%async_computation.1 | async-start | bytes 1441792 | tf_op jit(solution)/shard_map/all_to_all | solution.py:219
  77.0 50.9 %copy-start.2 = (f32[256,256]{1,0:T(8,128)S(1)}, f32[256,256]{1,0:T(8,128)}, u32[]{:S(2)}) copy-start(f32[256,256]{1,0:T(8,128)} %basis.1) | copy-start | bytes 786436

commit v3 on v2

--- a/solution.py
+++ b/solution.py
@@ -93,7 +93,7 @@
     lax.fori_loop(0, peers, one, 0)
 
 
-def terms_kernel(place, vectors, scales, jacobian, arrived, out):
+def turn_kernel(place, vectors, scales, jacobian, out):
     peers = vectors.shape[0] // vectors.shape[1]
     share = jacobian.shape[0] // peers
     first = place[0] * share
@@ -105,6 +105,22 @@
         block = vectors[h * half : (h + 1) * half, :]
         wide = jnp.where(same, jnp.concatenate([block] * 8, axis=1), 0.0) * scales[h : h + 1, :]
         turns.append(split(wide.T))
+    for f in range(share):
+        live = jnp.where(first + f < count, 1.0, 0.0).astype(F32)
+        for h in range(2):
+            block = jnp.concatenate(
+                [jacobian[(h * 8 + s) * share + f] for s in range(8)], axis=0
+            )
+            high, low = turns[h]
+            turned = (nn(high, block) + nn(low, block)) * live
+            out[f, h * half : (h + 1) * half, :] = turned.astype(BF16)
+
+
+def terms_kernel(place, turned, arrived, out):
+    share = turned.shape[0]
+    peers = arrived.shape[0] // (share + 1)
+    first = place[0] * share
+    count = place[1]
     b = arrived[share].astype(F32)
     for source in range(1, peers):
         b = b + arrived[source * (share + 1) + share].astype(F32)
@@ -112,19 +128,11 @@
     pull = jnp.zeros((8, MEM), F32)
     for f in range(share):
         live = jnp.where(first + f < count, 1.0, 0.0).astype(F32)
-        parts = []
-        for h in range(2):
-            block = jnp.concatenate(
-                [jacobian[(h * 8 + s) * share + f] for s in range(8)], axis=0
-            )
-            high, low = turns[h]
-            parts.append(((nn(high, block) + nn(low, block)) * live).astype(BF16))
-        turned = jnp.concatenate(parts, axis=0)
         column = jnp.concatenate(
             [arrived[s * (share + 1) + f] for s in range(peers)], axis=0
         )
         flipped = column.astype(F32).T.astype(BF16)
-        whitened = nt(flipped, turned).astype(BF16)
+        whitened = nt(flipped, turned[f]).astype(BF16)
         gram = gram + nt(whitened, whitened)
         mine = iota2(8, 128, 0) == f % 8
         high, low = split(jnp.where(mine, b[:, 128 * (f // 8) : 128 * (f // 8) + 128] * live, 0.0))
@@ -288,15 +296,25 @@
     payload, sensitivity = lax.optimization_barrier((payload, sensitivity))
     arrived = swap(payload, CHAN)
 
+    turned = pl.pallas_call(
+        turn_kernel,
+        out_shape=jax.ShapeDtypeStruct((share, peers * width, 128), BF16),
+        in_specs=[SM, VM, VM, VM],
+        out_specs=VM,
+        compiler_params=PARAMS,
+        cost_estimate=cost(4 * 512 * share * 256 * 128, 4 * jacobian.size),
+        name="turn",
+    )(place, error_vectors, 1.0 / jnp.sqrt(error_values).reshape(2, members), sensitivity)
+
     tiles = pl.pallas_call(
         terms_kernel,
         out_shape=jax.ShapeDtypeStruct((64, 8, 128), F32),
-        in_specs=[SM, VM, VM, VM, VM],
+        in_specs=[SM, VM, VM],
         out_specs=VM,
         compiler_params=PARAMS,
-        cost_estimate=cost(4 * 512 * share * 256 * 384, 2 * jacobian.size),
+        cost_estimate=cost(2 * 512 * share * 256 * 384, 2 * jacobian.size),
         name="terms",
-    )(place, error_vectors, 1.0 / jnp.sqrt(error_values).reshape(2, members), sensitivity, arrived)
+    )(place, turned, arrived)
 
     summed = summed_everywhere(tiles)
 

time: 172 us -> 169 us (0.983)
  waiting for transfers between devices: 29 us -> 26.2 us
    all_to_all x2, waiting for transfers between devices: 26.6 us -> 23.2 us  [swap(): return lax.all_to_all(x, axis, 0, 0, tiled=True)]
    pallas_call x1, Pallas kernels: 6.49 us -> 3.29 us  [local(): pl.pallas_call(terms_kernel, out_shape=jax.ShapeDtypeStruct((64, 8, 128),...]
    pallas_call x0 -> x1, Pallas kernels: none -> 3.13 us  [local(): pl.pallas_call(turn_kernel, out_shape=jax.ShapeDtypeStruct((share, peers...]
  transfers between devices with their start and end apart: 6 -> 6, of which waited for: 3 -> 3; matrix products, arithmetic and copies ran while one was open for 2% -> 1% of each run, Pallas kernels for 3% -> 5%
where the time goes in v3:
time: 169 us
  Pallas kernels  55.8 us (33%)
  blocking collectives  50.8 us (30%)
  starting transfers between devices  31.5 us (19%)
  waiting for transfers between devices  26.2 us (16%)
  local copies, waits for them, and re-layouts  2.6 us (2%)
    all_to_all x3, blocking collectives, swap(): return lax.all_to_all(x, axis, 0, 0, tiled=True)  50.8 us
    pallas_call x1, Pallas kernels, local(): pl.pallas_call(solve_kernel, out_shape=jax.ShapeDtypeStruct(flat_rows.sha...  43.8 us
    all_to_all x2, waiting for transfers between devices, swap(): return lax.all_to_all(x, axis, 0, 0, tiled=True)  23.2 us
    all_to_all x2, starting transfers between devices, swap(): return lax.all_to_all(x, axis, 0, 0, tiled=True)  16.1 us
    ppermute x4, starting transfers between devices, send_by(): lax.ppermute(value, axis, [(s, (s + steps) % count) for s in range(count)])  15.4 us
  transfers between devices with their start and end apart: 6, of which 3 were waited for; matrix products, arithmetic and copies ran while one was open for 1% of the time, Pallas kernels for 5%

profile of v3, /device:TPU:1, one launch (start us, length us, event | category | flops | bytes accessed | tf_op | source)
XLA Modules:
  0.0 168.6 jit_solution(4274465780889026864)
XLA Ops:
  0.0 0.0 copy-start.9
  0.0 0.0 copy-start
  0.0 12.0 %all-to-all-start = ((bf16[160,32,128]{2,1,0:T(8,128)(2,1)}), bf16[160,32,128]{2,1,0:T(8,128)(2,1)}, u32[]{:S(2)}, u32[]{:S(2)}) async-start(bf16[160,32,128]{2,1,0:T(8,128)(2,1)} %jacobian.1), calls=%async_computation | async-start | bytes 2621440 | tf_op jit(solution)/shard_map/all_to_all | solution.py:227
  12.0 0.0 copy-done.9
  12.0 0.0 copy-start.10
  12.0 0.0 copy-start.7
  12.0 0.0 copy-start.1
  12.0 0.1 reshape.17.pick
  12.1 0.0 copy-done
  12.1 1.7 %pick.1 = (bf16[40,8,256]{2,1,0:T(8,128)(2,1)}, bf16[40,8,256]{2,1,0:T(8,128)(2,1)}, bf16[40,8,256]{2,1,0:T(8,128)(2,1)S(1)}, bf16[40,8,256]{2,1,0:T(8,128)(2,1)}, bf16[40,8,256]{2,1,0:T(8,128)(2,1)}) custom-call(s32[200]{0:T(256)S(1)} %reshape.17.pick, bf16[384,8,256]{2,1,0:T(8,128)(2,1)S(1)} %copy-done), custom_call_target="tpu_custom_call" | custom-call | bytes 1572864 | tf_op jit(solution)/shard_map/pick/pallas_call | solution.py:258
  13.9 7.5 %collective-permute-start = (bf16[40,8,256]{2,1,0:T(8,128)(2,1)}, bf16[40,8,256]{2,1,0:T(8,128)(2,1)S(1)}, u32[]{:S(2)}, u32[]{:S(2)}) collective-permute-start(bf16[40,8,256]{2,1,0:T(8,128)(2,1)} %get-tuple-element.12), channel_id=1, source_target_pairs={{0,480},{16,496},{32,0},{48,16},{64,32},{80,48},{96,64},{112,80},{... | collective-permute-start | bytes 491528 | tf_op jit(solution)/shard_map/ppermute | solution.py:223
  21.4 2.8 %collective-permute-start.1 = (bf16[40,8,256]{2,1,0:T(8,128)(2,1)}, bf16[40,8,256]{2,1,0:T(8,128)(2,1)}, u32[]{:S(2)}, u32[]{:S(2)}) collective-permute-start(bf16[40,8,256]{2,1,0:T(8,128)(2,1)} %get-tuple-element.13), channel_id=1, source_target_pairs={{0,496},{16,0},{32,16},{48,32},{64,48},{80,64},{96,80},{112,96},{1... | collective-permute-start | bytes 491528 | tf_op jit(solution)/shard_map/ppermute | solution.py:223
  24.2 2.5 %collective-permute-start.2 = (bf16[40,8,256]{2,1,0:T(8,128)(2,1)}, bf16[40,8,256]{2,1,0:T(8,128)(2,1)}, u32[]{:S(2)}, u32[]{:S(2)}) collective-permute-start(bf16[40,8,256]{2,1,0:T(8,128)(2,1)} %get-tuple-element.15), channel_id=1, source_target_pairs={{0,16},{16,32},{32,48},{48,64},{64,80},{80,96},{96,112},{112,128},... | collective-permute-start | bytes 491528 | tf_op jit(solution)/shard_map/ppermute | solution.py:223
  26.7 2.6 %collective-permute-start.3 = (bf16[40,8,256]{2,1,0:T(8,128)(2,1)}, bf16[40,8,256]{2,1,0:T(8,128)(2,1)}, u32[]{:S(2)}, u32[]{:S(2)}) collective-permute-start(bf16[40,8,256]{2,1,0:T(8,128)(2,1)} %get-tuple-element.16), channel_id=1, source_target_pairs={{0,32},{16,48},{32,64},{48,80},{64,96},{80,112},{96,128},{112,144}... | collective-permute-start | bytes 491528 | tf_op jit(solution)/shard_map/ppermute | solution.py:223
  29.3 0.0 copy-done.10
  29.3 0.6 broadcast_divide_fusion
  30.5 0.7 div.15.inverses
  31.2 0.0 copy-done.7
  31.2 0.1 copy.13.innovation
  31.3 1.0 copy.15.vectors
  32.3 0.0 copy-start.6
  32.3 0.1 pad_add_fusion.place
  32.4 0.0 copy-done.1
  32.4 0.0 copy-start.3
  32.4 0.7 copy-done.3
  33.1 0.0 copy-start.4
  33.1 1.7 weights.1.slabs
  34.7 0.0 collective-permute-done.a0
  34.7 0.0 copy-done.4
  34.7 0.0 collective-permute-done.1.a1
  34.8 0.0 collective-permute-done.2.a3
  34.8 3.0 %collective-permute-done.3.a4 = bf16[40,8,256]{2,1,0:T(8,128)(2,1)} collective-permute-done((bf16[40,8,256]{2,1,0:T(8,128)(2,1)}, bf16[40,8,256]{2,1,0:T(8,128)(2,1)}, u32[]{:S(2)}, u32[]{:S(2)}) %collective-permute-start.3) | collective-permute-done | bytes 163872 | tf_op jit(solution)/shard_map/ppermute | solution.py:223
  37.7 0.0 copy-done.6
  37.7 0.0 copy-start.8
  37.7 0.0 copy-start.5
  37.7 2.2 %slots.1 = bf16[176,8,256]{2,1,0:T(8,128)(2,1)} custom-call(s32[160]{0:T(256)S(1)} %copy-done.6, bf16[40,8,256]{2,1,0:T(8,128)(2,1)S(1)} %collective-permute-done.a0, bf16[40,8,256]{2,1,0:T(8,128)(2,1)} %collective-permute-done.1.a1, bf16[40,8,256]{2,1,0:T(8,128)(2,1)S(1)} %get-tuple-element.14.a2, bf16[40,8,256]{2,1,0:T(8,128)(2,1)} %collective-permute-done.2.a3, ...), custom_call_target="tpu_custom_call" | custom-call | bytes 1310720 | tf_op jit(solution)/shard_map/slots/pallas_call | solution.py:286
  40.0 5.3 %all-to-all-done.jacobian = bf16[160,32,128]{2,1,0:T(8,128)(2,1)} async-done(((bf16[160,32,128]{2,1,0:T(8,128)(2,1)}), bf16[160,32,128]{2,1,0:T(8,128)(2,1)}, u32[]{:S(2)}, u32[]{:S(2)}) %all-to-all-start) | async-done | bytes 1310752 | tf_op jit(solution)/shard_map/all_to_all | solution.py:227
  45.3 4.2 %all-to-all-start.1 = ((bf16[176,8,256]{2,1,0:T(8,128)(2,1)}), bf16[176,8,256]{2,1,0:T(8,128)(2,1)}, u32[]{:S(2)}, u32[]{:S(2)}) async-start(bf16[176,8,256]{2,1,0:T(8,128)(2,1)} %slots.1), calls=%async_computation.1 | async-start | bytes 1441792 | tf_op jit(solution)/shard_map/all_to_all | solution.py:227
  49.5 0.0 copy-done.8
  49.5 0.0 copy-done.5
  49.5 3.1 %turn.1.turned = bf16[10,512,128]{2,1,0:T(8,128)(2,1)S(1)} custom-call(s32[2]{0:T(128)S(1)} %copy-done.5, f32[512,32]{1,0:T(8,128)S(1)} %copy.15.vectors, f32[2,256]{1,0:T(2,128)S(1)} %div.12.scales, bf16[160,32,128]{2,1,0:T(8,128)(2,1)} %all-to-all-done.jacobian), custom_call_target="tpu_custom_call" | custom-call | flops 671088640 | bytes 2621440 | tf_op jit(solution)/shard_map/turn/pallas_call | solution.py:299
  52.6 18.0 %all-to-all-done.1.arrived = bf16[176,8,256]{2,1,0:T(8,128)(2,1)} async-done(((bf16[176,8,256]{2,1,0:T(8,128)(2,1)}), bf16[176,8,256]{2,1,0:T(8,128)(2,1)}, u32[]{:S(2)}, u32[]{:S(2)}) %all-to-all-start.1) | async-done | bytes 720928 | tf_op jit(solution)/shard_map/all_to_all | solution.py:227
  70.6 3.3 %terms.1 = f32[64,8,128]{2,1,0:T(8,128)S(1)} custom-call(s32[2]{0:T(128)S(1)} %copy-done.5, bf16[10,512,128]{2,1,0:T(8,128)(2,1)S(1)} %turn.1.turned, bf16[176,8,256]{2,1,0:T(8,128)(2,1)} %all-to-all-done.1.arrived), custom_call_target="tpu_custom_call" | custom-call | flops 1006632960 | bytes 1310720 | tf_op jit(solution)/shard_map/terms/pallas_call | solution.py:309
  73.9 0.0 copy-start.2
  73.9 18.0 %all_to_all.25 = f32[64,8,128]{2,1,0:T(8,128)S(1)} all-to-all(f32[64,8,128]{2,1,0:T(8,128)S(1)} %terms.1), channel_id=1, replica_groups=mesh['y'=8,'x'=4,'z'=8,'c'=2] {'x','z','c'}, dimensions={0} | all-to-all | bytes 524288 | tf_op jit(solution)/shard_map/all_to_all | solution.py:227
  91.9 0.1 reduce_sum.18
  92.0 13.5 %all_to_all.26 = f32[8,8,128]{2,1,0:T(8,128)S(1)} all-to-all(f32[8,8,128]{2,1,0:T(8,128)S(1)} %broadcast_in_dim.7), channel_id=1, replica_groups=mesh['y'=8,'x'=4,'z'=8,'c'=2] {'y'}, dimensions={0} | all-to-all | bytes 65536 | tf_op jit(solution)/shard_map/all_to_all | solution.py:227
  105.6 19.3 %all_to_all.27.summed = f32[64,8,128]{2,1,0:T(8,128)S(1)} all-to-all(f32[64,8,128]{2,1,0:T(8,128)S(1)} %broadcast_in_dim.8), channel_id=1, replica_groups=mesh['y'=8,'x'=4,'z'=8,'c'=2] {'x','z','c'}, dimensions={0} | all-to-all | bytes 524288 | tf_op jit(solution)/shard_map/all_to_all | solution.py:227
  124.8 0.0 copy-done.2
  124.8 43.8 %solve.1 = bf16[3072,256]{1,0:T(8,128)(2,1)} custom-call(f32[64,8,128]{2,1,0:T(8,128)S(1)} %all_to_all.27.summed, f32[256,256]{1,0:T(8,128)S(1)} %copy-done.2, bf16[3072,256]{1,0:T(8,128)(2,1)S(1)} %bitcast.3), custom_call_target="tpu_custom_call" | custom-call | tf_op jit(solution)/shard_map/solve/pallas_call | solution.py:323
  (5 shorter events, 0.1 us)
Async XLA Ops:
  0.0 12.0 %copy-start.9 = (s32[1,5,40]{2,0,1:T(1,128)S(1)}, s32[1,5,40]{2,0,1:T(1,128)}, u32[]{:S(2)}) copy-start(s32[1,5,40]{2,0,1:T(1,128)} %param.15) | copy-start | bytes 2404
  0.0 12.1 %copy-start = (bf16[384,8,256]{2,1,0:T(8,128)(2,1)S(1)}, bf16[384,8,256]{2,1,0:T(8,128)(2,1)}, u32[]{:S(2)}) copy-start(bf16[384,8,256]{2,1,0:T(8,128)(2,1)} %ensemble.1) | copy-start | bytes 4718596
  0.0 45.3 %all-to-all-start = ((bf16[160,32,128]{2,1,0:T(8,128)(2,1)}), bf16[160,32,128]{2,1,0:T(8,128)(2,1)}, u32[]{:S(2)}, u32[]{:S(2)}) async-start(bf16[160,32,128]{2,1,0:T(8,128)(2,1)} %jacobian.1), calls=%async_computation | async-start | bytes 2621440 | tf_op jit(solution)/shard_map/all_to_all | solution.py:227
  12.0 17.3 %copy-start.10 = (f32[512]{0:T(512)S(1)}, f32[512]{0:T(512)}, u32[]{:S(2)}) copy-start(f32[512]{0:T(512)} %param.13) | copy-start | bytes 6148
  12.0 19.2 %copy-start.7 = (f32[160,32]{0,1:T(8,128)S(1)}, f32[160,32]{0,1:T(8,128)}, u32[]{:S(2)}) copy-start(f32[160,32]{0,1:T(8,128)} %param.11) | copy-start | bytes 61444
  12.0 20.4 %copy-start.1 = (bf16[160,32,128]{2,1,0:T(8,128)(2,1)S(1)}, bf16[160,32,128]{2,1,0:T(8,128)(2,1)}, u32[]{:S(2)}) copy-start(bf16[160,32,128]{2,1,0:T(8,128)(2,1)} %jacobian.1) | copy-start | bytes 3932164
  13.9 20.9 %collective-permute-start = (bf16[40,8,256]{2,1,0:T(8,128)(2,1)}, bf16[40,8,256]{2,1,0:T(8,128)(2,1)S(1)}, u32[]{:S(2)}, u32[]{:S(2)}) collective-permute-start(bf16[40,8,256]{2,1,0:T(8,128)(2,1)} %get-tuple-element.12), channel_id=1, source_target_pairs={{0,480},{16,496},{32,0},{48,16},{64,32},{80,48},{96,64},{112,80},{... | collective-permute-start | bytes 491528 | tf_op jit(solution)/shard_map/ppermute | solution.py:223
  21.4 13.3 %collective-permute-start.1 = (bf16[40,8,256]{2,1,0:T(8,128)(2,1)}, bf16[40,8,256]{2,1,0:T(8,128)(2,1)}, u32[]{:S(2)}, u32[]{:S(2)}) collective-permute-start(bf16[40,8,256]{2,1,0:T(8,128)(2,1)} %get-tuple-element.13), channel_id=1, source_target_pairs={{0,496},{16,0},{32,16},{48,32},{64,48},{80,64},{96,80},{112,96},{1... | collective-permute-start | bytes 491528 | tf_op jit(solution)/shard_map/ppermute | solution.py:223
  24.2 10.6 %collective-permute-start.2 = (bf16[40,8,256]{2,1,0:T(8,128)(2,1)}, bf16[40,8,256]{2,1,0:T(8,128)(2,1)}, u32[]{:S(2)}, u32[]{:S(2)}) collective-permute-start(bf16[40,8,256]{2,1,0:T(8,128)(2,1)} %get-tuple-element.15), channel_id=1, source_target_pairs={{0,16},{16,32},{32,48},{48,64},{64,80},{80,96},{96,112},{112,128},... | collective-permute-start | bytes 491528 | tf_op jit(solution)/shard_map/ppermute | solution.py:223
  26.7 11.0 %collective-permute-start.3 = (bf16[40,8,256]{2,1,0:T(8,128)(2,1)}, bf16[40,8,256]{2,1,0:T(8,128)(2,1)}, u32[]{:S(2)}, u32[]{:S(2)}) collective-permute-start(bf16[40,8,256]{2,1,0:T(8,128)(2,1)} %get-tuple-element.16), channel_id=1, source_target_pairs={{0,32},{16,48},{32,64},{48,80},{64,96},{80,112},{96,128},{112,144}... | collective-permute-start | bytes 491528 | tf_op jit(solution)/shard_map/ppermute | solution.py:223
  32.3 5.5 %copy-start.6 = (s32[160]{0:T(256)S(1)}, s32[160]{0:T(256)}, u32[]{:S(2)}) copy-start(s32[160]{0:T(256)} %slot.1) | copy-start | bytes 1924
  32.4 0.7 copy-start.3
  33.1 1.7 copy-start.4
  37.7 11.7 %copy-start.8 = (f32[512]{0:T(512)S(1)}, f32[512]{0:T(512)}, u32[]{:S(2)}) copy-start(f32[512]{0:T(512)} %get-tuple-element.20) | copy-start | bytes 6148
  37.7 11.7 %copy-start.5 = (s32[2]{0:T(128)S(1)}, s32[2]{0:T(128)}, u32[]{:S(2)}) copy-start(s32[2]{0:T(128)} %copy-done.4) | copy-start | bytes 28
  45.3 25.3 %all-to-all-start.1 = ((bf16[176,8,256]{2,1,0:T(8,128)(2,1)}), bf16[176,8,256]{2,1,0:T(8,128)(2,1)}, u32[]{:S(2)}, u32[]{:S(2)}) async-start(bf16[176,8,256]{2,1,0:T(8,128)(2,1)} %slots.1), calls=%async_computation.1 | async-start | bytes 1441792 | tf_op jit(solution)/shard_map/all_to_all | solution.py:227
  73.9 50.9 %copy-start.2 = (f32[256,256]{1,0:T(8,128)S(1)}, f32[256,256]{1,0:T(8,128)}, u32[]{:S(2)}) copy-start(f32[256,256]{1,0:T(8,128)} %basis.1) | copy-start | bytes 786436

commit v4 on v3

--- a/solution.py
+++ b/solution.py
@@ -8,8 +8,9 @@
 
 TILE = ("y", "x")
 CHAN = ("z", "c")
-NEAR = ("x", "z", "c")
+NEAR = ("x", "z")
 FAR = "y"
+CORE = "c"
 MEM = 256
 HI = lax.Precision.HIGHEST
 F32 = jnp.float32
@@ -116,7 +117,7 @@
             out[f, h * half : (h + 1) * half, :] = turned.astype(BF16)
 
 
-def terms_kernel(place, turned, arrived, out):
+def terms_kernel(place, turned, arrived, keep, give):
     share = turned.shape[0]
     peers = arrived.shape[0] // (share + 1)
     first = place[0] * share
@@ -137,15 +138,21 @@
         mine = iota2(8, 128, 0) == f % 8
         high, low = split(jnp.where(mine, b[:, 128 * (f // 8) : 128 * (f // 8) + 128] * live, 0.0))
         pull = pull + (nn(high, column) + nn(low, column))
-    out[0:16] = gram[0:128, 0:128].reshape(16, 8, 128)
-    out[16:32] = gram[128:256, 0:128].reshape(16, 8, 128)
-    out[32:48] = gram[128:256, 128:256].reshape(16, 8, 128)
     total = jnp.sum(pull, axis=0, keepdims=True)
     last = jnp.concatenate(
         [total[:, 0:128], total[:, 128:256], jnp.zeros((6, 128), F32)], axis=0
     )
-    out[48:64] = jnp.zeros((16, 8, 128), F32)
-    out[48] = last
+    halves = (
+        (gram[0:128, 0:128], gram[128:192, 0:128], last),
+        (gram[128:256, 128:256], gram[192:256, 0:128], jnp.zeros_like(last)),
+    )
+    even = lax.rem(place[0], 2) == 0
+    for out, (first_half, second_half) in ((keep, halves), (give, halves[::-1])):
+        x, y, z = (jnp.where(even, p, q) for p, q in zip(first_half, second_half))
+        out[0:16] = x.reshape(16, 8, 128)
+        out[16:24] = y.reshape(8, 8, 128)
+        out[24] = z
+        out[25:32] = jnp.zeros((7, 8, 128), F32)
 
 
 def lower_half(x):
@@ -153,11 +160,20 @@
     return jnp.where(i > j, x, jnp.where(i == j, 0.5 * x, 0.0))
 
 
-def solve_kernel(summed, basis, ensemble, out, system, inverse, rows, held, sems):
+def solve_kernel(
+    place, mine, other, basis, ensemble, out, system, inverse, rows, held, sems
+):
     eye = (iota2(MEM, MEM, 0) == iota2(MEM, MEM, 1)).astype(F32)
-    g00 = summed[0:16].reshape(128, 128)
-    g10 = summed[16:32].reshape(128, 128)
-    g11 = summed[32:48].reshape(128, 128)
+    even = lax.rem(place[0], 2) == 0
+    low = jnp.where(even, mine[...], other[...])
+    high = jnp.where(even, other[...], mine[...])
+    g00 = low[0:16].reshape(128, 128)
+    g11 = high[0:16].reshape(128, 128)
+    g10 = jnp.concatenate(
+        [low[16:24].reshape(64, 128), high[16:24].reshape(64, 128)], axis=0
+    )
+    last = low[24]
+    pull = jnp.concatenate([last[0:1, :], last[1:2, :]], axis=1)
     a = jnp.concatenate(
         [jnp.concatenate([g00, g10.T], axis=1), jnp.concatenate([g10, g11], axis=1)], axis=0
     ) + (MEM - 1.0) * eye
@@ -176,7 +192,7 @@
         step, _ = state
         x = inverse[...]
         residual = nt(nn(x, system[...], HI), x, HI) - eye
-        inverse[...] = x - nn(lower_half(residual), x, HI)
+        inverse[...] = x - nn(lower_half(residual), x)
         return step + 1, jnp.sum(residual * residual)
 
     _, size = lax.while_loop(go_on, refine, (jnp.int32(0), jnp.float32(1.0)))
@@ -201,9 +217,7 @@
         inverse[...] = rows[:, MEM : 2 * MEM]
 
     x = inverse[...]
-    last = summed[48]
-    pull = jnp.concatenate([last[0:1, :], last[1:2, :]], axis=1)
-    halfway = nt(x, jnp.broadcast_to(pull, (MEM, MEM)), HI)
+    halfway = jnp.sum(x * pull, axis=1, keepdims=True)
     target = (MEM - 1.0) ** 0.5 * basis[...] + halfway
     transform = nn(x.T, target, HI).astype(BF16)
     copies = []
@@ -227,11 +241,17 @@
     return lax.all_to_all(x, axis, 0, 0, tiled=True)
 
 
-def summed_everywhere(tiles):
+def other_core(x):
+    return lax.ppermute(x, CORE, [(0, 1), (1, 0)])
+
+
+def summed_everywhere(keep, give):
+    tiles = keep + other_core(give)
     mine = jnp.sum(swap(tiles, NEAR), axis=0, keepdims=True)
     far = lax.axis_size(FAR)
     mine = jnp.sum(swap(jnp.broadcast_to(mine, (far, 8, 128)), FAR), axis=0, keepdims=True)
-    return swap(jnp.broadcast_to(mine, (tiles.shape[0], 8, 128)), NEAR)
+    mine = swap(jnp.broadcast_to(mine, tiles.shape), NEAR)
+    return mine, other_core(mine)
 
 
 def local(
@@ -306,24 +326,24 @@
         name="turn",
     )(place, error_vectors, 1.0 / jnp.sqrt(error_values).reshape(2, members), sensitivity)
 
-    tiles = pl.pallas_call(
+    keep, give = pl.pallas_call(
         terms_kernel,
-        out_shape=jax.ShapeDtypeStruct((64, 8, 128), F32),
+        out_shape=[jax.ShapeDtypeStruct((32, 8, 128), F32)] * 2,
         in_specs=[SM, VM, VM],
-        out_specs=VM,
+        out_specs=[VM, VM],
         compiler_params=PARAMS,
         cost_estimate=cost(2 * 512 * share * 256 * 384, 2 * jacobian.size),
         name="terms",
     )(place, turned, arrived)
 
-    summed = summed_everywhere(tiles)
+    mine, other = summed_everywhere(keep, give)
 
     chunks = 6
     flat_rows = ensemble.reshape(-1, members)
     updated = pl.pallas_call(
         solve_kernel,
         out_shape=jax.ShapeDtypeStruct(flat_rows.shape, BF16),
-        in_specs=[VM, VM, VM],
+        in_specs=[SM, VM, VM, VM, VM],
         out_specs=pl.BlockSpec(memory_space=pl.ANY),
         scratch_shapes=[
             pltpu.VMEM((members, members), F32),
@@ -334,7 +354,7 @@
         ],
         compiler_params=PARAMS,
         name="solve",
-    )(summed, ensemble_vectors, flat_rows)
+    )(place, mine, other, ensemble_vectors, flat_rows)
     return updated.reshape(ensemble.shape)
 
 

time: 169 us -> 170 us (level)
  blocking collectives: 50.8 us -> 41.1 us
  starting transfers between devices: 31.5 us -> 39.6 us
  waiting for transfers between devices: 26.2 us -> 28.5 us
    all_to_all x3, blocking collectives: 50.8 us -> 41.1 us  [swap(): return lax.all_to_all(x, axis, 0, 0, tiled=True)]
    ppermute x0 -> x2, starting transfers between devices: none -> 8.07 us  [other_core(): return lax.ppermute(x, CORE, [(0, 1), (1, 0)])]
    ppermute x0 -> x2, waiting for transfers between devices: none -> 2.28 us  [other_core(): return lax.ppermute(x, CORE, [(0, 1), (1, 0)])]
  transfers between devices with their start and end apart: 6 -> 8, of which waited for: 3 -> 5; matrix products, arithmetic and copies ran while one was open for 1% -> 1% of each run, Pallas kernels for 5% -> 5%
where the time goes in v4:
time: 170 us; the launch traced here: 169 us
  Pallas kernels  55.8 us (33%)
  blocking collectives  41.1 us (24%)
  starting transfers between devices  39.6 us (23%)
  waiting for transfers between devices  28.5 us (17%)
  local copies, waits for them, and re-layouts  2.59 us (2%)
    pallas_call x1, Pallas kernels, local(): pl.pallas_call(solve_kernel, out_shape=jax.ShapeDtypeStruct(flat_rows.sha...  43.7 us
    all_to_all x3, blocking collectives, swap(): return lax.all_to_all(x, axis, 0, 0, tiled=True)  41.1 us
    all_to_all x2, waiting for transfers between devices, swap(): return lax.all_to_all(x, axis, 0, 0, tiled=True)  23.3 us
    all_to_all x2, starting transfers between devices, swap(): return lax.all_to_all(x, axis, 0, 0, tiled=True)  16.1 us
    ppermute x4, starting transfers between devices, send_by(): lax.ppermute(value, axis, [(s, (s + steps) % count) for s in range(count)])  15.4 us
    ppermute x2, starting transfers between devices, other_core(): return lax.ppermute(x, CORE, [(0, 1), (1, 0)])  8.07 us
  transfers between devices with their start and end apart: 8, of which 5 were waited for; matrix products, arithmetic and copies ran while one was open for 1% of the time, Pallas kernels for 5%

profile of v4, /device:TPU:1, one launch (start us, length us, event | category | flops | bytes accessed | tf_op | source)
XLA Modules:
  0.0 169.2 jit_solution(9386999378194312836)
XLA Ops:
  0.0 0.0 copy-start.9
  0.0 0.0 copy-start
  0.0 12.0 %all-to-all-start = ((bf16[160,32,128]{2,1,0:T(8,128)(2,1)}), bf16[160,32,128]{2,1,0:T(8,128)(2,1)}, u32[]{:S(2)}, u32[]{:S(2)}) async-start(bf16[160,32,128]{2,1,0:T(8,128)(2,1)} %jacobian.1), calls=%async_computation | async-start | bytes 2621440 | tf_op jit(solution)/shard_map/all_to_all | solution.py:241
  12.0 0.0 copy-done.9
  12.0 0.0 copy-start.10
  12.0 0.0 copy-start.7
  12.0 0.0 copy-start.1
  12.0 0.1 reshape.17.pick
  12.1 0.0 copy-done
  12.1 1.7 %pick.1 = (bf16[40,8,256]{2,1,0:T(8,128)(2,1)}, bf16[40,8,256]{2,1,0:T(8,128)(2,1)}, bf16[40,8,256]{2,1,0:T(8,128)(2,1)S(1)}, bf16[40,8,256]{2,1,0:T(8,128)(2,1)}, bf16[40,8,256]{2,1,0:T(8,128)(2,1)}) custom-call(s32[200]{0:T(256)S(1)} %reshape.17.pick, bf16[384,8,256]{2,1,0:T(8,128)(2,1)S(1)} %copy-done), custom_call_target="tpu_custom_call" | custom-call | bytes 1572864 | tf_op jit(solution)/shard_map/pick/pallas_call | solution.py:278
  13.9 7.5 %collective-permute-start = (bf16[40,8,256]{2,1,0:T(8,128)(2,1)}, bf16[40,8,256]{2,1,0:T(8,128)(2,1)S(1)}, u32[]{:S(2)}, u32[]{:S(2)}) collective-permute-start(bf16[40,8,256]{2,1,0:T(8,128)(2,1)} %get-tuple-element.14), channel_id=1, source_target_pairs={{0,480},{16,496},{32,0},{48,16},{64,32},{80,48},{96,64},{112,80},{... | collective-permute-start | bytes 491528 | tf_op jit(solution)/shard_map/ppermute | solution.py:237
  21.4 2.8 %collective-permute-start.1 = (bf16[40,8,256]{2,1,0:T(8,128)(2,1)}, bf16[40,8,256]{2,1,0:T(8,128)(2,1)}, u32[]{:S(2)}, u32[]{:S(2)}) collective-permute-start(bf16[40,8,256]{2,1,0:T(8,128)(2,1)} %get-tuple-element.15), channel_id=1, source_target_pairs={{0,496},{16,0},{32,16},{48,32},{64,48},{80,64},{96,80},{112,96},{1... | collective-permute-start | bytes 491528 | tf_op jit(solution)/shard_map/ppermute | solution.py:237
  24.2 2.5 %collective-permute-start.2 = (bf16[40,8,256]{2,1,0:T(8,128)(2,1)}, bf16[40,8,256]{2,1,0:T(8,128)(2,1)}, u32[]{:S(2)}, u32[]{:S(2)}) collective-permute-start(bf16[40,8,256]{2,1,0:T(8,128)(2,1)} %get-tuple-element.17), channel_id=1, source_target_pairs={{0,16},{16,32},{32,48},{48,64},{64,80},{80,96},{96,112},{112,128},... | collective-permute-start | bytes 491528 | tf_op jit(solution)/shard_map/ppermute | solution.py:237
  26.7 2.6 %collective-permute-start.3 = (bf16[40,8,256]{2,1,0:T(8,128)(2,1)}, bf16[40,8,256]{2,1,0:T(8,128)(2,1)}, u32[]{:S(2)}, u32[]{:S(2)}) collective-permute-start(bf16[40,8,256]{2,1,0:T(8,128)(2,1)} %get-tuple-element.18), channel_id=1, source_target_pairs={{0,32},{16,48},{32,64},{48,80},{64,96},{80,112},{96,128},{112,144}... | collective-permute-start | bytes 491528 | tf_op jit(solution)/shard_map/ppermute | solution.py:237
  29.3 0.0 copy-done.10
  29.3 0.6 broadcast_divide_fusion
  30.5 0.7 div.15.inverses
  31.2 0.0 copy-done.7
  31.2 0.1 copy.13.innovation
  31.3 1.0 copy.15.vectors
  32.3 0.0 copy-start.6
  32.3 0.1 pad_add_fusion.place
  32.4 0.0 copy-done.1
  32.4 0.0 copy-start.3
  32.4 0.7 copy-done.3
  33.1 0.0 copy-start.4
  33.1 1.7 weights.1.slabs
  34.7 0.0 collective-permute-done.a0
  34.7 0.0 copy-done.4
  34.8 0.0 collective-permute-done.1.a1
  34.8 0.0 collective-permute-done.2.a3
  34.8 3.0 %collective-permute-done.3.a4 = bf16[40,8,256]{2,1,0:T(8,128)(2,1)} collective-permute-done((bf16[40,8,256]{2,1,0:T(8,128)(2,1)}, bf16[40,8,256]{2,1,0:T(8,128)(2,1)}, u32[]{:S(2)}, u32[]{:S(2)}) %collective-permute-start.3) | collective-permute-done | bytes 163872 | tf_op jit(solution)/shard_map/ppermute | solution.py:237
  37.7 0.0 copy-done.6
  37.7 0.0 copy-start.8
  37.7 0.0 copy-start.5
  37.7 2.2 %slots.1 = bf16[176,8,256]{2,1,0:T(8,128)(2,1)} custom-call(s32[160]{0:T(256)S(1)} %copy-done.6, bf16[40,8,256]{2,1,0:T(8,128)(2,1)S(1)} %collective-permute-done.a0, bf16[40,8,256]{2,1,0:T(8,128)(2,1)} %collective-permute-done.1.a1, bf16[40,8,256]{2,1,0:T(8,128)(2,1)S(1)} %get-tuple-element.16.a2, bf16[40,8,256]{2,1,0:T(8,128)(2,1)} %collective-permute-done.2.a3, ...), custom_call_target="tpu_custom_call" | custom-call | bytes 1310720 | tf_op jit(solution)/shard_map/slots/pallas_call | solution.py:306
  40.0 5.3 %all-to-all-done.jacobian = bf16[160,32,128]{2,1,0:T(8,128)(2,1)} async-done(((bf16[160,32,128]{2,1,0:T(8,128)(2,1)}), bf16[160,32,128]{2,1,0:T(8,128)(2,1)}, u32[]{:S(2)}, u32[]{:S(2)}) %all-to-all-start) | async-done | bytes 1310752 | tf_op jit(solution)/shard_map/all_to_all | solution.py:241
  45.3 4.2 %all-to-all-start.1 = ((bf16[176,8,256]{2,1,0:T(8,128)(2,1)}), bf16[176,8,256]{2,1,0:T(8,128)(2,1)}, u32[]{:S(2)}, u32[]{:S(2)}) async-start(bf16[176,8,256]{2,1,0:T(8,128)(2,1)} %slots.1), calls=%async_computation.1 | async-start | bytes 1441792 | tf_op jit(solution)/shard_map/all_to_all | solution.py:241
  49.4 0.0 copy-done.8
  49.5 0.0 copy-done.5
  49.5 3.1 %turn.1.turned = bf16[10,512,128]{2,1,0:T(8,128)(2,1)S(1)} custom-call(s32[2]{0:T(128)S(1)} %copy-done.5, f32[512,32]{1,0:T(8,128)S(1)} %copy.15.vectors, f32[2,256]{1,0:T(2,128)S(1)} %div.12.scales, bf16[160,32,128]{2,1,0:T(8,128)(2,1)} %all-to-all-done.jacobian), custom_call_target="tpu_custom_call" | custom-call | flops 671088640 | bytes 2621440 | tf_op jit(solution)/shard_map/turn/pallas_call | solution.py:319
  52.6 18.0 %all-to-all-done.1.arrived = bf16[176,8,256]{2,1,0:T(8,128)(2,1)} async-done(((bf16[176,8,256]{2,1,0:T(8,128)(2,1)}), bf16[176,8,256]{2,1,0:T(8,128)(2,1)}, u32[]{:S(2)}, u32[]{:S(2)}) %all-to-all-start.1) | async-done | bytes 720928 | tf_op jit(solution)/shard_map/all_to_all | solution.py:241
  70.6 3.3 %terms.1 = (f32[32,8,128]{2,1,0:T(8,128)S(1)}, f32[32,8,128]{2,1,0:T(8,128)S(1)}) custom-call(s32[2]{0:T(128)S(1)} %copy-done.5, bf16[10,512,128]{2,1,0:T(8,128)(2,1)S(1)} %turn.1.turned, bf16[176,8,256]{2,1,0:T(8,128)(2,1)} %all-to-all-done.1.arrived), custom_call_target="tpu_custom_call" | custom-call | flops 1006632960 | bytes 1310720 | tf_op jit(solution)/shard_map/terms/pallas_call | solution.py:329
  73.9 0.0 copy-start.2
  73.9 2.1 %collective-permute-start.4 = (f32[32,8,128]{2,1,0:T(8,128)S(1)}, f32[32,8,128]{2,1,0:T(8,128)S(1)}, u32[]{:S(2)}, u32[]{:S(2)}) collective-permute-start(f32[32,8,128]{2,1,0:T(8,128)S(1)} %get-tuple-element.22), channel_id=1, source_target_pairs={{0,1},{1,0},{2,3},{3,2},{4,5},{5,4},{6,7},{7,6},{8,9},{9,8},{10,11... | collective-permute-start | bytes 393224 | tf_op jit(solution)/shard_map/ppermute | solution.py:245
  76.0 1.3 collective-permute-done.4
  77.3 14.3 %all_to_all.25 = f32[32,8,128]{2,1,0:T(8,128)S(1)} all-to-all(f32[32,8,128]{2,1,0:T(8,128)S(1)} %add.7), channel_id=1, replica_groups=mesh['y'=8,'x'=4,'z'=8,'c'=2] {'x','z'}, dimensions={0} | all-to-all | bytes 262144 | tf_op jit(solution)/shard_map/all_to_all | solution.py:241
  91.6 13.5 %all_to_all.26 = f32[8,8,128]{2,1,0:T(8,128)S(1)} all-to-all(f32[8,8,128]{2,1,0:T(8,128)S(1)} %broadcast_in_dim.7), channel_id=1, replica_groups=mesh['y'=8,'x'=4,'z'=8,'c'=2] {'y'}, dimensions={0} | all-to-all | bytes 65536 | tf_op jit(solution)/shard_map/all_to_all | solution.py:241
  105.1 13.3 %all_to_all.27.mine = f32[32,8,128]{2,1,0:T(8,128)S(1)} all-to-all(f32[32,8,128]{2,1,0:T(8,128)S(1)} %broadcast_in_dim.8), channel_id=1, replica_groups=mesh['y'=8,'x'=4,'z'=8,'c'=2] {'x','z'}, dimensions={0} | all-to-all | bytes 262144 | tf_op jit(solution)/shard_map/all_to_all | solution.py:241
  118.4 6.0 %collective-permute-start.5 = (f32[32,8,128]{2,1,0:T(8,128)S(1)}, f32[32,8,128]{2,1,0:T(8,128)S(1)}, u32[]{:S(2)}, u32[]{:S(2)}) collective-permute-start(f32[32,8,128]{2,1,0:T(8,128)S(1)} %all_to_all.27.mine), channel_id=1, source_target_pairs={{0,1},{1,0},{2,3},{3,2},{4,5},{5,4},{6,7},{7,6},{8,9},{9,8},{10,11... | collective-permute-start | bytes 393224 | tf_op jit(solution)/shard_map/ppermute | solution.py:245
  124.5 1.0 collective-permute-done.5.other
  125.4 0.0 copy-done.2
  125.4 43.7 %solve.1 = bf16[3072,256]{1,0:T(8,128)(2,1)} custom-call(s32[2]{0:T(128)S(1)} %copy-done.5, f32[32,8,128]{2,1,0:T(8,128)S(1)} %all_to_all.27.mine, f32[32,8,128]{2,1,0:T(8,128)S(1)} %collective-permute-done.5.other, f32[256,256]{1,0:T(8,128)S(1)} %copy-done.2, bf16[3072,256]{1,0:T(8,128)(2,1)S(1)} %bitcast.3), custom_call_target="tpu_custom_call" | custom-call | tf_op jit(solution)/shard_map/solve/pallas_call | solution.py:343
  (7 shorter events, 0.1 us)
Async XLA Ops:
  0.0 12.0 %copy-start.9 = (s32[1,5,40]{2,0,1:T(1,128)S(1)}, s32[1,5,40]{2,0,1:T(1,128)}, u32[]{:S(2)}) copy-start(s32[1,5,40]{2,0,1:T(1,128)} %param.15) | copy-start | bytes 2404
  0.0 12.1 %copy-start = (bf16[384,8,256]{2,1,0:T(8,128)(2,1)S(1)}, bf16[384,8,256]{2,1,0:T(8,128)(2,1)}, u32[]{:S(2)}) copy-start(bf16[384,8,256]{2,1,0:T(8,128)(2,1)} %ensemble.1) | copy-start | bytes 4718596
  0.0 45.3 %all-to-all-start = ((bf16[160,32,128]{2,1,0:T(8,128)(2,1)}), bf16[160,32,128]{2,1,0:T(8,128)(2,1)}, u32[]{:S(2)}, u32[]{:S(2)}) async-start(bf16[160,32,128]{2,1,0:T(8,128)(2,1)} %jacobian.1), calls=%async_computation | async-start | bytes 2621440 | tf_op jit(solution)/shard_map/all_to_all | solution.py:241
  12.0 17.3 %copy-start.10 = (f32[512]{0:T(512)S(1)}, f32[512]{0:T(512)}, u32[]{:S(2)}) copy-start(f32[512]{0:T(512)} %param.13) | copy-start | bytes 6148
  12.0 19.2 %copy-start.7 = (f32[160,32]{0,1:T(8,128)S(1)}, f32[160,32]{0,1:T(8,128)}, u32[]{:S(2)}) copy-start(f32[160,32]{0,1:T(8,128)} %param.11) | copy-start | bytes 61444
  12.0 20.4 %copy-start.1 = (bf16[160,32,128]{2,1,0:T(8,128)(2,1)S(1)}, bf16[160,32,128]{2,1,0:T(8,128)(2,1)}, u32[]{:S(2)}) copy-start(bf16[160,32,128]{2,1,0:T(8,128)(2,1)} %jacobian.1) | copy-start | bytes 3932164
  13.9 20.9 %collective-permute-start = (bf16[40,8,256]{2,1,0:T(8,128)(2,1)}, bf16[40,8,256]{2,1,0:T(8,128)(2,1)S(1)}, u32[]{:S(2)}, u32[]{:S(2)}) collective-permute-start(bf16[40,8,256]{2,1,0:T(8,128)(2,1)} %get-tuple-element.14), channel_id=1, source_target_pairs={{0,480},{16,496},{32,0},{48,16},{64,32},{80,48},{96,64},{112,80},{... | collective-permute-start | bytes 491528 | tf_op jit(solution)/shard_map/ppermute | solution.py:237
  21.4 13.3 %collective-permute-start.1 = (bf16[40,8,256]{2,1,0:T(8,128)(2,1)}, bf16[40,8,256]{2,1,0:T(8,128)(2,1)}, u32[]{:S(2)}, u32[]{:S(2)}) collective-permute-start(bf16[40,8,256]{2,1,0:T(8,128)(2,1)} %get-tuple-element.15), channel_id=1, source_target_pairs={{0,496},{16,0},{32,16},{48,32},{64,48},{80,64},{96,80},{112,96},{1... | collective-permute-start | bytes 491528 | tf_op jit(solution)/shard_map/ppermute | solution.py:237
  24.2 10.6 %collective-permute-start.2 = (bf16[40,8,256]{2,1,0:T(8,128)(2,1)}, bf16[40,8,256]{2,1,0:T(8,128)(2,1)}, u32[]{:S(2)}, u32[]{:S(2)}) collective-permute-start(bf16[40,8,256]{2,1,0:T(8,128)(2,1)} %get-tuple-element.17), channel_id=1, source_target_pairs={{0,16},{16,32},{32,48},{48,64},{64,80},{80,96},{96,112},{112,128},... | collective-permute-start | bytes 491528 | tf_op jit(solution)/shard_map/ppermute | solution.py:237
  26.7 11.0 %collective-permute-start.3 = (bf16[40,8,256]{2,1,0:T(8,128)(2,1)}, bf16[40,8,256]{2,1,0:T(8,128)(2,1)}, u32[]{:S(2)}, u32[]{:S(2)}) collective-permute-start(bf16[40,8,256]{2,1,0:T(8,128)(2,1)} %get-tuple-element.18), channel_id=1, source_target_pairs={{0,32},{16,48},{32,64},{48,80},{64,96},{80,112},{96,128},{112,144}... | collective-permute-start | bytes 491528 | tf_op jit(solution)/shard_map/ppermute | solution.py:237
  32.3 5.5 %copy-start.6 = (s32[160]{0:T(256)S(1)}, s32[160]{0:T(256)}, u32[]{:S(2)}) copy-start(s32[160]{0:T(256)} %slot.1) | copy-start | bytes 1924
  32.4 0.7 copy-start.3
  33.1 1.7 copy-start.4
  37.7 11.7 %copy-start.8 = (f32[512]{0:T(512)S(1)}, f32[512]{0:T(512)}, u32[]{:S(2)}) copy-start(f32[512]{0:T(512)} %get-tuple-element.24) | copy-start | bytes 6148
  37.7 11.7 %copy-start.5 = (s32[2]{0:T(128)S(1)}, s32[2]{0:T(128)}, u32[]{:S(2)}) copy-start(s32[2]{0:T(128)} %copy-done.4) | copy-start | bytes 28
  45.3 25.3 %all-to-all-start.1 = ((bf16[176,8,256]{2,1,0:T(8,128)(2,1)}), bf16[176,8,256]{2,1,0:T(8,128)(2,1)}, u32[]{:S(2)}, u32[]{:S(2)}) async-start(bf16[176,8,256]{2,1,0:T(8,128)(2,1)} %slots.1), calls=%async_computation.1 | async-start | bytes 1441792 | tf_op jit(solution)/shard_map/all_to_all | solution.py:241
  73.9 51.5 %copy-start.2 = (f32[256,256]{1,0:T(8,128)S(1)}, f32[256,256]{1,0:T(8,128)}, u32[]{:S(2)}) copy-start(f32[256,256]{1,0:T(8,128)} %basis.1) | copy-start | bytes 786436
  73.9 3.4 %collective-permute-start.4 = (f32[32,8,128]{2,1,0:T(8,128)S(1)}, f32[32,8,128]{2,1,0:T(8,128)S(1)}, u32[]{:S(2)}, u32[]{:S(2)}) collective-permute-start(f32[32,8,128]{2,1,0:T(8,128)S(1)} %get-tuple-element.22), channel_id=1, source_target_pairs={{0,1},{1,0},{2,3},{3,2},{4,5},{5,4},{6,7},{7,6},{8,9},{9,8},{10,11... | collective-permute-start | bytes 393224 | tf_op jit(solution)/shard_map/ppermute | solution.py:245
  118.4 7.0 %collective-permute-start.5 = (f32[32,8,128]{2,1,0:T(8,128)S(1)}, f32[32,8,128]{2,1,0:T(8,128)S(1)}, u32[]{:S(2)}, u32[]{:S(2)}) collective-permute-start(f32[32,8,128]{2,1,0:T(8,128)S(1)} %all_to_all.27.mine), channel_id=1, source_target_pairs={{0,1},{1,0},{2,3},{3,2},{4,5},{5,4},{6,7},{7,6},{8,9},{9,8},{10,11... | collective-permute-start | bytes 393224 | tf_op jit(solution)/shard_map/ppermute | solution.py:245

commit v5 on v3

--- a/solution.py
+++ b/solution.py
@@ -16,7 +16,7 @@
 BF16 = jnp.bfloat16
 VM = pl.BlockSpec(memory_space=pltpu.VMEM)
 SM = pl.BlockSpec(memory_space=pltpu.SMEM)
-PARAMS = pltpu.CompilerParams(vmem_limit_bytes=48 * 2**20)
+PARAMS = pltpu.CompilerParams(vmem_limit_bytes=20 * 2**20)
 
 
 def cost(flops, size):
@@ -55,39 +55,36 @@
         lax.fori_loop(0, capacity, one, 0, unroll=8)
 
 
-def weights_kernel(place, innovation, vectors, inverses, jacobian, slabs, sums):
+def misfit_kernel(place, innovation, vectors, scales, out):
     group = place[0]
     width = vectors.shape[1]
     start = pl.multiple_of(group * width, width)
-    basis = vectors[pl.ds(start, width), :]
-    scaled = basis * inverses[pl.ds(group, 1), :]
-    tiled = nt(scaled, jnp.concatenate([basis] * 8, axis=0), HI)
-    weights = nn(innovation[...], tiled, HI)
-    mine = iota2(8, 8 * width, 1) // width == iota2(8, 8 * width, 0)
-    rows = innovation.shape[0]
-    for k in range(rows // 8):
-        high, low = split(jnp.where(mine, weights[8 * k : 8 * k + 8], 0.0))
-        block = jacobian[8 * k : 8 * k + 8].reshape(8 * width, 128)
-        sums[8 * k : 8 * k + 8, :] = nn(high, block) + nn(low, block)
-    share = rows // slabs.shape[0]
-    zero = jnp.zeros((8 - (share - 8), 128), F32)
-    for i in range(slabs.shape[0]):
-        left = sums[share * i : share * i + 8, :]
-        right = jnp.concatenate([sums[share * i + 8 : share * i + share, :], zero], axis=0)
-        slabs[i] = jnp.concatenate([left, right], axis=1).astype(BF16)
-
-
-def slot_kernel(slot, a0, a1, a2, a3, a4, slabs, out, held):
+    basis = vectors[pl.ds(start, width), :] * scales[pl.ds(group, 1), :]
+    misfit = nn(innovation[...], basis, HI)
+    peers = out.shape[0]
+    share = misfit.shape[0] // peers
+    rest = jnp.zeros((16 - share, width), F32)
+    blank = jnp.zeros((8, 128 - 2 * width), F32)
+    for i in range(peers):
+        left = misfit[share * i : share * i + 8, :]
+        right = jnp.concatenate([misfit[share * i + 8 : share * (i + 1), :], rest], axis=0)
+        out[i] = jnp.concatenate([left, right, blank], axis=1).astype(BF16)
+
+
+def slot_kernel(slot, a0, a1, a2, a3, a4, misfits, out, held):
     capacity = a0.shape[0]
     for o, part in enumerate((a0, a1, a2, a3, a4)):
         held[o * capacity : (o + 1) * capacity] = part[...]
-    peers = slabs.shape[0]
-    share = out.shape[0] // peers - 1
+    peers = misfits.shape[0]
+    step = out.shape[0] // peers
+    share = step // 2
 
     def one(i, carry):
         for f in range(share):
-            out[i * (share + 1) + f] = held[slot[i * share + f]]
-        out[i * (share + 1) + share] = slabs[i]
+            column = held[slot[i * share + f]]
+            out[i * step + 2 * f] = column[:, 0:128]
+            out[i * step + 2 * f + 1] = column[:, 128:256]
+        out[i * step + 2 * share] = misfits[i]
         return carry
 
     lax.fori_loop(0, peers, one, 0)
@@ -116,27 +113,35 @@
             out[f, h * half : (h + 1) * half, :] = turned.astype(BF16)
 
 
-def terms_kernel(place, turned, arrived, out):
-    share = turned.shape[0]
-    peers = arrived.shape[0] // (share + 1)
-    first = place[0] * share
-    count = place[1]
-    b = arrived[share].astype(F32)
-    for source in range(1, peers):
-        b = b + arrived[source * (share + 1) + share].astype(F32)
-    gram = jnp.zeros((MEM, MEM), F32)
-    pull = jnp.zeros((8, MEM), F32)
-    for f in range(share):
-        live = jnp.where(first + f < count, 1.0, 0.0).astype(F32)
-        column = jnp.concatenate(
-            [arrived[s * (share + 1) + f] for s in range(peers)], axis=0
-        )
-        flipped = column.astype(F32).T.astype(BF16)
-        whitened = nt(flipped, turned[f]).astype(BF16)
-        gram = gram + nt(whitened, whitened)
-        mine = iota2(8, 128, 0) == f % 8
-        high, low = split(jnp.where(mine, b[:, 128 * (f // 8) : 128 * (f // 8) + 128] * live, 0.0))
-        pull = pull + (nn(high, column) + nn(low, column))
+def terms_kernel(turned, arrived, out):
+    share, channels = turned.shape[:2]
+    step = 2 * share + 1
+    peers = arrived.shape[0] // step
+    width = channels // peers
+    tiles = [arrived[s * step + 2 * share].astype(F32) for s in range(peers)]
+    misfit = [
+        jnp.concatenate([t[:, width * k : width * (k + 1)] for t in tiles], axis=1)
+        for k in range(2)
+    ]
+    blank = jnp.zeros((8, channels), F32)
+    gram = jnp.zeros((MEM + 16, MEM), F32)
+    batch = 5
+    for begin in range(0, share, batch):
+        lefts, rights = [], []
+        for f in range(begin, begin + batch):
+            flipped = []
+            for h in range(2):
+                column = jnp.concatenate(
+                    [arrived[s * step + 2 * f + h] for s in range(peers)], axis=0
+                )
+                flipped.append(column.astype(F32).T.astype(BF16))
+            whitened = nt(jnp.concatenate(flipped, axis=0), turned[f]).astype(BF16)
+            row = jnp.where(iota2(8, channels, 0) == f % 8, misfit[f // 8], 0.0)
+            rows = jnp.concatenate([row, blank], axis=0).astype(BF16)
+            rights.append(whitened)
+            lefts.append(jnp.concatenate([whitened, rows], axis=0))
+        gram = gram + nt(jnp.concatenate(lefts, axis=1), jnp.concatenate(rights, axis=1))
+    pull = gram[MEM : MEM + 16, :]
     out[0:16] = gram[0:128, 0:128].reshape(16, 8, 128)
     out[16:32] = gram[128:256, 0:128].reshape(16, 8, 128)
     out[32:48] = gram[128:256, 128:256].reshape(16, 8, 128)
@@ -151,6 +156,20 @@
 def lower_half(x):
     i, j = iota2(MEM, MEM, 0), iota2(MEM, MEM, 1)
     return jnp.where(i > j, x, jnp.where(i == j, 0.5 * x, 0.0))
+
+
+def nn3(a, b):
+    (ah, al), (bh, bl) = split(a), split(b)
+    return nn(ah, bh) + (nn(ah, bl) + nn(al, bh))
+
+
+def nt3(a, b):
+    (ah, al), (bh, bl) = split(a), split(b)
+    return nt(ah, bh) + (nt(ah, bl) + nt(al, bh))
+
+
+def corrected(x, residual):
+    return x - nn(lower_half(residual).astype(BF16), x.astype(BF16))
 
 
 def solve_kernel(summed, basis, ensemble, out, system, inverse, rows, held, sems):
@@ -165,8 +184,9 @@
     across = lax.rsqrt(jnp.sum(a * eye, axis=0, keepdims=True))
     down = lax.rsqrt(jnp.sum(a * eye, axis=1, keepdims=True))
     x = across * (eye - lower_half(a * across * down - eye))
-    residual = nt(nn(x, a), x) - eye
-    inverse[...] = x - nn(lower_half(residual), x)
+    rough = x.astype(BF16)
+    x = corrected(x, nt(nn(rough, a.astype(BF16)).astype(BF16), rough) - eye)
+    inverse[...] = corrected(x, nt3(nn3(x, a), x) - eye)
 
     def go_on(state):
         step, size = state
@@ -176,7 +196,7 @@
         step, _ = state
         x = inverse[...]
         residual = nt(nn(x, system[...], HI), x, HI) - eye
-        inverse[...] = x - nn(lower_half(residual), x, HI)
+        inverse[...] = corrected(x, residual)
         return step + 1, jnp.sum(residual * residual)
 
     _, size = lax.while_loop(go_on, refine, (jnp.int32(0), jnp.float32(1.0)))
@@ -203,9 +223,9 @@
     x = inverse[...]
     last = summed[48]
     pull = jnp.concatenate([last[0:1, :], last[1:2, :]], axis=1)
-    halfway = nt(x, jnp.broadcast_to(pull, (MEM, MEM)), HI)
+    halfway = jnp.sum(x * pull, axis=1, keepdims=True)
     target = (MEM - 1.0) ** 0.5 * basis[...] + halfway
-    transform = nn(x.T, target, HI).astype(BF16)
+    transform = nn3(x.T, target).astype(BF16)
     copies = []
     for i in range(held.shape[0]):
         size = held.shape[1]
@@ -272,27 +292,27 @@
     place = jnp.concatenate(
         [lax.axis_index(CHAN).astype(jnp.int32)[None], footprint_count.astype(jnp.int32)]
     )
-    slabs = pl.pallas_call(
-        weights_kernel,
-        out_shape=jax.ShapeDtypeStruct((peers, *slab), BF16),
-        in_specs=[SM, VM, VM, VM, VM],
+    scales = 1.0 / jnp.sqrt(error_values)
+    misfits = pl.pallas_call(
+        misfit_kernel,
+        out_shape=jax.ShapeDtypeStruct((peers, 8, 128), BF16),
+        in_specs=[SM, VM, VM, VM],
         out_specs=VM,
-        scratch_shapes=[pltpu.VMEM((foot_rows, 128), F32)],
-        compiler_params=PARAMS,
-        cost_estimate=cost(2 * foot_rows * 256 * 128, 2 * jacobian.size),
-        name="weights",
-    )(place, innovation, error_vectors, 1.0 / error_values.reshape(peers, width), jacobian)
+        compiler_params=PARAMS,
+        cost_estimate=cost(2 * foot_rows * width * width, 4 * error_vectors.size),
+        name="misfit",
+    )(place, innovation, error_vectors, scales.reshape(peers, width))
 
     payload = pl.pallas_call(
         slot_kernel,
-        out_shape=jax.ShapeDtypeStruct((foot_rows + peers, *slab), BF16),
+        out_shape=jax.ShapeDtypeStruct((2 * foot_rows + peers, 8, 128), BF16),
         in_specs=[SM] + [VM] * (window + 1),
         out_specs=VM,
         scratch_shapes=[pltpu.VMEM((window * capacity, *slab), BF16)],
         compiler_params=PARAMS,
         cost_estimate=cost(0, 4 * foot_rows * levels * members),
         name="slots",
-    )(footprint_slot, *parts, slabs)
+    )(footprint_slot, *parts, misfits)
     payload, sensitivity = lax.optimization_barrier((payload, sensitivity))
     arrived = swap(payload, CHAN)
 
@@ -304,17 +324,17 @@
         compiler_params=PARAMS,
         cost_estimate=cost(4 * 512 * share * 256 * 128, 4 * jacobian.size),
         name="turn",
-    )(place, error_vectors, 1.0 / jnp.sqrt(error_values).reshape(2, members), sensitivity)
+    )(place, error_vectors, scales.reshape(2, members), sensitivity)
 
     tiles = pl.pallas_call(
         terms_kernel,
         out_shape=jax.ShapeDtypeStruct((64, 8, 128), F32),
-        in_specs=[SM, VM, VM],
+        in_specs=[VM, VM],
         out_specs=VM,
         compiler_params=PARAMS,
         cost_estimate=cost(2 * 512 * share * 256 * 384, 2 * jacobian.size),
         name="terms",
-    )(place, turned, arrived)
+    )(turned, arrived)
 
     summed = summed_everywhere(tiles)
 

time: 169 us -> 169 us (level)
  local copies, waits for them, and re-layouts: 2.6 us -> 7.06 us
  Pallas kernels: 55.8 us -> 52.6 us
    unnamed x24 -> x30, local copies, waits for them, and re-layouts: 1.81 us -> 6.26 us
  transfers between devices with their start and end apart: 6 -> 6, of which waited for: 3 -> 4; matrix products, arithmetic and copies ran while one was open for 1% -> 1% of each run, Pallas kernels for 5% -> 4%
where the time goes in v5:
time: 169 us; the launch traced here: 168 us
  Pallas kernels  52.6 us (31%)
  blocking collectives  50 us (30%)
  starting transfers between devices  32 us (19%)
  waiting for transfers between devices  25.1 us (15%)
  local copies, waits for them, and re-layouts  7.06 us (4%)
    all_to_all x3, blocking collectives, swap(): return lax.all_to_all(x, axis, 0, 0, tiled=True)  50 us
    pallas_call x1, Pallas kernels, local(): pl.pallas_call(solve_kernel, out_shape=jax.ShapeDtypeStruct(flat_rows.sha...  43.6 us
    all_to_all x2, waiting for transfers between devices, swap(): return lax.all_to_all(x, axis, 0, 0, tiled=True)  21.7 us
    all_to_all x2, starting transfers between devices, swap(): return lax.all_to_all(x, axis, 0, 0, tiled=True)  16.6 us
    ppermute x4, starting transfers between devices, send_by(): lax.ppermute(value, axis, [(s, (s + steps) % count) for s in range(count)])  15.4 us
    unnamed x30, local copies, waits for them, and re-layouts  6.26 us
    ppermute x4, waiting for transfers between devices, send_by(): lax.ppermute(value, axis, [(s, (s + steps) % count) for s in range(count)])  3.43 us
  transfers between devices with their start and end apart: 6, of which 4 were waited for; matrix products, arithmetic and copies ran while one was open for 1% of the time, Pallas kernels for 4%

profile of v5, /device:TPU:1, one launch (start us, length us, event | category | flops | bytes accessed | tf_op | source)
XLA Modules:
  0.0 168.3 jit_solution(10769763995092028599)
XLA Ops:
  0.0 0.0 copy-start.12
  0.0 0.0 copy-start
  0.0 12.0 %all-to-all-start = ((bf16[160,32,128]{2,1,0:T(8,128)(2,1)}), bf16[160,32,128]{2,1,0:T(8,128)(2,1)S(1)}, u32[]{:S(2)}, u32[]{:S(2)}) async-start(bf16[160,32,128]{2,1,0:T(8,128)(2,1)} %param.10), calls=%async_computation | async-start | bytes 2621440 | tf_op jit(solution)/shard_map/all_to_all | solution.py:247
  12.0 0.0 copy-done.12
  12.0 0.0 copy-start.13
  12.0 0.0 copy-start.9
  12.0 0.1 reshape.18.pick
  12.1 0.0 copy-done
  12.1 1.7 %pick.1 = (bf16[40,8,256]{2,1,0:T(8,128)(2,1)}, bf16[40,8,256]{2,1,0:T(8,128)(2,1)}, bf16[40,8,256]{2,1,0:T(8,128)(2,1)S(1)}, bf16[40,8,256]{2,1,0:T(8,128)(2,1)}, bf16[40,8,256]{2,1,0:T(8,128)(2,1)}) custom-call(s32[200]{0:T(256)S(1)} %reshape.18.pick, bf16[384,8,256]{2,1,0:T(8,128)(2,1)S(1)} %copy-done), custom_call_target="tpu_custom_call" | custom-call | bytes 1572864 | tf_op jit(solution)/shard_map/pick/pallas_call | solution.py:278
  13.8 7.6 %collective-permute-start = (bf16[40,8,256]{2,1,0:T(8,128)(2,1)}, bf16[40,8,256]{2,1,0:T(8,128)(2,1)S(1)}, u32[]{:S(2)}, u32[]{:S(2)}) collective-permute-start(bf16[40,8,256]{2,1,0:T(8,128)(2,1)} %get-tuple-element.12), channel_id=1, source_target_pairs={{0,480},{16,496},{32,0},{48,16},{64,32},{80,48},{96,64},{112,80},{... | collective-permute-start | bytes 491528 | tf_op jit(solution)/shard_map/ppermute | solution.py:243
  21.4 2.8 %collective-permute-start.1 = (bf16[40,8,256]{2,1,0:T(8,128)(2,1)}, bf16[40,8,256]{2,1,0:T(8,128)(2,1)}, u32[]{:S(2)}, u32[]{:S(2)}) collective-permute-start(bf16[40,8,256]{2,1,0:T(8,128)(2,1)} %get-tuple-element.13), channel_id=1, source_target_pairs={{0,496},{16,0},{32,16},{48,32},{64,48},{80,64},{96,80},{112,96},{1... | collective-permute-start | bytes 491528 | tf_op jit(solution)/shard_map/ppermute | solution.py:243
  24.2 2.5 %collective-permute-start.2 = (bf16[40,8,256]{2,1,0:T(8,128)(2,1)}, bf16[40,8,256]{2,1,0:T(8,128)(2,1)}, u32[]{:S(2)}, u32[]{:S(2)}) collective-permute-start(bf16[40,8,256]{2,1,0:T(8,128)(2,1)} %get-tuple-element.15), channel_id=1, source_target_pairs={{0,16},{16,32},{32,48},{48,64},{64,80},{80,96},{96,112},{112,128},... | collective-permute-start | bytes 491528 | tf_op jit(solution)/shard_map/ppermute | solution.py:243
  26.7 2.6 %collective-permute-start.3 = (bf16[40,8,256]{2,1,0:T(8,128)(2,1)}, bf16[40,8,256]{2,1,0:T(8,128)(2,1)}, u32[]{:S(2)}, u32[]{:S(2)}) collective-permute-start(bf16[40,8,256]{2,1,0:T(8,128)(2,1)} %get-tuple-element.16), channel_id=1, source_target_pairs={{0,32},{16,48},{32,64},{48,80},{64,96},{80,112},{96,128},{112,144}... | collective-permute-start | bytes 491528 | tf_op jit(solution)/shard_map/ppermute | solution.py:243
  29.9 0.0 copy-done.13
  30.0 0.0 copy-start.10
  30.0 0.7 reshape.19.scales
  30.6 0.0 copy-done.9
  30.6 0.1 copy.13.innovation
  30.7 0.0 copy-done.10
  30.7 0.6 pad_add_fusion.place
  31.3 1.0 copy.15.vectors
  32.3 0.0 copy-start.5
  32.3 0.7 copy-done.5
  33.0 0.0 copy-start.6
  33.0 0.6 copy-done.6
  33.5 0.8 misfit.1.misfits
  34.4 0.0 collective-permute-done.a0
  34.4 0.0 collective-permute-done.1.a1
  34.4 0.4 collective-permute-done.2.a3
  34.8 3.0 %collective-permute-done.3.a4 = bf16[40,8,256]{2,1,0:T(8,128)(2,1)} collective-permute-done((bf16[40,8,256]{2,1,0:T(8,128)(2,1)}, bf16[40,8,256]{2,1,0:T(8,128)(2,1)}, u32[]{:S(2)}, u32[]{:S(2)}) %collective-permute-start.3) | collective-permute-done | bytes 163872 | tf_op jit(solution)/shard_map/ppermute | solution.py:243
  37.8 0.0 copy-start.8
  37.8 0.7 copy-done.8
  38.5 0.0 copy-start.11
  38.5 0.0 copy-start.7
  38.5 1.4 slots.1
  39.9 0.0 copy-start.1
  39.9 0.9 copy-done.1
  40.8 4.4 %all-to-all-done.jacobian = bf16[160,32,128]{2,1,0:T(8,128)(2,1)S(1)} async-done(((bf16[160,32,128]{2,1,0:T(8,128)(2,1)}), bf16[160,32,128]{2,1,0:T(8,128)(2,1)S(1)}, u32[]{:S(2)}, u32[]{:S(2)}) %all-to-all-start) | async-done | bytes 1310752 | tf_op jit(solution)/shard_map/all_to_all | solution.py:247
  45.2 4.6 %all-to-all-start.1 = ((bf16[336,8,128]{2,1,0:T(8,128)(2,1)}), bf16[336,8,128]{2,1,0:T(8,128)(2,1)}, u32[]{:S(2)}, u32[]{:S(2)}) async-start(bf16[336,8,128]{2,1,0:T(8,128)(2,1)} %copy-done.1), calls=%async_computation.1 | async-start | bytes 1376256 | tf_op jit(solution)/shard_map/all_to_all | solution.py:247
  49.8 0.0 copy-done.11
  49.8 0.0 copy-done.7
  49.8 2.3 %turn.1.turned = bf16[10,512,128]{2,1,0:T(8,128)(2,1)S(1)} custom-call(s32[2]{0:T(128)S(1)} %copy-done.7, f32[512,32]{1,0:T(8,128)S(1)} %copy.15.vectors, f32[2,256]{1,0:T(2,128)S(1)} %reshape.17.scales, bf16[160,32,128]{2,1,0:T(8,128)(2,1)S(1)} %all-to-all-done.jacobian), custom_call_target="tpu_custom_call" | custom-call | flops 671088640 | bytes 2621440 | tf_op jit(solution)/shard_map/turn/pallas_call | solution.py:319
  52.2 0.0 copy-start.2
  52.2 1.0 copy-done.2
  53.2 17.3 %all-to-all-done.1.arrived = bf16[336,8,128]{2,1,0:T(8,128)(2,1)} async-done(((bf16[336,8,128]{2,1,0:T(8,128)(2,1)}), bf16[336,8,128]{2,1,0:T(8,128)(2,1)}, u32[]{:S(2)}, u32[]{:S(2)}) %all-to-all-start.1) | async-done | bytes 688160 | tf_op jit(solution)/shard_map/all_to_all | solution.py:247
  70.6 0.0 copy-start.3
  70.6 1.3 copy-done.3
  71.9 2.7 %terms.1 = f32[64,8,128]{2,1,0:T(8,128)S(1)} custom-call(bf16[10,512,128]{2,1,0:T(8,128)(2,1)S(1)} %copy-done.3, bf16[336,8,128]{2,1,0:T(8,128)(2,1)} %all-to-all-done.1.arrived), custom_call_target="tpu_custom_call" | custom-call | flops 1006632960 | bytes 1310720 | tf_op jit(solution)/shard_map/terms/pallas_call | solution.py:329
  74.6 0.0 copy-start.4
  74.6 17.3 %all_to_all.25 = f32[64,8,128]{2,1,0:T(8,128)S(1)} all-to-all(f32[64,8,128]{2,1,0:T(8,128)S(1)} %terms.1), channel_id=1, replica_groups=mesh['y'=8,'x'=4,'z'=8,'c'=2] {'x','z','c'}, dimensions={0} | all-to-all | bytes 524288 | tf_op jit(solution)/shard_map/all_to_all | solution.py:247
  91.9 0.1 reduce_sum.18
  92.0 13.5 %all_to_all.26 = f32[8,8,128]{2,1,0:T(8,128)S(1)} all-to-all(f32[8,8,128]{2,1,0:T(8,128)S(1)} %broadcast_in_dim.7), channel_id=1, replica_groups=mesh['y'=8,'x'=4,'z'=8,'c'=2] {'y'}, dimensions={0} | all-to-all | bytes 65536 | tf_op jit(solution)/shard_map/all_to_all | solution.py:247
  105.5 19.3 %all_to_all.27.summed = f32[64,8,128]{2,1,0:T(8,128)S(1)} all-to-all(f32[64,8,128]{2,1,0:T(8,128)S(1)} %broadcast_in_dim.8), channel_id=1, replica_groups=mesh['y'=8,'x'=4,'z'=8,'c'=2] {'x','z','c'}, dimensions={0} | all-to-all | bytes 524288 | tf_op jit(solution)/shard_map/all_to_all | solution.py:247
  124.7 0.0 copy-done.4
  124.7 43.6 %solve.1 = bf16[3072,256]{1,0:T(8,128)(2,1)} custom-call(f32[64,8,128]{2,1,0:T(8,128)S(1)} %all_to_all.27.summed, f32[256,256]{1,0:T(8,128)S(1)} %copy-done.4, bf16[3072,256]{1,0:T(8,128)(2,1)S(1)} %bitcast.3), custom_call_target="tpu_custom_call" | custom-call | tf_op jit(solution)/shard_map/solve/pallas_call | solution.py:343
  (6 shorter events, 0.1 us)
Async XLA Ops:
  0.0 12.0 %copy-start.12 = (s32[1,5,40]{2,0,1:T(1,128)S(1)}, s32[1,5,40]{2,0,1:T(1,128)}, u32[]{:S(2)}) copy-start(s32[1,5,40]{2,0,1:T(1,128)} %param.15) | copy-start | bytes 2404
  0.0 12.1 %copy-start = (bf16[384,8,256]{2,1,0:T(8,128)(2,1)S(1)}, bf16[384,8,256]{2,1,0:T(8,128)(2,1)}, u32[]{:S(2)}) copy-start(bf16[384,8,256]{2,1,0:T(8,128)(2,1)} %ensemble.1) | copy-start | bytes 4718596
  0.0 45.2 %all-to-all-start = ((bf16[160,32,128]{2,1,0:T(8,128)(2,1)}), bf16[160,32,128]{2,1,0:T(8,128)(2,1)S(1)}, u32[]{:S(2)}, u32[]{:S(2)}) async-start(bf16[160,32,128]{2,1,0:T(8,128)(2,1)} %param.10), calls=%async_computation | async-start | bytes 2621440 | tf_op jit(solution)/shard_map/all_to_all | solution.py:247
  12.0 18.0 %copy-start.13 = (f32[512]{0:T(512)S(1)}, f32[512]{0:T(512)}, u32[]{:S(2)}) copy-start(f32[512]{0:T(512)} %param.13) | copy-start | bytes 6148
  12.0 18.6 %copy-start.9 = (f32[160,32]{0,1:T(8,128)S(1)}, f32[160,32]{0,1:T(8,128)}, u32[]{:S(2)}) copy-start(f32[160,32]{0,1:T(8,128)} %param.11) | copy-start | bytes 61444
  13.8 20.5 %collective-permute-start = (bf16[40,8,256]{2,1,0:T(8,128)(2,1)}, bf16[40,8,256]{2,1,0:T(8,128)(2,1)S(1)}, u32[]{:S(2)}, u32[]{:S(2)}) collective-permute-start(bf16[40,8,256]{2,1,0:T(8,128)(2,1)} %get-tuple-element.12), channel_id=1, source_target_pairs={{0,480},{16,496},{32,0},{48,16},{64,32},{80,48},{96,64},{112,80},{... | collective-permute-start | bytes 491528 | tf_op jit(solution)/shard_map/ppermute | solution.py:243
  21.4 13.0 %collective-permute-start.1 = (bf16[40,8,256]{2,1,0:T(8,128)(2,1)}, bf16[40,8,256]{2,1,0:T(8,128)(2,1)}, u32[]{:S(2)}, u32[]{:S(2)}) collective-permute-start(bf16[40,8,256]{2,1,0:T(8,128)(2,1)} %get-tuple-element.13), channel_id=1, source_target_pairs={{0,496},{16,0},{32,16},{48,32},{64,48},{80,64},{96,80},{112,96},{1... | collective-permute-start | bytes 491528 | tf_op jit(solution)/shard_map/ppermute | solution.py:243
  24.2 10.6 %collective-permute-start.2 = (bf16[40,8,256]{2,1,0:T(8,128)(2,1)}, bf16[40,8,256]{2,1,0:T(8,128)(2,1)}, u32[]{:S(2)}, u32[]{:S(2)}) collective-permute-start(bf16[40,8,256]{2,1,0:T(8,128)(2,1)} %get-tuple-element.15), channel_id=1, source_target_pairs={{0,16},{16,32},{32,48},{48,64},{64,80},{80,96},{96,112},{112,128},... | collective-permute-start | bytes 491528 | tf_op jit(solution)/shard_map/ppermute | solution.py:243
  26.7 11.1 %collective-permute-start.3 = (bf16[40,8,256]{2,1,0:T(8,128)(2,1)}, bf16[40,8,256]{2,1,0:T(8,128)(2,1)}, u32[]{:S(2)}, u32[]{:S(2)}) collective-permute-start(bf16[40,8,256]{2,1,0:T(8,128)(2,1)} %get-tuple-element.16), channel_id=1, source_target_pairs={{0,32},{16,48},{32,64},{48,80},{64,96},{80,112},{96,128},{112,144}... | collective-permute-start | bytes 491528 | tf_op jit(solution)/shard_map/ppermute | solution.py:243
  30.0 0.8 copy-start.10
  32.3 0.7 copy-start.5
  33.0 0.6 copy-start.6
  37.8 0.7 copy-start.8
  38.5 11.3 %copy-start.11 = (f32[512]{0:T(512)S(1)}, f32[512]{0:T(512)}, u32[]{:S(2)}) copy-start(f32[512]{0:T(512)} %copy-done.10) | copy-start | bytes 6148
  38.5 11.3 %copy-start.7 = (s32[2]{0:T(128)S(1)}, s32[2]{0:T(128)}, u32[]{:S(2)}) copy-start(s32[2]{0:T(128)} %pad_add_fusion.place) | copy-start | bytes 28
  39.9 0.9 copy-start.1
  45.2 25.4 %all-to-all-start.1 = ((bf16[336,8,128]{2,1,0:T(8,128)(2,1)}), bf16[336,8,128]{2,1,0:T(8,128)(2,1)}, u32[]{:S(2)}, u32[]{:S(2)}) async-start(bf16[336,8,128]{2,1,0:T(8,128)(2,1)} %copy-done.1), calls=%async_computation.1 | async-start | bytes 1376256 | tf_op jit(solution)/shard_map/all_to_all | solution.py:247
  52.2 1.1 copy-start.2
  70.6 1.3 copy-start.3
  74.6 50.1 %copy-start.4 = (f32[256,256]{1,0:T(8,128)S(1)}, f32[256,256]{1,0:T(8,128)}, u32[]{:S(2)}) copy-start(f32[256,256]{1,0:T(8,128)} %basis.1) | copy-start | bytes 786436

commit v6 on v5

--- a/solution.py
+++ b/solution.py
@@ -16,7 +16,10 @@
 BF16 = jnp.bfloat16
 VM = pl.BlockSpec(memory_space=pltpu.VMEM)
 SM = pl.BlockSpec(memory_space=pltpu.SMEM)
+HB = pl.BlockSpec(memory_space=pltpu.HBM)
+BATCH = 5
 PARAMS = pltpu.CompilerParams(vmem_limit_bytes=20 * 2**20)
+WHOLE = pltpu.CompilerParams(vmem_limit_bytes=57 * 2**20)
 
 
 def cost(flops, size):
@@ -71,26 +74,33 @@
         out[i] = jnp.concatenate([left, right, blank], axis=1).astype(BF16)
 
 
-def slot_kernel(slot, a0, a1, a2, a3, a4, misfits, out, held):
+def slot_kernel(slot, a0, a1, a2, a3, a4, misfits, out, held, built, sems):
     capacity = a0.shape[0]
     for o, part in enumerate((a0, a1, a2, a3, a4)):
         held[o * capacity : (o + 1) * capacity] = part[...]
-    peers = misfits.shape[0]
-    step = out.shape[0] // peers
+    peers, step = out.shape[:2]
     share = step // 2
 
     def one(i, carry):
         for f in range(share):
             column = held[slot[i * share + f]]
-            out[i * step + 2 * f] = column[:, 0:128]
-            out[i * step + 2 * f + 1] = column[:, 128:256]
-        out[i * step + 2 * share] = misfits[i]
+            built[i, 2 * f] = column[:, 0:128]
+            built[i, 2 * f + 1] = column[:, 128:256]
+        built[i, 2 * share] = misfits[i]
         return carry
 
-    lax.fori_loop(0, peers, one, 0)
-
-
-def turn_kernel(place, vectors, scales, jacobian, out):
+    copies = []
+    half = peers // 2
+    for k in range(2):
+        lax.fori_loop(k * half, (k + 1) * half, one, 0)
+        piece = pl.ds(k * half, half)
+        copies.append(pltpu.make_async_copy(built.at[piece], out.at[piece], sems.at[k]))
+        copies[-1].start()
+    for copy in copies:
+        copy.wait()
+
+
+def turn_kernel(place, vectors, scales, jacobian, out, built, sems):
     peers = vectors.shape[0] // vectors.shape[1]
     share = jacobian.shape[0] // peers
     first = place[0] * share
@@ -102,6 +112,7 @@
         block = vectors[h * half : (h + 1) * half, :]
         wide = jnp.where(same, jnp.concatenate([block] * 8, axis=1), 0.0) * scales[h : h + 1, :]
         turns.append(split(wide.T))
+    copies = []
     for f in range(share):
         live = jnp.where(first + f < count, 1.0, 0.0).astype(F32)
         for h in range(2):
@@ -110,37 +121,63 @@
             )
             high, low = turns[h]
             turned = (nn(high, block) + nn(low, block)) * live
-            out[f, h * half : (h + 1) * half, :] = turned.astype(BF16)
-
-
-def terms_kernel(turned, arrived, out):
+            built[f, h * half : (h + 1) * half, :] = turned.astype(BF16)
+        if f % BATCH == BATCH - 1:
+            piece = pl.ds(f + 1 - BATCH, BATCH)
+            copies.append(
+                pltpu.make_async_copy(built.at[piece], out.at[piece], sems.at[f // BATCH])
+            )
+            copies[-1].start()
+    for copy in copies:
+        copy.wait()
+
+
+def terms_kernel(turned_far, arrived_far, out, turned, arrived, sems):
     share, channels = turned.shape[:2]
-    step = 2 * share + 1
-    peers = arrived.shape[0] // step
+    peers = arrived.shape[0]
     width = channels // peers
-    tiles = [arrived[s * step + 2 * share].astype(F32) for s in range(peers)]
+    loads = []
+    for k in range(share // BATCH):
+        first = 2 * BATCH * k
+        count = 2 * BATCH if k < share // BATCH - 1 else 2 * BATCH + 1
+        tiles = pl.ds(first, count)
+        rows = pl.ds(BATCH * k, BATCH)
+        pair = (
+            pltpu.make_async_copy(arrived_far.at[:, tiles], arrived.at[:, tiles], sems.at[2 * k]),
+            pltpu.make_async_copy(turned_far.at[rows], turned.at[rows], sems.at[2 * k + 1]),
+        )
+        for copy in pair:
+            copy.start()
+        loads.append(pair)
+    batches = []
+    for k in range(share // BATCH):
+        loads[k][0].wait()
+        columns = []
+        for f in range(BATCH * k, BATCH * (k + 1)):
+            flipped = []
+            for h in range(2):
+                column = jnp.concatenate([arrived[s, 2 * f + h] for s in range(peers)], axis=0)
+                flipped.append(column.astype(F32).T.astype(BF16))
+            columns.append(jnp.concatenate(flipped, axis=0))
+        loads[k][1].wait()
+        batches.append(
+            [nt(column, turned[BATCH * k + i]).astype(BF16) for i, column in enumerate(columns)]
+        )
+    tiles = [arrived[s, 2 * share].astype(F32) for s in range(peers)]
     misfit = [
         jnp.concatenate([t[:, width * k : width * (k + 1)] for t in tiles], axis=1)
         for k in range(2)
     ]
     blank = jnp.zeros((8, channels), F32)
     gram = jnp.zeros((MEM + 16, MEM), F32)
-    batch = 5
-    for begin in range(0, share, batch):
-        lefts, rights = [], []
-        for f in range(begin, begin + batch):
-            flipped = []
-            for h in range(2):
-                column = jnp.concatenate(
-                    [arrived[s * step + 2 * f + h] for s in range(peers)], axis=0
-                )
-                flipped.append(column.astype(F32).T.astype(BF16))
-            whitened = nt(jnp.concatenate(flipped, axis=0), turned[f]).astype(BF16)
+    for k, batch in enumerate(batches):
+        lefts = []
+        for i, whitened in enumerate(batch):
+            f = BATCH * k + i
             row = jnp.where(iota2(8, channels, 0) == f % 8, misfit[f // 8], 0.0)
             rows = jnp.concatenate([row, blank], axis=0).astype(BF16)
-            rights.append(whitened)
             lefts.append(jnp.concatenate([whitened, rows], axis=0))
-        gram = gram + nt(jnp.concatenate(lefts, axis=1), jnp.concatenate(rights, axis=1))
+        gram = gram + nt(jnp.concatenate(lefts, axis=1), jnp.concatenate(batch, axis=1))
     pull = gram[MEM : MEM + 16, :]
     out[0:16] = gram[0:128, 0:128].reshape(16, 8, 128)
     out[16:32] = gram[128:256, 0:128].reshape(16, 8, 128)
@@ -305,11 +342,15 @@
 
     payload = pl.pallas_call(
         slot_kernel,
-        out_shape=jax.ShapeDtypeStruct((2 * foot_rows + peers, 8, 128), BF16),
+        out_shape=jax.ShapeDtypeStruct((peers, 2 * share + 1, 8, 128), BF16),
         in_specs=[SM] + [VM] * (window + 1),
-        out_specs=VM,
-        scratch_shapes=[pltpu.VMEM((window * capacity, *slab), BF16)],
-        compiler_params=PARAMS,
+        out_specs=HB,
+        scratch_shapes=[
+            pltpu.VMEM((window * capacity, *slab), BF16),
+            pltpu.VMEM((peers, 2 * share + 1, 8, 128), BF16),
+            pltpu.SemaphoreType.DMA((2,)),
+        ],
+        compiler_params=WHOLE,
         cost_estimate=cost(0, 4 * foot_rows * levels * members),
         name="slots",
     )(footprint_slot, *parts, misfits)
@@ -320,7 +361,11 @@
         turn_kernel,
         out_shape=jax.ShapeDtypeStruct((share, peers * width, 128), BF16),
         in_specs=[SM, VM, VM, VM],
-        out_specs=VM,
+        out_specs=HB,
+        scratch_shapes=[
+            pltpu.VMEM((share, peers * width, 128), BF16),
+            pltpu.SemaphoreType.DMA((share // BATCH,)),
+        ],
         compiler_params=PARAMS,
         cost_estimate=cost(4 * 512 * share * 256 * 128, 4 * jacobian.size),
         name="turn",
@@ -329,9 +374,14 @@
     tiles = pl.pallas_call(
         terms_kernel,
         out_shape=jax.ShapeDtypeStruct((64, 8, 128), F32),
-        in_specs=[VM, VM],
+        in_specs=[HB, HB],
         out_specs=VM,
-        compiler_params=PARAMS,
+        scratch_shapes=[
+            pltpu.VMEM(turned.shape, BF16),
+            pltpu.VMEM(arrived.shape, BF16),
+            pltpu.SemaphoreType.DMA((2 * (share // BATCH),)),
+        ],
+        compiler_params=WHOLE,
         cost_estimate=cost(2 * 512 * share * 256 * 384, 2 * jacobian.size),
         name="terms",
     )(turned, arrived)

time: 169 us -> 169 us (level)
  local copies, waits for them, and re-layouts: 7.06 us -> 2.77 us
  Pallas kernels: 52.6 us -> 55.2 us
  waiting for transfers between devices: 25.1 us -> 27.2 us
    unnamed x30 -> x20, local copies, waits for them, and re-layouts: 6.26 us -> 2.57 us
    ppermute x4, waiting for transfers between devices: 3.43 us -> 6.04 us  [send_by(): lax.ppermute(value, axis, [(s, (s + steps) % count) for s in range(count)])]
  transfers between devices with their start and end apart: 6 -> 6, of which waited for: 4 -> 4; matrix products, arithmetic and copies ran while one was open for 1% -> 0% of each run, Pallas kernels for 4% -> 5%
where the time goes in v6:
time: 169 us; the launch traced here: 168 us
  Pallas kernels  55.2 us (33%)
  blocking collectives  50.2 us (30%)
  starting transfers between devices  32 us (19%)
  waiting for transfers between devices  27.2 us (16%)
  local copies, waits for them, and re-layouts  2.77 us (2%)
    all_to_all x3, blocking collectives, swap(): return lax.all_to_all(x, axis, 0, 0, tiled=True)  50.2 us
    pallas_call x1, Pallas kernels, local(): pl.pallas_call(solve_kernel, out_shape=jax.ShapeDtypeStruct(flat_rows.sha...  43.6 us
    all_to_all x2, waiting for transfers between devices, swap(): return lax.all_to_all(x, axis, 0, 0, tiled=True)  21.1 us
    all_to_all x2, starting transfers between devices, swap(): return lax.all_to_all(x, axis, 0, 0, tiled=True)  16.6 us
    ppermute x4, starting transfers between devices, send_by(): lax.ppermute(value, axis, [(s, (s + steps) % count) for s in range(count)])  15.4 us
    ppermute x4, waiting for transfers between devices, send_by(): lax.ppermute(value, axis, [(s, (s + steps) % count) for s in range(count)])  6.04 us
    pallas_call x1, Pallas kernels, local(): pl.pallas_call(terms_kernel, out_shape=jax.ShapeDtypeStruct((64, 8, 128),...  3.83 us
  transfers between devices with their start and end apart: 6, of which 4 were waited for; matrix products, arithmetic and copies ran while one was open for 0% of the time, Pallas kernels for 5%

profile of v6, /device:TPU:1, one launch (start us, length us, event | category | flops | bytes accessed | tf_op | source)
XLA Modules:
  0.0 168.3 jit_solution(17205121347385794893)
XLA Ops:
  0.0 0.0 copy-start.7
  0.0 0.0 copy-start
  0.0 12.0 %all-to-all-start = ((bf16[160,32,128]{2,1,0:T(8,128)(2,1)}), bf16[160,32,128]{2,1,0:T(8,128)(2,1)S(1)}, u32[]{:S(2)}, u32[]{:S(2)}) async-start(bf16[160,32,128]{2,1,0:T(8,128)(2,1)} %param.10), calls=%async_computation | async-start | bytes 2621440 | tf_op jit(solution)/shard_map/all_to_all | solution.py:284
  12.0 0.0 copy-done.7
  12.0 0.0 copy-start.8
  12.0 0.0 copy-start.6
  12.0 0.0 copy-start.5
  12.0 0.1 reshape.18.pick
  12.1 0.0 copy-done
  12.1 1.7 pick.1
  13.8 0.0 copy-start.3
  13.8 0.7 copy-done.3
  14.5 7.6 %collective-permute-start = (bf16[40,8,256]{2,1,0:T(8,128)(2,1)}, bf16[40,8,256]{2,1,0:T(8,128)(2,1)}, u32[]{:S(2)}, u32[]{:S(2)}) collective-permute-start(bf16[40,8,256]{2,1,0:T(8,128)(2,1)} %get-tuple-element.12), channel_id=1, source_target_pairs={{0,480},{16,496},{32,0},{48,16},{64,32},{80,48},{96,64},{112,80},{... | collective-permute-start | bytes 491528 | tf_op jit(solution)/shard_map/ppermute | solution.py:280
  22.0 2.8 %collective-permute-start.1 = (bf16[40,8,256]{2,1,0:T(8,128)(2,1)}, bf16[40,8,256]{2,1,0:T(8,128)(2,1)}, u32[]{:S(2)}, u32[]{:S(2)}) collective-permute-start(bf16[40,8,256]{2,1,0:T(8,128)(2,1)} %get-tuple-element.13), channel_id=1, source_target_pairs={{0,496},{16,0},{32,16},{48,32},{64,48},{80,64},{96,80},{112,96},{1... | collective-permute-start | bytes 491528 | tf_op jit(solution)/shard_map/ppermute | solution.py:280
  24.8 2.5 %collective-permute-start.2 = (bf16[40,8,256]{2,1,0:T(8,128)(2,1)}, bf16[40,8,256]{2,1,0:T(8,128)(2,1)}, u32[]{:S(2)}, u32[]{:S(2)}) collective-permute-start(bf16[40,8,256]{2,1,0:T(8,128)(2,1)} %get-tuple-element.15), channel_id=1, source_target_pairs={{0,16},{16,32},{32,48},{48,64},{64,80},{80,96},{96,112},{112,128},... | collective-permute-start | bytes 491528 | tf_op jit(solution)/shard_map/ppermute | solution.py:280
  27.3 2.6 %collective-permute-start.3 = (bf16[40,8,256]{2,1,0:T(8,128)(2,1)S(1)}, bf16[40,8,256]{2,1,0:T(8,128)(2,1)}, u32[]{:S(2)}, u32[]{:S(2)}) collective-permute-start(bf16[40,8,256]{2,1,0:T(8,128)(2,1)S(1)} %get-tuple-element.16), channel_id=1, source_target_pairs={{0,32},{16,48},{32,64},{48,80},{64,96},{80,112},{96,128},{112,144}... | collective-permute-start | bytes 491528 | tf_op jit(solution)/shard_map/ppermute | solution.py:280
  30.6 0.0 copy-done.8
  30.6 0.1 reshape.19.scales
  30.7 0.0 copy-done.6
  30.7 0.1 copy.13.innovation
  30.8 0.1 pad_add_fusion.place
  30.8 0.0 copy-done.5
  30.8 0.1 copy.15.vectors
  31.0 0.8 misfit.1.misfits
  31.8 0.0 copy-start.4
  31.8 0.6 copy-done.4
  32.4 0.0 collective-permute-done.a0
  32.4 0.0 collective-permute-done.1.a1
  32.4 3.0 %collective-permute-done.2.a3 = bf16[40,8,256]{2,1,0:T(8,128)(2,1)} collective-permute-done((bf16[40,8,256]{2,1,0:T(8,128)(2,1)}, bf16[40,8,256]{2,1,0:T(8,128)(2,1)}, u32[]{:S(2)}, u32[]{:S(2)}) %collective-permute-start.2) | collective-permute-done | bytes 163872 | tf_op jit(solution)/shard_map/ppermute | solution.py:280
  35.5 3.0 %collective-permute-done.3.a4 = bf16[40,8,256]{2,1,0:T(8,128)(2,1)} collective-permute-done((bf16[40,8,256]{2,1,0:T(8,128)(2,1)S(1)}, bf16[40,8,256]{2,1,0:T(8,128)(2,1)}, u32[]{:S(2)}, u32[]{:S(2)}) %collective-permute-start.3) | collective-permute-done | bytes 163872 | tf_op jit(solution)/shard_map/ppermute | solution.py:280
  38.5 2.3 %slots.1 = bf16[16,21,8,128]{3,2,1,0:T(8,128)(2,1)} custom-call(s32[160]{0:T(256)} %slot.1, bf16[40,8,256]{2,1,0:T(8,128)(2,1)} %collective-permute-done.a0, bf16[40,8,256]{2,1,0:T(8,128)(2,1)} %collective-permute-done.1.a1, bf16[40,8,256]{2,1,0:T(8,128)(2,1)} %copy-done.3, bf16[40,8,256]{2,1,0:T(8,128)(2,1)} %collective-permute-done.2.a3, ...), custom_call_target="tpu_custom_call" | custom-call | bytes 1310720 | tf_op jit(solution)/shard_map/slots/pallas_call | solution.py:343
  40.8 4.4 %all-to-all-done.jacobian = bf16[160,32,128]{2,1,0:T(8,128)(2,1)S(1)} async-done(((bf16[160,32,128]{2,1,0:T(8,128)(2,1)}), bf16[160,32,128]{2,1,0:T(8,128)(2,1)S(1)}, u32[]{:S(2)}, u32[]{:S(2)}) %all-to-all-start) | async-done | bytes 1310752 | tf_op jit(solution)/shard_map/all_to_all | solution.py:284
  45.2 4.6 %all-to-all-start.1 = ((bf16[16,21,8,128]{3,2,1,0:T(8,128)(2,1)}), bf16[16,21,8,128]{3,2,1,0:T(8,128)(2,1)}, u32[]{:S(2)}, u32[]{:S(2)}) async-start(bf16[16,21,8,128]{3,2,1,0:T(8,128)(2,1)} %slots.1), calls=%async_computation.1 | async-start | bytes 1376256 | tf_op jit(solution)/shard_map/all_to_all | solution.py:284
  49.8 2.9 %turn.1.turned_far = bf16[10,512,128]{2,1,0:T(8,128)(2,1)S(1)} custom-call(s32[2]{0:T(128)S(1)} %pad_add_fusion.place, f32[512,32]{1,0:T(8,128)S(1)} %copy.15.vectors, f32[2,256]{1,0:T(2,128)S(1)} %reshape.17.scales, bf16[160,32,128]{2,1,0:T(8,128)(2,1)S(1)} %all-to-all-done.jacobian), custom_call_target="tpu_custom_call" | custom-call | flops 671088640 | bytes 2621440 | tf_op jit(solution)/shard_map/turn/pallas_call | solution.py:360
  52.8 0.0 copy-start.1
  52.8 1.0 copy-done.1
  53.8 16.8 %all-to-all-done.1.arrived_far = bf16[16,21,8,128]{3,2,1,0:T(8,128)(2,1)} async-done(((bf16[16,21,8,128]{3,2,1,0:T(8,128)(2,1)}), bf16[16,21,8,128]{3,2,1,0:T(8,128)(2,1)}, u32[]{:S(2)}, u32[]{:S(2)}) %all-to-all-start.1) | async-done | bytes 688160 | tf_op jit(solution)/shard_map/all_to_all | solution.py:284
  70.6 3.8 %terms.1 = f32[64,8,128]{2,1,0:T(8,128)} custom-call(bf16[10,512,128]{2,1,0:T(8,128)(2,1)} %copy-done.1, bf16[16,21,8,128]{3,2,1,0:T(8,128)(2,1)} %all-to-all-done.1.arrived_far), custom_call_target="tpu_custom_call" | custom-call | flops 1006632960 | bytes 1310720 | tf_op jit(solution)/shard_map/terms/pallas_call | solution.py:374
  74.4 0.0 copy-start.2
  74.4 17.4 %all_to_all.25 = f32[64,8,128]{2,1,0:T(8,128)S(1)} all-to-all(f32[64,8,128]{2,1,0:T(8,128)} %terms.1), channel_id=1, replica_groups=mesh['y'=8,'x'=4,'z'=8,'c'=2] {'x','z','c'}, dimensions={0} | all-to-all | bytes 524288 | tf_op jit(solution)/shard_map/all_to_all | solution.py:284
  91.9 0.1 reduce_sum.18
  92.0 13.5 %all_to_all.26 = f32[8,8,128]{2,1,0:T(8,128)S(1)} all-to-all(f32[8,8,128]{2,1,0:T(8,128)S(1)} %broadcast_in_dim.7), channel_id=1, replica_groups=mesh['y'=8,'x'=4,'z'=8,'c'=2] {'y'}, dimensions={0} | all-to-all | bytes 65536 | tf_op jit(solution)/shard_map/all_to_all | solution.py:284
  105.5 19.3 %all_to_all.27.summed = f32[64,8,128]{2,1,0:T(8,128)S(1)} all-to-all(f32[64,8,128]{2,1,0:T(8,128)S(1)} %broadcast_in_dim.8), channel_id=1, replica_groups=mesh['y'=8,'x'=4,'z'=8,'c'=2] {'x','z','c'}, dimensions={0} | all-to-all | bytes 524288 | tf_op jit(solution)/shard_map/all_to_all | solution.py:284
  124.7 0.0 copy-done.2
  124.7 43.6 %solve.1 = bf16[3072,256]{1,0:T(8,128)(2,1)} custom-call(f32[64,8,128]{2,1,0:T(8,128)S(1)} %all_to_all.27.summed, f32[256,256]{1,0:T(8,128)S(1)} %copy-done.2, bf16[3072,256]{1,0:T(8,128)(2,1)S(1)} %bitcast.3), custom_call_target="tpu_custom_call" | custom-call | tf_op jit(solution)/shard_map/solve/pallas_call | solution.py:393
  (6 shorter events, 0.1 us)
Async XLA Ops:
  0.0 12.0 %copy-start.7 = (s32[1,5,40]{2,0,1:T(1,128)S(1)}, s32[1,5,40]{2,0,1:T(1,128)}, u32[]{:S(2)}) copy-start(s32[1,5,40]{2,0,1:T(1,128)} %param.15) | copy-start | bytes 2404
  0.0 12.1 %copy-start = (bf16[384,8,256]{2,1,0:T(8,128)(2,1)S(1)}, bf16[384,8,256]{2,1,0:T(8,128)(2,1)}, u32[]{:S(2)}) copy-start(bf16[384,8,256]{2,1,0:T(8,128)(2,1)} %ensemble.1) | copy-start | bytes 4718596
  0.0 45.2 %all-to-all-start = ((bf16[160,32,128]{2,1,0:T(8,128)(2,1)}), bf16[160,32,128]{2,1,0:T(8,128)(2,1)S(1)}, u32[]{:S(2)}, u32[]{:S(2)}) async-start(bf16[160,32,128]{2,1,0:T(8,128)(2,1)} %param.10), calls=%async_computation | async-start | bytes 2621440 | tf_op jit(solution)/shard_map/all_to_all | solution.py:284
  12.0 18.6 %copy-start.8 = (f32[512]{0:T(512)S(1)}, f32[512]{0:T(512)}, u32[]{:S(2)}) copy-start(f32[512]{0:T(512)} %param.13) | copy-start | bytes 6148
  12.0 18.7 %copy-start.6 = (f32[160,32]{0,1:T(8,128)S(1)}, f32[160,32]{0,1:T(8,128)}, u32[]{:S(2)}) copy-start(f32[160,32]{0,1:T(8,128)} %param.11) | copy-start | bytes 61444
  12.0 18.8 %copy-start.5 = (f32[512,32]{0,1:T(8,128)S(1)}, f32[512,32]{0,1:T(8,128)}, u32[]{:S(2)}) copy-start(f32[512,32]{0,1:T(8,128)} %param.12) | copy-start | bytes 196612
  13.8 0.7 copy-start.3
  14.5 18.0 %collective-permute-start = (bf16[40,8,256]{2,1,0:T(8,128)(2,1)}, bf16[40,8,256]{2,1,0:T(8,128)(2,1)}, u32[]{:S(2)}, u32[]{:S(2)}) collective-permute-start(bf16[40,8,256]{2,1,0:T(8,128)(2,1)} %get-tuple-element.12), channel_id=1, source_target_pairs={{0,480},{16,496},{32,0},{48,16},{64,32},{80,48},{96,64},{112,80},{... | collective-permute-start | bytes 491528 | tf_op jit(solution)/shard_map/ppermute | solution.py:280
  22.0 10.4 %collective-permute-start.1 = (bf16[40,8,256]{2,1,0:T(8,128)(2,1)}, bf16[40,8,256]{2,1,0:T(8,128)(2,1)}, u32[]{:S(2)}, u32[]{:S(2)}) collective-permute-start(bf16[40,8,256]{2,1,0:T(8,128)(2,1)} %get-tuple-element.13), channel_id=1, source_target_pairs={{0,496},{16,0},{32,16},{48,32},{64,48},{80,64},{96,80},{112,96},{1... | collective-permute-start | bytes 491528 | tf_op jit(solution)/shard_map/ppermute | solution.py:280
  24.8 10.6 %collective-permute-start.2 = (bf16[40,8,256]{2,1,0:T(8,128)(2,1)}, bf16[40,8,256]{2,1,0:T(8,128)(2,1)}, u32[]{:S(2)}, u32[]{:S(2)}) collective-permute-start(bf16[40,8,256]{2,1,0:T(8,128)(2,1)} %get-tuple-element.15), channel_id=1, source_target_pairs={{0,16},{16,32},{32,48},{48,64},{64,80},{80,96},{96,112},{112,128},... | collective-permute-start | bytes 491528 | tf_op jit(solution)/shard_map/ppermute | solution.py:280
  27.3 11.1 %collective-permute-start.3 = (bf16[40,8,256]{2,1,0:T(8,128)(2,1)S(1)}, bf16[40,8,256]{2,1,0:T(8,128)(2,1)}, u32[]{:S(2)}, u32[]{:S(2)}) collective-permute-start(bf16[40,8,256]{2,1,0:T(8,128)(2,1)S(1)} %get-tuple-element.16), channel_id=1, source_target_pairs={{0,32},{16,48},{32,64},{48,80},{64,96},{80,112},{96,128},{112,144}... | collective-permute-start | bytes 491528 | tf_op jit(solution)/shard_map/ppermute | solution.py:280
  31.8 0.6 copy-start.4
  45.2 25.4 %all-to-all-start.1 = ((bf16[16,21,8,128]{3,2,1,0:T(8,128)(2,1)}), bf16[16,21,8,128]{3,2,1,0:T(8,128)(2,1)}, u32[]{:S(2)}, u32[]{:S(2)}) async-start(bf16[16,21,8,128]{3,2,1,0:T(8,128)(2,1)} %slots.1), calls=%async_computation.1 | async-start | bytes 1376256 | tf_op jit(solution)/shard_map/all_to_all | solution.py:284
  52.8 1.1 copy-start.1
  74.4 50.3 %copy-start.2 = (f32[256,256]{1,0:T(8,128)S(1)}, f32[256,256]{1,0:T(8,128)}, u32[]{:S(2)}) copy-start(f32[256,256]{1,0:T(8,128)} %basis.1) | copy-start | bytes 786436

commit v7 on v5

--- a/solution.py
+++ b/solution.py
@@ -16,7 +16,10 @@
 BF16 = jnp.bfloat16
 VM = pl.BlockSpec(memory_space=pltpu.VMEM)
 SM = pl.BlockSpec(memory_space=pltpu.SMEM)
-PARAMS = pltpu.CompilerParams(vmem_limit_bytes=20 * 2**20)
+
+
+def grant(mebibytes):
+    return pltpu.CompilerParams(vmem_limit_bytes=mebibytes * 2**20)
 
 
 def cost(flops, size):
@@ -280,7 +283,7 @@
         out_shape=[jax.ShapeDtypeStruct((capacity, *slab), BF16)] * window,
         in_specs=[SM, VM],
         out_specs=[VM] * window,
-        compiler_params=PARAMS,
+        compiler_params=grant(57),
         cost_estimate=cost(0, 2 * ensemble.size),
         name="pick",
     )(column_pick.reshape(-1), ensemble)
@@ -298,7 +301,7 @@
         out_shape=jax.ShapeDtypeStruct((peers, 8, 128), BF16),
         in_specs=[SM, VM, VM, VM],
         out_specs=VM,
-        compiler_params=PARAMS,
+        compiler_params=grant(12),
         cost_estimate=cost(2 * foot_rows * width * width, 4 * error_vectors.size),
         name="misfit",
     )(place, innovation, error_vectors, scales.reshape(peers, width))
@@ -309,7 +312,7 @@
         in_specs=[SM] + [VM] * (window + 1),
         out_specs=VM,
         scratch_shapes=[pltpu.VMEM((window * capacity, *slab), BF16)],
-        compiler_params=PARAMS,
+        compiler_params=grant(48),
         cost_estimate=cost(0, 4 * foot_rows * levels * members),
         name="slots",
     )(footprint_slot, *parts, misfits)
@@ -321,7 +324,7 @@
         out_shape=jax.ShapeDtypeStruct((share, peers * width, 128), BF16),
         in_specs=[SM, VM, VM, VM],
         out_specs=VM,
-        compiler_params=PARAMS,
+        compiler_params=grant(6),
         cost_estimate=cost(4 * 512 * share * 256 * 128, 4 * jacobian.size),
         name="turn",
     )(place, error_vectors, scales.reshape(2, members), sensitivity)
@@ -331,7 +334,7 @@
         out_shape=jax.ShapeDtypeStruct((64, 8, 128), F32),
         in_specs=[VM, VM],
         out_specs=VM,
-        compiler_params=PARAMS,
+        compiler_params=grant(20),
         cost_estimate=cost(2 * 512 * share * 256 * 384, 2 * jacobian.size),
         name="terms",
     )(turned, arrived)
@@ -352,7 +355,7 @@
             pltpu.VMEM((chunks, flat_rows.shape[0] // chunks, members), BF16),
             pltpu.SemaphoreType.DMA((chunks,)),
         ],
-        compiler_params=PARAMS,
+        compiler_params=grant(12),
         name="solve",
     )(summed, ensemble_vectors, flat_rows)
     return updated.reshape(ensemble.shape)

time: 169 us -> 168 us (level)
  local copies, waits for them, and re-layouts: 7.06 us -> 1.95 us
  waiting for transfers between devices: 25.1 us -> 28.2 us
    unnamed x30 -> x18, local copies, waits for them, and re-layouts: 6.26 us -> 1.17 us
    ppermute x4, waiting for transfers between devices: 3.43 us -> 6.52 us  [send_by(): lax.ppermute(value, axis, [(s, (s + steps) % count) for s in range(count)])]
  transfers between devices with their start and end apart: 6 -> 6, of which waited for: 4 -> 4; matrix products, arithmetic and copies ran while one was open for 1% -> 1% of each run, Pallas kernels for 4% -> 5%
where the time goes in v7:
time: 168 us; the launch traced here: 167 us
  Pallas kernels  54 us (32%)
  blocking collectives  48.9 us (29%)
  starting transfers between devices  33.1 us (20%)
  waiting for transfers between devices  28.2 us (17%)
  local copies, waits for them, and re-layouts  1.95 us (1%)
    all_to_all x3, blocking collectives, swap(): return lax.all_to_all(x, axis, 0, 0, tiled=True)  48.9 us
    pallas_call x1, Pallas kernels, local(): pl.pallas_call(solve_kernel, out_shape=jax.ShapeDtypeStruct(flat_rows.sha...  43.6 us
    all_to_all x2, waiting for transfers between devices, swap(): return lax.all_to_all(x, axis, 0, 0, tiled=True)  21.7 us
    all_to_all x2, starting transfers between devices, swap(): return lax.all_to_all(x, axis, 0, 0, tiled=True)  17.7 us
    ppermute x4, starting transfers between devices, send_by(): lax.ppermute(value, axis, [(s, (s + steps) % count) for s in range(count)])  15.4 us
    ppermute x4, waiting for transfers between devices, send_by(): lax.ppermute(value, axis, [(s, (s + steps) % count) for s in range(count)])  6.52 us
  transfers between devices with their start and end apart: 6, of which 4 were waited for; matrix products, arithmetic and copies ran while one was open for 1% of the time, Pallas kernels for 5%

profile of v7, /device:TPU:1, one launch (start us, length us, event | category | flops | bytes accessed | tf_op | source)
XLA Modules:
  0.0 167.1 jit_solution(11227294315775975349)
XLA Ops:
  0.0 0.0 copy-start.6
  0.0 12.0 %all-to-all-start = ((bf16[160,32,128]{2,1,0:T(8,128)(2,1)}), bf16[160,32,128]{2,1,0:T(8,128)(2,1)S(1)}, u32[]{:S(2)}, u32[]{:S(2)}) async-start(bf16[160,32,128]{2,1,0:T(8,128)(2,1)} %param.10), calls=%async_computation | async-start | bytes 2621440 | tf_op jit(solution)/shard_map/all_to_all | solution.py:250
  12.0 0.0 copy-done.6
  12.0 0.0 copy-start.7
  12.0 0.0 copy-start.5
  12.0 0.0 copy-start.4
  12.0 0.0 copy-start.3
  12.0 0.7 reshape.18.pick
  12.7 2.7 %pick.1 = (bf16[40,8,256]{2,1,0:T(8,128)(2,1)}, bf16[40,8,256]{2,1,0:T(8,128)(2,1)}, bf16[40,8,256]{2,1,0:T(8,128)(2,1)}, bf16[40,8,256]{2,1,0:T(8,128)(2,1)}, bf16[40,8,256]{2,1,0:T(8,128)(2,1)}) custom-call(s32[200]{0:T(256)} %reshape.18.pick, bf16[384,8,256]{2,1,0:T(8,128)(2,1)} %ensemble.1), custom_call_target="tpu_custom_call" | custom-call | bytes 1572864 | tf_op jit(solution)/shard_map/pick/pallas_call | solution.py:281
  15.4 7.6 %collective-permute-start = (bf16[40,8,256]{2,1,0:T(8,128)(2,1)}, bf16[40,8,256]{2,1,0:T(8,128)(2,1)S(1)}, u32[]{:S(2)}, u32[]{:S(2)}) collective-permute-start(bf16[40,8,256]{2,1,0:T(8,128)(2,1)} %get-tuple-element.12), channel_id=1, source_target_pairs={{0,480},{16,496},{32,0},{48,16},{64,32},{80,48},{96,64},{112,80},{... | collective-permute-start | bytes 491528 | tf_op jit(solution)/shard_map/ppermute | solution.py:246
  22.9 2.8 %collective-permute-start.1 = (bf16[40,8,256]{2,1,0:T(8,128)(2,1)}, bf16[40,8,256]{2,1,0:T(8,128)(2,1)S(1)}, u32[]{:S(2)}, u32[]{:S(2)}) collective-permute-start(bf16[40,8,256]{2,1,0:T(8,128)(2,1)} %get-tuple-element.13), channel_id=1, source_target_pairs={{0,496},{16,0},{32,16},{48,32},{64,48},{80,64},{96,80},{112,96},{1... | collective-permute-start | bytes 491528 | tf_op jit(solution)/shard_map/ppermute | solution.py:246
  25.7 2.5 %collective-permute-start.2 = (bf16[40,8,256]{2,1,0:T(8,128)(2,1)}, bf16[40,8,256]{2,1,0:T(8,128)(2,1)S(1)}, u32[]{:S(2)}, u32[]{:S(2)}) collective-permute-start(bf16[40,8,256]{2,1,0:T(8,128)(2,1)} %get-tuple-element.15), channel_id=1, source_target_pairs={{0,16},{16,32},{32,48},{48,64},{64,80},{80,96},{96,112},{112,128},... | collective-permute-start | bytes 491528 | tf_op jit(solution)/shard_map/ppermute | solution.py:246
  28.2 2.6 %collective-permute-start.3 = (bf16[40,8,256]{2,1,0:T(8,128)(2,1)}, bf16[40,8,256]{2,1,0:T(8,128)(2,1)S(1)}, u32[]{:S(2)}, u32[]{:S(2)}) collective-permute-start(bf16[40,8,256]{2,1,0:T(8,128)(2,1)} %get-tuple-element.16), channel_id=1, source_target_pairs={{0,32},{16,48},{32,64},{48,80},{64,96},{80,112},{96,128},{112,144}... | collective-permute-start | bytes 491528 | tf_op jit(solution)/shard_map/ppermute | solution.py:246
  31.5 0.0 copy-done.7
  31.5 0.1 reshape.19.scales
  31.5 0.0 copy-done.5
  31.6 0.1 copy.13.innovation
  31.7 0.1 pad_add_fusion.place
  31.7 0.0 copy-done.4
  31.7 0.1 copy.15.vectors
  31.9 0.8 misfit.1.misfits
  32.7 0.0 collective-permute-done.a0
  32.7 0.0 collective-permute-done.1.a1
  32.7 3.5 %collective-permute-done.2.a3 = bf16[40,8,256]{2,1,0:T(8,128)(2,1)S(1)} collective-permute-done((bf16[40,8,256]{2,1,0:T(8,128)(2,1)}, bf16[40,8,256]{2,1,0:T(8,128)(2,1)S(1)}, u32[]{:S(2)}, u32[]{:S(2)}) %collective-permute-start.2) | collective-permute-done | bytes 163872 | tf_op jit(solution)/shard_map/ppermute | solution.py:246
  36.2 3.0 %collective-permute-done.3.a4 = bf16[40,8,256]{2,1,0:T(8,128)(2,1)S(1)} collective-permute-done((bf16[40,8,256]{2,1,0:T(8,128)(2,1)}, bf16[40,8,256]{2,1,0:T(8,128)(2,1)S(1)}, u32[]{:S(2)}, u32[]{:S(2)}) %collective-permute-start.3) | collective-permute-done | bytes 163872 | tf_op jit(solution)/shard_map/ppermute | solution.py:246
  39.2 0.0 copy-done.3
  39.2 0.0 copy-start.2
  39.3 0.9 copy-done.2
  40.2 1.7 %slots.1 = bf16[336,8,128]{2,1,0:T(8,128)(2,1)} custom-call(s32[160]{0:T(256)S(1)} %copy-done.3, bf16[40,8,256]{2,1,0:T(8,128)(2,1)S(1)} %collective-permute-done.a0, bf16[40,8,256]{2,1,0:T(8,128)(2,1)S(1)} %collective-permute-done.1.a1, bf16[40,8,256]{2,1,0:T(8,128)(2,1)S(1)} %copy-done.2, bf16[40,8,256]{2,1,0:T(8,128)(2,1)S(1)} %collective-permute-done.2.a3, ...), custom_call_target="tpu_custom_call" | custom-call | bytes 1310720 | tf_op jit(solution)/shard_map/slots/pallas_call | solution.py:309
  41.9 3.3 %all-to-all-done.jacobian = bf16[160,32,128]{2,1,0:T(8,128)(2,1)S(1)} async-done(((bf16[160,32,128]{2,1,0:T(8,128)(2,1)}), bf16[160,32,128]{2,1,0:T(8,128)(2,1)S(1)}, u32[]{:S(2)}, u32[]{:S(2)}) %all-to-all-start) | async-done | bytes 1310752 | tf_op jit(solution)/shard_map/all_to_all | solution.py:250
  45.2 5.7 %all-to-all-start.1 = ((bf16[336,8,128]{2,1,0:T(8,128)(2,1)}), bf16[336,8,128]{2,1,0:T(8,128)(2,1)}, u32[]{:S(2)}, u32[]{:S(2)}) async-start(bf16[336,8,128]{2,1,0:T(8,128)(2,1)} %slots.1), calls=%async_computation.1 | async-start | bytes 1376256 | tf_op jit(solution)/shard_map/all_to_all | solution.py:250
  50.9 2.3 %turn.1.turned = bf16[10,512,128]{2,1,0:T(8,128)(2,1)S(1)} custom-call(s32[2]{0:T(128)S(1)} %pad_add_fusion.place, f32[512,32]{1,0:T(8,128)S(1)} %copy.15.vectors, f32[2,256]{1,0:T(2,128)S(1)} %reshape.17.scales, bf16[160,32,128]{2,1,0:T(8,128)(2,1)S(1)} %all-to-all-done.jacobian), custom_call_target="tpu_custom_call" | custom-call | flops 671088640 | bytes 2621440 | tf_op jit(solution)/shard_map/turn/pallas_call | solution.py:322
  53.2 18.4 %all-to-all-done.1.arrived = bf16[336,8,128]{2,1,0:T(8,128)(2,1)} async-done(((bf16[336,8,128]{2,1,0:T(8,128)(2,1)}), bf16[336,8,128]{2,1,0:T(8,128)(2,1)}, u32[]{:S(2)}, u32[]{:S(2)}) %all-to-all-start.1) | async-done | bytes 688160 | tf_op jit(solution)/shard_map/all_to_all | solution.py:250
  71.7 0.0 copy-start.1
  71.7 2.8 %terms.1 = f32[64,8,128]{2,1,0:T(8,128)S(1)} custom-call(bf16[10,512,128]{2,1,0:T(8,128)(2,1)S(1)} %turn.1.turned, bf16[336,8,128]{2,1,0:T(8,128)(2,1)} %all-to-all-done.1.arrived), custom_call_target="tpu_custom_call" | custom-call | flops 1006632960 | bytes 1310720 | tf_op jit(solution)/shard_map/terms/pallas_call | solution.py:332
  74.4 0.0 copy-start
  74.5 16.2 %all_to_all.25 = f32[64,8,128]{2,1,0:T(8,128)S(1)} all-to-all(f32[64,8,128]{2,1,0:T(8,128)S(1)} %terms.1), channel_id=1, replica_groups=mesh['y'=8,'x'=4,'z'=8,'c'=2] {'x','z','c'}, dimensions={0} | all-to-all | bytes 524288 | tf_op jit(solution)/shard_map/all_to_all | solution.py:250
  90.6 0.1 reduce_sum.18
  90.7 13.5 %all_to_all.26 = f32[8,8,128]{2,1,0:T(8,128)S(1)} all-to-all(f32[8,8,128]{2,1,0:T(8,128)S(1)} %broadcast_in_dim.7), channel_id=1, replica_groups=mesh['y'=8,'x'=4,'z'=8,'c'=2] {'y'}, dimensions={0} | all-to-all | bytes 65536 | tf_op jit(solution)/shard_map/all_to_all | solution.py:250
  104.2 19.3 %all_to_all.27.summed = f32[64,8,128]{2,1,0:T(8,128)S(1)} all-to-all(f32[64,8,128]{2,1,0:T(8,128)S(1)} %broadcast_in_dim.8), channel_id=1, replica_groups=mesh['y'=8,'x'=4,'z'=8,'c'=2] {'x','z','c'}, dimensions={0} | all-to-all | bytes 524288 | tf_op jit(solution)/shard_map/all_to_all | solution.py:250
  123.5 0.0 copy-done.1
  123.5 0.0 copy-done
  123.5 43.6 %solve.1 = bf16[3072,256]{1,0:T(8,128)(2,1)} custom-call(f32[64,8,128]{2,1,0:T(8,128)S(1)} %all_to_all.27.summed, f32[256,256]{1,0:T(8,128)S(1)} %copy-done.1, bf16[3072,256]{1,0:T(8,128)(2,1)S(1)} %bitcast.3), custom_call_target="tpu_custom_call" | custom-call | tf_op jit(solution)/shard_map/solve/pallas_call | solution.py:346
  (6 shorter events, 0.1 us)
Async XLA Ops:
  0.0 12.0 %copy-start.6 = (s32[1,5,40]{2,0,1:T(1,128)S(1)}, s32[1,5,40]{2,0,1:T(1,128)}, u32[]{:S(2)}) copy-start(s32[1,5,40]{2,0,1:T(1,128)} %param.15) | copy-start | bytes 2404
  0.0 45.2 %all-to-all-start = ((bf16[160,32,128]{2,1,0:T(8,128)(2,1)}), bf16[160,32,128]{2,1,0:T(8,128)(2,1)S(1)}, u32[]{:S(2)}, u32[]{:S(2)}) async-start(bf16[160,32,128]{2,1,0:T(8,128)(2,1)} %param.10), calls=%async_computation | async-start | bytes 2621440 | tf_op jit(solution)/shard_map/all_to_all | solution.py:250
  12.0 19.5 %copy-start.7 = (f32[512]{0:T(512)S(1)}, f32[512]{0:T(512)}, u32[]{:S(2)}) copy-start(f32[512]{0:T(512)} %param.13) | copy-start | bytes 6148
  12.0 19.6 %copy-start.5 = (f32[160,32]{0,1:T(8,128)S(1)}, f32[160,32]{0,1:T(8,128)}, u32[]{:S(2)}) copy-start(f32[160,32]{0,1:T(8,128)} %param.11) | copy-start | bytes 61444
  12.0 19.7 %copy-start.4 = (f32[512,32]{0,1:T(8,128)S(1)}, f32[512,32]{0,1:T(8,128)}, u32[]{:S(2)}) copy-start(f32[512,32]{0,1:T(8,128)} %param.12) | copy-start | bytes 196612
  12.0 27.2 %copy-start.3 = (s32[160]{0:T(256)S(1)}, s32[160]{0:T(256)}, u32[]{:S(2)}) copy-start(s32[160]{0:T(256)} %slot.1) | copy-start | bytes 1924
  15.4 17.3 %collective-permute-start = (bf16[40,8,256]{2,1,0:T(8,128)(2,1)}, bf16[40,8,256]{2,1,0:T(8,128)(2,1)S(1)}, u32[]{:S(2)}, u32[]{:S(2)}) collective-permute-start(bf16[40,8,256]{2,1,0:T(8,128)(2,1)} %get-tuple-element.12), channel_id=1, source_target_pairs={{0,480},{16,496},{32,0},{48,16},{64,32},{80,48},{96,64},{112,80},{... | collective-permute-start | bytes 491528 | tf_op jit(solution)/shard_map/ppermute | solution.py:246
  22.9 9.8 %collective-permute-start.1 = (bf16[40,8,256]{2,1,0:T(8,128)(2,1)}, bf16[40,8,256]{2,1,0:T(8,128)(2,1)S(1)}, u32[]{:S(2)}, u32[]{:S(2)}) collective-permute-start(bf16[40,8,256]{2,1,0:T(8,128)(2,1)} %get-tuple-element.13), channel_id=1, source_target_pairs={{0,496},{16,0},{32,16},{48,32},{64,48},{80,64},{96,80},{112,96},{1... | collective-permute-start | bytes 491528 | tf_op jit(solution)/shard_map/ppermute | solution.py:246
  25.7 10.5 %collective-permute-start.2 = (bf16[40,8,256]{2,1,0:T(8,128)(2,1)}, bf16[40,8,256]{2,1,0:T(8,128)(2,1)S(1)}, u32[]{:S(2)}, u32[]{:S(2)}) collective-permute-start(bf16[40,8,256]{2,1,0:T(8,128)(2,1)} %get-tuple-element.15), channel_id=1, source_target_pairs={{0,16},{16,32},{32,48},{48,64},{64,80},{80,96},{96,112},{112,128},... | collective-permute-start | bytes 491528 | tf_op jit(solution)/shard_map/ppermute | solution.py:246
  28.2 11.0 %collective-permute-start.3 = (bf16[40,8,256]{2,1,0:T(8,128)(2,1)}, bf16[40,8,256]{2,1,0:T(8,128)(2,1)S(1)}, u32[]{:S(2)}, u32[]{:S(2)}) collective-permute-start(bf16[40,8,256]{2,1,0:T(8,128)(2,1)} %get-tuple-element.16), channel_id=1, source_target_pairs={{0,32},{16,48},{32,64},{48,80},{64,96},{80,112},{96,128},{112,144}... | collective-permute-start | bytes 491528 | tf_op jit(solution)/shard_map/ppermute | solution.py:246
  39.2 0.9 copy-start.2
  45.2 26.5 %all-to-all-start.1 = ((bf16[336,8,128]{2,1,0:T(8,128)(2,1)}), bf16[336,8,128]{2,1,0:T(8,128)(2,1)}, u32[]{:S(2)}, u32[]{:S(2)}) async-start(bf16[336,8,128]{2,1,0:T(8,128)(2,1)} %slots.1), calls=%async_computation.1 | async-start | bytes 1376256 | tf_op jit(solution)/shard_map/all_to_all | solution.py:250
  71.7 51.8 %copy-start.1 = (f32[256,256]{1,0:T(8,128)S(1)}, f32[256,256]{1,0:T(8,128)}, u32[]{:S(2)}) copy-start(f32[256,256]{1,0:T(8,128)} %basis.1) | copy-start | bytes 786436
  74.4 49.0 %copy-start = (bf16[384,8,256]{2,1,0:T(8,128)(2,1)S(1)}, bf16[384,8,256]{2,1,0:T(8,128)(2,1)}, u32[]{:S(2)}) copy-start(bf16[384,8,256]{2,1,0:T(8,128)(2,1)} %ensemble.1) | copy-start | bytes 4718596

commit v8 on v7

--- a/solution.py
+++ b/solution.py
@@ -16,6 +16,7 @@
 BF16 = jnp.bfloat16
 VM = pl.BlockSpec(memory_space=pltpu.VMEM)
 SM = pl.BlockSpec(memory_space=pltpu.SMEM)
+ANY = pl.BlockSpec(memory_space=pl.ANY)
 
 
 def grant(mebibytes):
@@ -175,7 +176,11 @@
     return x - nn(lower_half(residual).astype(BF16), x.astype(BF16))
 
 
-def solve_kernel(summed, basis, ensemble, out, system, inverse, rows, held, sems):
+def solve_kernel(
+    summed, basis, ensemble_far, out, system, inverse, rows, ensemble, held, load_sem, sems
+):
+    load = pltpu.make_async_copy(ensemble_far, ensemble, load_sem)
+    load.start()
     eye = (iota2(MEM, MEM, 0) == iota2(MEM, MEM, 1)).astype(F32)
     g00 = summed[0:16].reshape(128, 128)
     g10 = summed[16:32].reshape(128, 128)
@@ -229,6 +234,7 @@
     halfway = jnp.sum(x * pull, axis=1, keepdims=True)
     target = (MEM - 1.0) ** 0.5 * basis[...] + halfway
     transform = nn3(x.T, target).astype(BF16)
+    load.wait()
     copies = []
     for i in range(held.shape[0]):
         size = held.shape[1]
@@ -283,7 +289,7 @@
         out_shape=[jax.ShapeDtypeStruct((capacity, *slab), BF16)] * window,
         in_specs=[SM, VM],
         out_specs=[VM] * window,
-        compiler_params=grant(57),
+        compiler_params=grant(20),
         cost_estimate=cost(0, 2 * ensemble.size),
         name="pick",
     )(column_pick.reshape(-1), ensemble)
@@ -301,7 +307,7 @@
         out_shape=jax.ShapeDtypeStruct((peers, 8, 128), BF16),
         in_specs=[SM, VM, VM, VM],
         out_specs=VM,
-        compiler_params=grant(12),
+        compiler_params=grant(20),
         cost_estimate=cost(2 * foot_rows * width * width, 4 * error_vectors.size),
         name="misfit",
     )(place, innovation, error_vectors, scales.reshape(peers, width))
@@ -312,7 +318,7 @@
         in_specs=[SM] + [VM] * (window + 1),
         out_specs=VM,
         scratch_shapes=[pltpu.VMEM((window * capacity, *slab), BF16)],
-        compiler_params=grant(48),
+        compiler_params=grant(20),
         cost_estimate=cost(0, 4 * foot_rows * levels * members),
         name="slots",
     )(footprint_slot, *parts, misfits)
@@ -324,7 +330,7 @@
         out_shape=jax.ShapeDtypeStruct((share, peers * width, 128), BF16),
         in_specs=[SM, VM, VM, VM],
         out_specs=VM,
-        compiler_params=grant(6),
+        compiler_params=grant(20),
         cost_estimate=cost(4 * 512 * share * 256 * 128, 4 * jacobian.size),
         name="turn",
     )(place, error_vectors, scales.reshape(2, members), sensitivity)
@@ -346,16 +352,18 @@
     updated = pl.pallas_call(
         solve_kernel,
         out_shape=jax.ShapeDtypeStruct(flat_rows.shape, BF16),
-        in_specs=[VM, VM, VM],
-        out_specs=pl.BlockSpec(memory_space=pl.ANY),
+        in_specs=[VM, VM, ANY],
+        out_specs=ANY,
         scratch_shapes=[
             pltpu.VMEM((members, members), F32),
             pltpu.VMEM((members, members), F32),
             pltpu.VMEM((members, 2 * members), F32),
+            pltpu.VMEM(flat_rows.shape, BF16),
             pltpu.VMEM((chunks, flat_rows.shape[0] // chunks, members), BF16),
+            pltpu.SemaphoreType.DMA,
             pltpu.SemaphoreType.DMA((chunks,)),
         ],
-        compiler_params=grant(12),
+        compiler_params=grant(57),
         name="solve",
     )(summed, ensemble_vectors, flat_rows)
     return updated.reshape(ensemble.shape)

time: 168 us -> 169 us (level)
  blocking collectives: 48.9 us -> 50.7 us
    all_to_all x2, waiting for transfers between devices: 21.7 us -> 24.2 us  [swap(): return lax.all_to_all(x, axis, 0, 0, tiled=True)]
    all_to_all x3, blocking collectives: 48.9 us -> 50.7 us  [swap(): return lax.all_to_all(x, axis, 0, 0, tiled=True)]
    ppermute x4, waiting for transfers between devices: 6.52 us -> 4.72 us  [send_by(): lax.ppermute(value, axis, [(s, (s + steps) % count) for s in range(count)])]
  transfers between devices with their start and end apart: 6 -> 6, of which waited for: 4 -> 4; matrix products, arithmetic and copies ran while one was open for 1% -> 1% of each run, Pallas kernels for 5% -> 4%
where the time goes in v8:
time: 169 us; the launch traced here: 168 us
  Pallas kernels  53.9 us (32%)
  blocking collectives  50.7 us (30%)
  starting transfers between devices  31.5 us (19%)
  waiting for transfers between devices  28.9 us (17%)
  local copies, waits for them, and re-layouts  2.04 us (1%)
    all_to_all x3, blocking collectives, swap(): return lax.all_to_all(x, axis, 0, 0, tiled=True)  50.7 us
    pallas_call x1, Pallas kernels, local(): pl.pallas_call(solve_kernel, out_shape=jax.ShapeDtypeStruct(flat_rows.sha...  44.7 us
    all_to_all x2, waiting for transfers between devices, swap(): return lax.all_to_all(x, axis, 0, 0, tiled=True)  24.2 us
    all_to_all x2, starting transfers between devices, swap(): return lax.all_to_all(x, axis, 0, 0, tiled=True)  16.1 us
    ppermute x4, starting transfers between devices, send_by(): lax.ppermute(value, axis, [(s, (s + steps) % count) for s in range(count)])  15.4 us
    ppermute x4, waiting for transfers between devices, send_by(): lax.ppermute(value, axis, [(s, (s + steps) % count) for s in range(count)])  4.72 us
  transfers between devices with their start and end apart: 6, of which 4 were waited for; matrix products, arithmetic and copies ran while one was open for 1% of the time, Pallas kernels for 4%

profile of v8, /device:TPU:1, one launch (start us, length us, event | category | flops | bytes accessed | tf_op | source)
XLA Modules:
  0.0 168.1 jit_solution(15208254585904242312)
XLA Ops:
  0.0 0.0 copy-start.2
  0.0 0.0 copy-start
  0.0 12.0 %all-to-all-start = ((bf16[160,32,128]{2,1,0:T(8,128)(2,1)}), bf16[160,32,128]{2,1,0:T(8,128)(2,1)S(1)}, u32[]{:S(2)}, u32[]{:S(2)}) async-start(bf16[160,32,128]{2,1,0:T(8,128)(2,1)} %param.10), calls=%async_computation | async-start | bytes 2621440 | tf_op jit(solution)/shard_map/all_to_all | solution.py:256
  12.0 0.0 copy-done.2
  12.0 0.0 copy-start.3
  12.0 0.0 copy-start.1
  12.0 0.1 reshape.18.pick
  12.1 0.0 copy-done
  12.1 1.6 pick.1
  13.7 7.6 %collective-permute-start = (bf16[40,8,256]{2,1,0:T(8,128)(2,1)}, bf16[40,8,256]{2,1,0:T(8,128)(2,1)S(1)}, u32[]{:S(2)}, u32[]{:S(2)}) collective-permute-start(bf16[40,8,256]{2,1,0:T(8,128)(2,1)} %get-tuple-element.12), channel_id=1, source_target_pairs={{0,480},{16,496},{32,0},{48,16},{64,32},{80,48},{96,64},{112,80},{... | collective-permute-start | bytes 491528 | tf_op jit(solution)/shard_map/ppermute | solution.py:252
  21.3 2.8 %collective-permute-start.1 = (bf16[40,8,256]{2,1,0:T(8,128)(2,1)S(1)}, bf16[40,8,256]{2,1,0:T(8,128)(2,1)S(1)}, u32[]{:S(2)}, u32[]{:S(2)}) collective-permute-start(bf16[40,8,256]{2,1,0:T(8,128)(2,1)S(1)} %get-tuple-element.13), channel_id=1, source_target_pairs={{0,496},{16,0},{32,16},{48,32},{64,48},{80,64},{96,80},{112,96},{1... | collective-permute-start | bytes 491528 | tf_op jit(solution)/shard_map/ppermute | solution.py:252
  24.0 2.5 %collective-permute-start.2 = (bf16[40,8,256]{2,1,0:T(8,128)(2,1)S(1)}, bf16[40,8,256]{2,1,0:T(8,128)(2,1)S(1)}, u32[]{:S(2)}, u32[]{:S(2)}) collective-permute-start(bf16[40,8,256]{2,1,0:T(8,128)(2,1)S(1)} %get-tuple-element.15), channel_id=1, source_target_pairs={{0,16},{16,32},{32,48},{48,64},{64,80},{80,96},{96,112},{112,128},... | collective-permute-start | bytes 491528 | tf_op jit(solution)/shard_map/ppermute | solution.py:252
  26.6 2.6 %collective-permute-start.3 = (bf16[40,8,256]{2,1,0:T(8,128)(2,1)S(1)}, bf16[40,8,256]{2,1,0:T(8,128)(2,1)S(1)}, u32[]{:S(2)}, u32[]{:S(2)}) collective-permute-start(bf16[40,8,256]{2,1,0:T(8,128)(2,1)S(1)} %get-tuple-element.16), channel_id=1, source_target_pairs={{0,32},{16,48},{32,64},{48,80},{64,96},{80,112},{96,128},{112,144}... | collective-permute-start | bytes 491528 | tf_op jit(solution)/shard_map/ppermute | solution.py:252
  29.8 0.0 copy-done.3
  29.8 0.1 reshape.19.scales
  29.9 0.9 copy.13.innovation
  30.7 0.1 pad_add_fusion.place
  30.8 1.0 copy.15.vectors
  31.8 0.8 misfit.1.misfits
  32.6 0.0 collective-permute-done.a0
  32.6 0.0 collective-permute-done.1.a1
  32.6 1.7 %collective-permute-done.2.a3 = bf16[40,8,256]{2,1,0:T(8,128)(2,1)S(1)} collective-permute-done((bf16[40,8,256]{2,1,0:T(8,128)(2,1)S(1)}, bf16[40,8,256]{2,1,0:T(8,128)(2,1)S(1)}, u32[]{:S(2)}, u32[]{:S(2)}) %collective-permute-start.2) | collective-permute-done | bytes 163872 | tf_op jit(solution)/shard_map/ppermute | solution.py:252
  34.4 3.0 %collective-permute-done.3.a4 = bf16[40,8,256]{2,1,0:T(8,128)(2,1)S(1)} collective-permute-done((bf16[40,8,256]{2,1,0:T(8,128)(2,1)S(1)}, bf16[40,8,256]{2,1,0:T(8,128)(2,1)S(1)}, u32[]{:S(2)}, u32[]{:S(2)}) %collective-permute-start.3) | collective-permute-done | bytes 163872 | tf_op jit(solution)/shard_map/ppermute | solution.py:252
  37.4 0.0 copy-done.1
  37.4 1.7 %slots.1 = bf16[336,8,128]{2,1,0:T(8,128)(2,1)} custom-call(s32[160]{0:T(256)S(1)} %copy-done.1, bf16[40,8,256]{2,1,0:T(8,128)(2,1)S(1)} %collective-permute-done.a0, bf16[40,8,256]{2,1,0:T(8,128)(2,1)S(1)} %collective-permute-done.1.a1, bf16[40,8,256]{2,1,0:T(8,128)(2,1)S(1)} %get-tuple-element.14.a2, bf16[40,8,256]{2,1,0:T(8,128)(2,1)S(1)} %collective-permute-done.2.a3, ...), custom_call_target="tpu_custom_call" | custom-call | bytes 1310720 | tf_op jit(solution)/shard_map/slots/pallas_call | solution.py:315
  39.1 6.1 %all-to-all-done.jacobian = bf16[160,32,128]{2,1,0:T(8,128)(2,1)S(1)} async-done(((bf16[160,32,128]{2,1,0:T(8,128)(2,1)}), bf16[160,32,128]{2,1,0:T(8,128)(2,1)S(1)}, u32[]{:S(2)}, u32[]{:S(2)}) %all-to-all-start) | async-done | bytes 1310752 | tf_op jit(solution)/shard_map/all_to_all | solution.py:256
  45.2 4.2 %all-to-all-start.1 = ((bf16[336,8,128]{2,1,0:T(8,128)(2,1)}), bf16[336,8,128]{2,1,0:T(8,128)(2,1)}, u32[]{:S(2)}, u32[]{:S(2)}) async-start(bf16[336,8,128]{2,1,0:T(8,128)(2,1)} %slots.1), calls=%async_computation.1 | async-start | bytes 1376256 | tf_op jit(solution)/shard_map/all_to_all | solution.py:256
  49.4 2.3 %turn.1.turned = bf16[10,512,128]{2,1,0:T(8,128)(2,1)S(1)} custom-call(s32[2]{0:T(128)S(1)} %pad_add_fusion.place, f32[512,32]{1,0:T(8,128)S(1)} %copy.15.vectors, f32[2,256]{1,0:T(2,128)S(1)} %reshape.17.scales, bf16[160,32,128]{2,1,0:T(8,128)(2,1)S(1)} %all-to-all-done.jacobian), custom_call_target="tpu_custom_call" | custom-call | flops 671088640 | bytes 2621440 | tf_op jit(solution)/shard_map/turn/pallas_call | solution.py:328
  51.7 18.1 %all-to-all-done.1.arrived = bf16[336,8,128]{2,1,0:T(8,128)(2,1)} async-done(((bf16[336,8,128]{2,1,0:T(8,128)(2,1)}), bf16[336,8,128]{2,1,0:T(8,128)(2,1)}, u32[]{:S(2)}, u32[]{:S(2)}) %all-to-all-start.1) | async-done | bytes 688160 | tf_op jit(solution)/shard_map/all_to_all | solution.py:256
  69.8 2.7 %terms.1 = f32[64,8,128]{2,1,0:T(8,128)S(1)} custom-call(bf16[10,512,128]{2,1,0:T(8,128)(2,1)S(1)} %turn.1.turned, bf16[336,8,128]{2,1,0:T(8,128)(2,1)} %all-to-all-done.1.arrived), custom_call_target="tpu_custom_call" | custom-call | flops 1006632960 | bytes 1310720 | tf_op jit(solution)/shard_map/terms/pallas_call | solution.py:338
  72.5 17.9 %all_to_all.25 = f32[64,8,128]{2,1,0:T(8,128)S(1)} all-to-all(f32[64,8,128]{2,1,0:T(8,128)S(1)} %terms.1), channel_id=1, replica_groups=mesh['y'=8,'x'=4,'z'=8,'c'=2] {'x','z','c'}, dimensions={0} | all-to-all | bytes 524288 | tf_op jit(solution)/shard_map/all_to_all | solution.py:256
  90.4 0.1 reduce_sum.18
  90.5 13.5 %all_to_all.26 = f32[8,8,128]{2,1,0:T(8,128)S(1)} all-to-all(f32[8,8,128]{2,1,0:T(8,128)S(1)} %broadcast_in_dim.7), channel_id=1, replica_groups=mesh['y'=8,'x'=4,'z'=8,'c'=2] {'y'}, dimensions={0} | all-to-all | bytes 65536 | tf_op jit(solution)/shard_map/all_to_all | solution.py:256
  104.0 19.4 %all_to_all.27.summed = f32[64,8,128]{2,1,0:T(8,128)} all-to-all(f32[64,8,128]{2,1,0:T(8,128)S(1)} %broadcast_in_dim.8), channel_id=1, replica_groups=mesh['y'=8,'x'=4,'z'=8,'c'=2] {'x','z','c'}, dimensions={0} | all-to-all | bytes 524288 | tf_op jit(solution)/shard_map/all_to_all | solution.py:256
  123.4 44.7 %solve.1 = bf16[3072,256]{1,0:T(8,128)(2,1)} custom-call(f32[64,8,128]{2,1,0:T(8,128)} %all_to_all.27.summed, f32[256,256]{1,0:T(8,128)} %basis.1, bf16[3072,256]{1,0:T(8,128)(2,1)} %bitcast.3), custom_call_target="tpu_custom_call" | custom-call | tf_op jit(solution)/shard_map/solve/pallas_call | solution.py:352
  (6 shorter events, 0.1 us)
Async XLA Ops:
  0.0 12.0 %copy-start.2 = (s32[1,5,40]{2,0,1:T(1,128)S(1)}, s32[1,5,40]{2,0,1:T(1,128)}, u32[]{:S(2)}) copy-start(s32[1,5,40]{2,0,1:T(1,128)} %param.15) | copy-start | bytes 2404
  0.0 12.1 %copy-start = (bf16[384,8,256]{2,1,0:T(8,128)(2,1)S(1)}, bf16[384,8,256]{2,1,0:T(8,128)(2,1)}, u32[]{:S(2)}) copy-start(bf16[384,8,256]{2,1,0:T(8,128)(2,1)} %ensemble.1) | copy-start | bytes 4718596
  0.0 45.2 %all-to-all-start = ((bf16[160,32,128]{2,1,0:T(8,128)(2,1)}), bf16[160,32,128]{2,1,0:T(8,128)(2,1)S(1)}, u32[]{:S(2)}, u32[]{:S(2)}) async-start(bf16[160,32,128]{2,1,0:T(8,128)(2,1)} %param.10), calls=%async_computation | async-start | bytes 2621440 | tf_op jit(solution)/shard_map/all_to_all | solution.py:256
  12.0 17.8 %copy-start.3 = (f32[512]{0:T(512)S(1)}, f32[512]{0:T(512)}, u32[]{:S(2)}) copy-start(f32[512]{0:T(512)} %param.13) | copy-start | bytes 6148
  12.0 25.4 %copy-start.1 = (s32[160]{0:T(256)S(1)}, s32[160]{0:T(256)}, u32[]{:S(2)}) copy-start(s32[160]{0:T(256)} %slot.1) | copy-start | bytes 1924
  13.7 18.9 %collective-permute-start = (bf16[40,8,256]{2,1,0:T(8,128)(2,1)}, bf16[40,8,256]{2,1,0:T(8,128)(2,1)S(1)}, u32[]{:S(2)}, u32[]{:S(2)}) collective-permute-start(bf16[40,8,256]{2,1,0:T(8,128)(2,1)} %get-tuple-element.12), channel_id=1, source_target_pairs={{0,480},{16,496},{32,0},{48,16},{64,32},{80,48},{96,64},{112,80},{... | collective-permute-start | bytes 491528 | tf_op jit(solution)/shard_map/ppermute | solution.py:252
  21.3 11.4 %collective-permute-start.1 = (bf16[40,8,256]{2,1,0:T(8,128)(2,1)S(1)}, bf16[40,8,256]{2,1,0:T(8,128)(2,1)S(1)}, u32[]{:S(2)}, u32[]{:S(2)}) collective-permute-start(bf16[40,8,256]{2,1,0:T(8,128)(2,1)S(1)} %get-tuple-element.13), channel_id=1, source_target_pairs={{0,496},{16,0},{32,16},{48,32},{64,48},{80,64},{96,80},{112,96},{1... | collective-permute-start | bytes 491528 | tf_op jit(solution)/shard_map/ppermute | solution.py:252
  24.0 10.3 %collective-permute-start.2 = (bf16[40,8,256]{2,1,0:T(8,128)(2,1)S(1)}, bf16[40,8,256]{2,1,0:T(8,128)(2,1)S(1)}, u32[]{:S(2)}, u32[]{:S(2)}) collective-permute-start(bf16[40,8,256]{2,1,0:T(8,128)(2,1)S(1)} %get-tuple-element.15), channel_id=1, source_target_pairs={{0,16},{16,32},{32,48},{48,64},{64,80},{80,96},{96,112},{112,128},... | collective-permute-start | bytes 491528 | tf_op jit(solution)/shard_map/ppermute | solution.py:252
  26.6 10.8 %collective-permute-start.3 = (bf16[40,8,256]{2,1,0:T(8,128)(2,1)S(1)}, bf16[40,8,256]{2,1,0:T(8,128)(2,1)S(1)}, u32[]{:S(2)}, u32[]{:S(2)}) collective-permute-start(bf16[40,8,256]{2,1,0:T(8,128)(2,1)S(1)} %get-tuple-element.16), channel_id=1, source_target_pairs={{0,32},{16,48},{32,64},{48,80},{64,96},{80,112},{96,128},{112,144}... | collective-permute-start | bytes 491528 | tf_op jit(solution)/shard_map/ppermute | solution.py:252
  45.2 24.6 %all-to-all-start.1 = ((bf16[336,8,128]{2,1,0:T(8,128)(2,1)}), bf16[336,8,128]{2,1,0:T(8,128)(2,1)}, u32[]{:S(2)}, u32[]{:S(2)}) async-start(bf16[336,8,128]{2,1,0:T(8,128)(2,1)} %slots.1), calls=%async_computation.1 | async-start | bytes 1376256 | tf_op jit(solution)/shard_map/all_to_all | solution.py:256

commit v9 on v8

--- a/solution.py
+++ b/solution.py
@@ -363,7 +363,7 @@
             pltpu.SemaphoreType.DMA,
             pltpu.SemaphoreType.DMA((chunks,)),
         ],
-        compiler_params=grant(57),
+        compiler_params=grant(53),
         name="solve",
     )(summed, ensemble_vectors, flat_rows)
     return updated.reshape(ensemble.shape)

time: 169 us -> 168 us (level)
  no operation moved by 1% of the time
where the time goes in v9:
time: 168 us; the launch traced here: 167 us
  Pallas kernels  52.8 us (31%)
  blocking collectives  50.8 us (30%)
  starting transfers between devices  31.5 us (19%)
  waiting for transfers between devices  28.9 us (17%)
  local copies, waits for them, and re-layouts  2.04 us (1%)
    all_to_all x3, blocking collectives, swap(): return lax.all_to_all(x, axis, 0, 0, tiled=True)  50.8 us
    pallas_call x1, Pallas kernels, local(): pl.pallas_call(solve_kernel, out_shape=jax.ShapeDtypeStruct(flat_rows.sha...  43.6 us
    all_to_all x2, waiting for transfers between devices, swap(): return lax.all_to_all(x, axis, 0, 0, tiled=True)  24.2 us
    all_to_all x2, starting transfers between devices, swap(): return lax.all_to_all(x, axis, 0, 0, tiled=True)  16.1 us
    ppermute x4, starting transfers between devices, send_by(): lax.ppermute(value, axis, [(s, (s + steps) % count) for s in range(count)])  15.4 us
    ppermute x4, waiting for transfers between devices, send_by(): lax.ppermute(value, axis, [(s, (s + steps) % count) for s in range(count)])  4.72 us
  transfers between devices with their start and end apart: 6, of which 4 were waited for; matrix products, arithmetic and copies ran while one was open for 1% of the time, Pallas kernels for 4%

profile of v9, /device:TPU:1, one launch (start us, length us, event | category | flops | bytes accessed | tf_op | source)
XLA Modules:
  0.0 167.1 jit_solution(15304994692399891965)
XLA Ops:
  0.0 0.0 copy-start.3
  0.0 0.0 copy-start
  0.0 12.0 %all-to-all-start = ((bf16[160,32,128]{2,1,0:T(8,128)(2,1)}), bf16[160,32,128]{2,1,0:T(8,128)(2,1)S(1)}, u32[]{:S(2)}, u32[]{:S(2)}) async-start(bf16[160,32,128]{2,1,0:T(8,128)(2,1)} %param.10), calls=%async_computation | async-start | bytes 2621440 | tf_op jit(solution)/shard_map/all_to_all | solution.py:256
  12.0 0.0 copy-done.3
  12.0 0.0 copy-start.4
  12.0 0.0 copy-start.2
  12.0 0.1 reshape.18.pick
  12.1 0.0 copy-done
  12.1 1.6 pick.1
  13.7 7.6 %collective-permute-start = (bf16[40,8,256]{2,1,0:T(8,128)(2,1)}, bf16[40,8,256]{2,1,0:T(8,128)(2,1)S(1)}, u32[]{:S(2)}, u32[]{:S(2)}) collective-permute-start(bf16[40,8,256]{2,1,0:T(8,128)(2,1)} %get-tuple-element.12), channel_id=1, source_target_pairs={{0,480},{16,496},{32,0},{48,16},{64,32},{80,48},{96,64},{112,80},{... | collective-permute-start | bytes 491528 | tf_op jit(solution)/shard_map/ppermute | solution.py:252
  21.3 2.8 %collective-permute-start.1 = (bf16[40,8,256]{2,1,0:T(8,128)(2,1)S(1)}, bf16[40,8,256]{2,1,0:T(8,128)(2,1)S(1)}, u32[]{:S(2)}, u32[]{:S(2)}) collective-permute-start(bf16[40,8,256]{2,1,0:T(8,128)(2,1)S(1)} %get-tuple-element.13), channel_id=1, source_target_pairs={{0,496},{16,0},{32,16},{48,32},{64,48},{80,64},{96,80},{112,96},{1... | collective-permute-start | bytes 491528 | tf_op jit(solution)/shard_map/ppermute | solution.py:252
  24.0 2.5 %collective-permute-start.2 = (bf16[40,8,256]{2,1,0:T(8,128)(2,1)S(1)}, bf16[40,8,256]{2,1,0:T(8,128)(2,1)S(1)}, u32[]{:S(2)}, u32[]{:S(2)}) collective-permute-start(bf16[40,8,256]{2,1,0:T(8,128)(2,1)S(1)} %get-tuple-element.15), channel_id=1, source_target_pairs={{0,16},{16,32},{32,48},{48,64},{64,80},{80,96},{96,112},{112,128},... | collective-permute-start | bytes 491528 | tf_op jit(solution)/shard_map/ppermute | solution.py:252
  26.6 2.6 %collective-permute-start.3 = (bf16[40,8,256]{2,1,0:T(8,128)(2,1)S(1)}, bf16[40,8,256]{2,1,0:T(8,128)(2,1)S(1)}, u32[]{:S(2)}, u32[]{:S(2)}) collective-permute-start(bf16[40,8,256]{2,1,0:T(8,128)(2,1)S(1)} %get-tuple-element.16), channel_id=1, source_target_pairs={{0,32},{16,48},{32,64},{48,80},{64,96},{80,112},{96,128},{112,144}... | collective-permute-start | bytes 491528 | tf_op jit(solution)/shard_map/ppermute | solution.py:252
  29.8 0.0 copy-done.4
  29.8 0.1 reshape.19.scales
  29.9 0.9 copy.13.innovation
  30.7 0.1 pad_add_fusion.place
  30.8 1.0 copy.15.vectors
  31.8 0.8 misfit.1.misfits
  32.6 0.0 collective-permute-done.a0
  32.6 0.0 collective-permute-done.1.a1
  32.6 1.7 %collective-permute-done.2.a3 = bf16[40,8,256]{2,1,0:T(8,128)(2,1)S(1)} collective-permute-done((bf16[40,8,256]{2,1,0:T(8,128)(2,1)S(1)}, bf16[40,8,256]{2,1,0:T(8,128)(2,1)S(1)}, u32[]{:S(2)}, u32[]{:S(2)}) %collective-permute-start.2) | collective-permute-done | bytes 163872 | tf_op jit(solution)/shard_map/ppermute | solution.py:252
  34.4 3.0 %collective-permute-done.3.a4 = bf16[40,8,256]{2,1,0:T(8,128)(2,1)S(1)} collective-permute-done((bf16[40,8,256]{2,1,0:T(8,128)(2,1)S(1)}, bf16[40,8,256]{2,1,0:T(8,128)(2,1)S(1)}, u32[]{:S(2)}, u32[]{:S(2)}) %collective-permute-start.3) | collective-permute-done | bytes 163872 | tf_op jit(solution)/shard_map/ppermute | solution.py:252
  37.4 0.0 copy-done.2
  37.4 1.7 %slots.1 = bf16[336,8,128]{2,1,0:T(8,128)(2,1)} custom-call(s32[160]{0:T(256)S(1)} %copy-done.2, bf16[40,8,256]{2,1,0:T(8,128)(2,1)S(1)} %collective-permute-done.a0, bf16[40,8,256]{2,1,0:T(8,128)(2,1)S(1)} %collective-permute-done.1.a1, bf16[40,8,256]{2,1,0:T(8,128)(2,1)S(1)} %get-tuple-element.14.a2, bf16[40,8,256]{2,1,0:T(8,128)(2,1)S(1)} %collective-permute-done.2.a3, ...), custom_call_target="tpu_custom_call" | custom-call | bytes 1310720 | tf_op jit(solution)/shard_map/slots/pallas_call | solution.py:315
  39.1 6.1 %all-to-all-done.jacobian = bf16[160,32,128]{2,1,0:T(8,128)(2,1)S(1)} async-done(((bf16[160,32,128]{2,1,0:T(8,128)(2,1)}), bf16[160,32,128]{2,1,0:T(8,128)(2,1)S(1)}, u32[]{:S(2)}, u32[]{:S(2)}) %all-to-all-start) | async-done | bytes 1310752 | tf_op jit(solution)/shard_map/all_to_all | solution.py:256
  45.2 4.2 %all-to-all-start.1 = ((bf16[336,8,128]{2,1,0:T(8,128)(2,1)}), bf16[336,8,128]{2,1,0:T(8,128)(2,1)}, u32[]{:S(2)}, u32[]{:S(2)}) async-start(bf16[336,8,128]{2,1,0:T(8,128)(2,1)} %slots.1), calls=%async_computation.1 | async-start | bytes 1376256 | tf_op jit(solution)/shard_map/all_to_all | solution.py:256
  49.4 2.3 %turn.1.turned = bf16[10,512,128]{2,1,0:T(8,128)(2,1)S(1)} custom-call(s32[2]{0:T(128)S(1)} %pad_add_fusion.place, f32[512,32]{1,0:T(8,128)S(1)} %copy.15.vectors, f32[2,256]{1,0:T(2,128)S(1)} %reshape.17.scales, bf16[160,32,128]{2,1,0:T(8,128)(2,1)S(1)} %all-to-all-done.jacobian), custom_call_target="tpu_custom_call" | custom-call | flops 671088640 | bytes 2621440 | tf_op jit(solution)/shard_map/turn/pallas_call | solution.py:328
  51.7 18.1 %all-to-all-done.1.arrived = bf16[336,8,128]{2,1,0:T(8,128)(2,1)} async-done(((bf16[336,8,128]{2,1,0:T(8,128)(2,1)}), bf16[336,8,128]{2,1,0:T(8,128)(2,1)}, u32[]{:S(2)}, u32[]{:S(2)}) %all-to-all-start.1) | async-done | bytes 688160 | tf_op jit(solution)/shard_map/all_to_all | solution.py:256
  69.8 2.7 %terms.1 = f32[64,8,128]{2,1,0:T(8,128)S(1)} custom-call(bf16[10,512,128]{2,1,0:T(8,128)(2,1)S(1)} %turn.1.turned, bf16[336,8,128]{2,1,0:T(8,128)(2,1)} %all-to-all-done.1.arrived), custom_call_target="tpu_custom_call" | custom-call | flops 1006632960 | bytes 1310720 | tf_op jit(solution)/shard_map/terms/pallas_call | solution.py:338
  72.5 0.0 copy-start.1
  72.6 18.0 %all_to_all.25 = f32[64,8,128]{2,1,0:T(8,128)S(1)} all-to-all(f32[64,8,128]{2,1,0:T(8,128)S(1)} %terms.1), channel_id=1, replica_groups=mesh['y'=8,'x'=4,'z'=8,'c'=2] {'x','z','c'}, dimensions={0} | all-to-all | bytes 524288 | tf_op jit(solution)/shard_map/all_to_all | solution.py:256
  90.6 0.1 reduce_sum.18
  90.6 13.5 %all_to_all.26 = f32[8,8,128]{2,1,0:T(8,128)S(1)} all-to-all(f32[8,8,128]{2,1,0:T(8,128)S(1)} %broadcast_in_dim.7), channel_id=1, replica_groups=mesh['y'=8,'x'=4,'z'=8,'c'=2] {'y'}, dimensions={0} | all-to-all | bytes 65536 | tf_op jit(solution)/shard_map/all_to_all | solution.py:256
  104.2 19.3 %all_to_all.27.summed = f32[64,8,128]{2,1,0:T(8,128)S(1)} all-to-all(f32[64,8,128]{2,1,0:T(8,128)S(1)} %broadcast_in_dim.8), channel_id=1, replica_groups=mesh['y'=8,'x'=4,'z'=8,'c'=2] {'x','z','c'}, dimensions={0} | all-to-all | bytes 524288 | tf_op jit(solution)/shard_map/all_to_all | solution.py:256
  123.4 0.0 copy-done.1
  123.4 43.6 %solve.1 = bf16[3072,256]{1,0:T(8,128)(2,1)} custom-call(f32[64,8,128]{2,1,0:T(8,128)S(1)} %all_to_all.27.summed, f32[256,256]{1,0:T(8,128)S(1)} %copy-done.1, bf16[3072,256]{1,0:T(8,128)(2,1)} %bitcast.3), custom_call_target="tpu_custom_call" | custom-call | tf_op jit(solution)/shard_map/solve/pallas_call | solution.py:352
  (6 shorter events, 0.1 us)
Async XLA Ops:
  0.0 12.0 %copy-start.3 = (s32[1,5,40]{2,0,1:T(1,128)S(1)}, s32[1,5,40]{2,0,1:T(1,128)}, u32[]{:S(2)}) copy-start(s32[1,5,40]{2,0,1:T(1,128)} %param.15) | copy-start | bytes 2404
  0.0 12.1 %copy-start = (bf16[384,8,256]{2,1,0:T(8,128)(2,1)S(1)}, bf16[384,8,256]{2,1,0:T(8,128)(2,1)}, u32[]{:S(2)}) copy-start(bf16[384,8,256]{2,1,0:T(8,128)(2,1)} %ensemble.1) | copy-start | bytes 4718596
  0.0 45.2 %all-to-all-start = ((bf16[160,32,128]{2,1,0:T(8,128)(2,1)}), bf16[160,32,128]{2,1,0:T(8,128)(2,1)S(1)}, u32[]{:S(2)}, u32[]{:S(2)}) async-start(bf16[160,32,128]{2,1,0:T(8,128)(2,1)} %param.10), calls=%async_computation | async-start | bytes 2621440 | tf_op jit(solution)/shard_map/all_to_all | solution.py:256
  12.0 17.8 %copy-start.4 = (f32[512]{0:T(512)S(1)}, f32[512]{0:T(512)}, u32[]{:S(2)}) copy-start(f32[512]{0:T(512)} %param.13) | copy-start | bytes 6148
  12.0 25.4 %copy-start.2 = (s32[160]{0:T(256)S(1)}, s32[160]{0:T(256)}, u32[]{:S(2)}) copy-start(s32[160]{0:T(256)} %slot.1) | copy-start | bytes 1924
  13.7 18.9 %collective-permute-start = (bf16[40,8,256]{2,1,0:T(8,128)(2,1)}, bf16[40,8,256]{2,1,0:T(8,128)(2,1)S(1)}, u32[]{:S(2)}, u32[]{:S(2)}) collective-permute-start(bf16[40,8,256]{2,1,0:T(8,128)(2,1)} %get-tuple-element.12), channel_id=1, source_target_pairs={{0,480},{16,496},{32,0},{48,16},{64,32},{80,48},{96,64},{112,80},{... | collective-permute-start | bytes 491528 | tf_op jit(solution)/shard_map/ppermute | solution.py:252
  21.3 11.4 %collective-permute-start.1 = (bf16[40,8,256]{2,1,0:T(8,128)(2,1)S(1)}, bf16[40,8,256]{2,1,0:T(8,128)(2,1)S(1)}, u32[]{:S(2)}, u32[]{:S(2)}) collective-permute-start(bf16[40,8,256]{2,1,0:T(8,128)(2,1)S(1)} %get-tuple-element.13), channel_id=1, source_target_pairs={{0,496},{16,0},{32,16},{48,32},{64,48},{80,64},{96,80},{112,96},{1... | collective-permute-start | bytes 491528 | tf_op jit(solution)/shard_map/ppermute | solution.py:252
  24.0 10.3 %collective-permute-start.2 = (bf16[40,8,256]{2,1,0:T(8,128)(2,1)S(1)}, bf16[40,8,256]{2,1,0:T(8,128)(2,1)S(1)}, u32[]{:S(2)}, u32[]{:S(2)}) collective-permute-start(bf16[40,8,256]{2,1,0:T(8,128)(2,1)S(1)} %get-tuple-element.15), channel_id=1, source_target_pairs={{0,16},{16,32},{32,48},{48,64},{64,80},{80,96},{96,112},{112,128},... | collective-permute-start | bytes 491528 | tf_op jit(solution)/shard_map/ppermute | solution.py:252
  26.6 10.8 %collective-permute-start.3 = (bf16[40,8,256]{2,1,0:T(8,128)(2,1)S(1)}, bf16[40,8,256]{2,1,0:T(8,128)(2,1)S(1)}, u32[]{:S(2)}, u32[]{:S(2)}) collective-permute-start(bf16[40,8,256]{2,1,0:T(8,128)(2,1)S(1)} %get-tuple-element.16), channel_id=1, source_target_pairs={{0,32},{16,48},{32,64},{48,80},{64,96},{80,112},{96,128},{112,144}... | collective-permute-start | bytes 491528 | tf_op jit(solution)/shard_map/ppermute | solution.py:252
  45.2 24.6 %all-to-all-start.1 = ((bf16[336,8,128]{2,1,0:T(8,128)(2,1)}), bf16[336,8,128]{2,1,0:T(8,128)(2,1)}, u32[]{:S(2)}, u32[]{:S(2)}) async-start(bf16[336,8,128]{2,1,0:T(8,128)(2,1)} %slots.1), calls=%async_computation.1 | async-start | bytes 1376256 | tf_op jit(solution)/shard_map/all_to_all | solution.py:256
  72.5 50.9 %copy-start.1 = (f32[256,256]{1,0:T(8,128)S(1)}, f32[256,256]{1,0:T(8,128)}, u32[]{:S(2)}) copy-start(f32[256,256]{1,0:T(8,128)} %basis.1) | copy-start | bytes 786436

commit v10 on v9

--- a/solution.py
+++ b/solution.py
@@ -11,6 +11,7 @@
 NEAR = ("x", "z", "c")
 FAR = "y"
 MEM = 256
+CHUNK = 7
 HI = lax.Precision.HIGHEST
 F32 = jnp.float32
 BF16 = jnp.bfloat16
@@ -146,15 +147,33 @@
             lefts.append(jnp.concatenate([whitened, rows], axis=0))
         gram = gram + nt(jnp.concatenate(lefts, axis=1), jnp.concatenate(rights, axis=1))
     pull = gram[MEM : MEM + 16, :]
-    out[0:16] = gram[0:128, 0:128].reshape(16, 8, 128)
-    out[16:32] = gram[128:256, 0:128].reshape(16, 8, 128)
-    out[32:48] = gram[128:256, 128:256].reshape(16, 8, 128)
     total = jnp.sum(pull, axis=0, keepdims=True)
-    last = jnp.concatenate(
-        [total[:, 0:128], total[:, 128:256], jnp.zeros((6, 128), F32)], axis=0
-    )
-    out[48:64] = jnp.zeros((16, 8, 128), F32)
-    out[48] = last
+    out[0:128, :] = gram[0:128, 0:128]
+    out[128:256, :] = gram[128:256, 0:128]
+    out[256:384, :] = gram[128:256, 128:256]
+    unused = jnp.zeros((out.shape[0] - 386, 128), F32)
+    out[384:, :] = jnp.concatenate([total[:, 0:128], total[:, 128:256], unused], axis=0)
+
+
+def near_sum_kernel(parts, out):
+    span = 8 * CHUNK
+    x = parts[0:span, :]
+    for k in range(1, parts.shape[0] // span):
+        x = x + parts[k * span : (k + 1) * span, :]
+    y = x[0:CHUNK, :]
+    for k in range(1, 8):
+        y = y + x[k * CHUNK : (k + 1) * CHUNK, :]
+    tile = jnp.concatenate([y, jnp.zeros((8 - CHUNK, 128), F32)], axis=0)
+    for k in range(out.shape[0]):
+        out[k] = tile
+
+
+def far_sum_kernel(parts, out):
+    y = jnp.sum(parts[...], axis=0)[0:CHUNK, :]
+    x = jnp.concatenate([y] * 8, axis=0)
+    span = 8 * CHUNK
+    for k in range(out.shape[0] // span):
+        out[k * span : (k + 1) * span, :] = x
 
 
 def lower_half(x):
@@ -182,9 +201,9 @@
     load = pltpu.make_async_copy(ensemble_far, ensemble, load_sem)
     load.start()
     eye = (iota2(MEM, MEM, 0) == iota2(MEM, MEM, 1)).astype(F32)
-    g00 = summed[0:16].reshape(128, 128)
-    g10 = summed[16:32].reshape(128, 128)
-    g11 = summed[32:48].reshape(128, 128)
+    g00 = summed[0:128, :]
+    g10 = summed[128:256, :]
+    g11 = summed[256:384, :]
     a = jnp.concatenate(
         [jnp.concatenate([g00, g10.T], axis=1), jnp.concatenate([g10, g11], axis=1)], axis=0
     ) + (MEM - 1.0) * eye
@@ -229,8 +248,7 @@
         inverse[...] = rows[:, MEM : 2 * MEM]
 
     x = inverse[...]
-    last = summed[48]
-    pull = jnp.concatenate([last[0:1, :], last[1:2, :]], axis=1)
+    pull = jnp.concatenate([summed[384:385, :], summed[385:386, :]], axis=1)
     halfway = jnp.sum(x * pull, axis=1, keepdims=True)
     target = (MEM - 1.0) ** 0.5 * basis[...] + halfway
     transform = nn3(x.T, target).astype(BF16)
@@ -256,11 +274,29 @@
     return lax.all_to_all(x, axis, 0, 0, tiled=True)
 
 
-def summed_everywhere(tiles):
-    mine = jnp.sum(swap(tiles, NEAR), axis=0, keepdims=True)
+def swap_rows(x, axis):
+    return swap(x.reshape(-1, 1, 128), axis).reshape(-1, 128)
+
+
+def summed_everywhere(rows):
     far = lax.axis_size(FAR)
-    mine = jnp.sum(swap(jnp.broadcast_to(mine, (far, 8, 128)), FAR), axis=0, keepdims=True)
-    return swap(jnp.broadcast_to(mine, (tiles.shape[0], 8, 128)), NEAR)
+    mine = pl.pallas_call(
+        near_sum_kernel,
+        out_shape=jax.ShapeDtypeStruct((far, 8, 128), F32),
+        in_specs=[VM],
+        out_specs=VM,
+        compiler_params=grant(20),
+        name="near_sum",
+    )(swap_rows(rows, NEAR))
+    mine = pl.pallas_call(
+        far_sum_kernel,
+        out_shape=jax.ShapeDtypeStruct(rows.shape, F32),
+        in_specs=[VM],
+        out_specs=VM,
+        compiler_params=grant(20),
+        name="far_sum",
+    )(swap(mine, FAR))
+    return swap_rows(mine, NEAR)
 
 
 def local(
@@ -337,7 +373,7 @@
 
     tiles = pl.pallas_call(
         terms_kernel,
-        out_shape=jax.ShapeDtypeStruct((64, 8, 128), F32),
+        out_shape=jax.ShapeDtypeStruct((64 * CHUNK, 128), F32),
         in_specs=[VM, VM],
         out_specs=VM,
         compiler_params=grant(20),

time: 168 us -> 166 us (0.988)
  no operation moved by 1% of the time
where the time goes in v10:
time: 166 us; the launch traced here: 165 us
  Pallas kernels  52.9 us (32%)
  blocking collectives  49.2 us (30%)
  starting transfers between devices  31.5 us (19%)
  waiting for transfers between devices  28.9 us (17%)
  local copies, waits for them, and re-layouts  2.01 us (1%)
    all_to_all x3, blocking collectives, swap(): return lax.all_to_all(x, axis, 0, 0, tiled=True)  49.2 us
    pallas_call x1, Pallas kernels, local(): pl.pallas_call(solve_kernel, out_shape=jax.ShapeDtypeStruct(flat_rows.sha...  43.6 us
    all_to_all x2, waiting for transfers between devices, swap(): return lax.all_to_all(x, axis, 0, 0, tiled=True)  24.2 us
    all_to_all x2, starting transfers between devices, swap(): return lax.all_to_all(x, axis, 0, 0, tiled=True)  16.1 us
    ppermute x4, starting transfers between devices, send_by(): lax.ppermute(value, axis, [(s, (s + steps) % count) for s in range(count)])  15.4 us
    ppermute x4, waiting for transfers between devices, send_by(): lax.ppermute(value, axis, [(s, (s + steps) % count) for s in range(count)])  4.72 us
  transfers between devices with their start and end apart: 6, of which 4 were waited for; matrix products, arithmetic and copies ran while one was open for 1% of the time, Pallas kernels for 4%

profile of v10, /device:TPU:1, one launch (start us, length us, event | category | flops | bytes accessed | tf_op | source)
XLA Modules:
  0.0 165.4 jit_solution(11294070468533061590)
XLA Ops:
  0.0 0.0 copy-start.3
  0.0 0.0 copy-start
  0.0 12.0 %all-to-all-start = ((bf16[160,32,128]{2,1,0:T(8,128)(2,1)}), bf16[160,32,128]{2,1,0:T(8,128)(2,1)S(1)}, u32[]{:S(2)}, u32[]{:S(2)}) async-start(bf16[160,32,128]{2,1,0:T(8,128)(2,1)} %param.10), calls=%async_computation | async-start | bytes 2621440 | tf_op jit(solution)/shard_map/all_to_all | solution.py:274
  12.0 0.0 copy-done.3
  12.0 0.0 copy-start.4
  12.0 0.0 copy-start.2
  12.0 0.1 reshape.28.pick
  12.1 0.0 copy-done
  12.1 1.6 pick.1
  13.7 7.6 %collective-permute-start = (bf16[40,8,256]{2,1,0:T(8,128)(2,1)}, bf16[40,8,256]{2,1,0:T(8,128)(2,1)S(1)}, u32[]{:S(2)}, u32[]{:S(2)}) collective-permute-start(bf16[40,8,256]{2,1,0:T(8,128)(2,1)} %get-tuple-element.12), channel_id=1, source_target_pairs={{0,480},{16,496},{32,0},{48,16},{64,32},{80,48},{96,64},{112,80},{... | collective-permute-start | bytes 491528 | tf_op jit(solution)/shard_map/ppermute | solution.py:270
  21.3 2.8 %collective-permute-start.1 = (bf16[40,8,256]{2,1,0:T(8,128)(2,1)S(1)}, bf16[40,8,256]{2,1,0:T(8,128)(2,1)S(1)}, u32[]{:S(2)}, u32[]{:S(2)}) collective-permute-start(bf16[40,8,256]{2,1,0:T(8,128)(2,1)S(1)} %get-tuple-element.13), channel_id=1, source_target_pairs={{0,496},{16,0},{32,16},{48,32},{64,48},{80,64},{96,80},{112,96},{1... | collective-permute-start | bytes 491528 | tf_op jit(solution)/shard_map/ppermute | solution.py:270
  24.0 2.5 %collective-permute-start.2 = (bf16[40,8,256]{2,1,0:T(8,128)(2,1)S(1)}, bf16[40,8,256]{2,1,0:T(8,128)(2,1)S(1)}, u32[]{:S(2)}, u32[]{:S(2)}) collective-permute-start(bf16[40,8,256]{2,1,0:T(8,128)(2,1)S(1)} %get-tuple-element.15), channel_id=1, source_target_pairs={{0,16},{16,32},{32,48},{48,64},{64,80},{80,96},{96,112},{112,128},... | collective-permute-start | bytes 491528 | tf_op jit(solution)/shard_map/ppermute | solution.py:270
  26.6 2.6 %collective-permute-start.3 = (bf16[40,8,256]{2,1,0:T(8,128)(2,1)S(1)}, bf16[40,8,256]{2,1,0:T(8,128)(2,1)S(1)}, u32[]{:S(2)}, u32[]{:S(2)}) collective-permute-start(bf16[40,8,256]{2,1,0:T(8,128)(2,1)S(1)} %get-tuple-element.16), channel_id=1, source_target_pairs={{0,32},{16,48},{32,64},{48,80},{64,96},{80,112},{96,128},{112,144}... | collective-permute-start | bytes 491528 | tf_op jit(solution)/shard_map/ppermute | solution.py:270
  29.8 0.0 copy-done.4
  29.8 0.1 reshape.29.scales
  29.9 0.9 copy.13.innovation
  30.7 0.1 pad_add_fusion.place
  30.8 1.0 copy.15.vectors
  31.8 0.8 misfit.1.misfits
  32.6 0.0 collective-permute-done.a0
  32.6 0.0 collective-permute-done.1.a1
  32.6 1.7 %collective-permute-done.2.a3 = bf16[40,8,256]{2,1,0:T(8,128)(2,1)S(1)} collective-permute-done((bf16[40,8,256]{2,1,0:T(8,128)(2,1)S(1)}, bf16[40,8,256]{2,1,0:T(8,128)(2,1)S(1)}, u32[]{:S(2)}, u32[]{:S(2)}) %collective-permute-start.2) | collective-permute-done | bytes 163872 | tf_op jit(solution)/shard_map/ppermute | solution.py:270
  34.4 3.0 %collective-permute-done.3.a4 = bf16[40,8,256]{2,1,0:T(8,128)(2,1)S(1)} collective-permute-done((bf16[40,8,256]{2,1,0:T(8,128)(2,1)S(1)}, bf16[40,8,256]{2,1,0:T(8,128)(2,1)S(1)}, u32[]{:S(2)}, u32[]{:S(2)}) %collective-permute-start.3) | collective-permute-done | bytes 163872 | tf_op jit(solution)/shard_map/ppermute | solution.py:270
  37.4 0.0 copy-done.2
  37.4 1.7 %slots.1 = bf16[336,8,128]{2,1,0:T(8,128)(2,1)} custom-call(s32[160]{0:T(256)S(1)} %copy-done.2, bf16[40,8,256]{2,1,0:T(8,128)(2,1)S(1)} %collective-permute-done.a0, bf16[40,8,256]{2,1,0:T(8,128)(2,1)S(1)} %collective-permute-done.1.a1, bf16[40,8,256]{2,1,0:T(8,128)(2,1)S(1)} %get-tuple-element.14.a2, bf16[40,8,256]{2,1,0:T(8,128)(2,1)S(1)} %collective-permute-done.2.a3, ...), custom_call_target="tpu_custom_call" | custom-call | bytes 1310720 | tf_op jit(solution)/shard_map/slots/pallas_call | solution.py:351
  39.1 6.1 %all-to-all-done.jacobian = bf16[160,32,128]{2,1,0:T(8,128)(2,1)S(1)} async-done(((bf16[160,32,128]{2,1,0:T(8,128)(2,1)}), bf16[160,32,128]{2,1,0:T(8,128)(2,1)S(1)}, u32[]{:S(2)}, u32[]{:S(2)}) %all-to-all-start) | async-done | bytes 1310752 | tf_op jit(solution)/shard_map/all_to_all | solution.py:274
  45.2 4.2 %all-to-all-start.1 = ((bf16[336,8,128]{2,1,0:T(8,128)(2,1)}), bf16[336,8,128]{2,1,0:T(8,128)(2,1)}, u32[]{:S(2)}, u32[]{:S(2)}) async-start(bf16[336,8,128]{2,1,0:T(8,128)(2,1)} %slots.1), calls=%async_computation.1 | async-start | bytes 1376256 | tf_op jit(solution)/shard_map/all_to_all | solution.py:274
  49.4 2.3 %turn.1.turned = bf16[10,512,128]{2,1,0:T(8,128)(2,1)S(1)} custom-call(s32[2]{0:T(128)S(1)} %pad_add_fusion.place, f32[512,32]{1,0:T(8,128)S(1)} %copy.15.vectors, f32[2,256]{1,0:T(2,128)S(1)} %reshape.27.scales, bf16[160,32,128]{2,1,0:T(8,128)(2,1)S(1)} %all-to-all-done.jacobian), custom_call_target="tpu_custom_call" | custom-call | flops 671088640 | bytes 2621440 | tf_op jit(solution)/shard_map/turn/pallas_call | solution.py:364
  51.7 18.1 %all-to-all-done.1.arrived = bf16[336,8,128]{2,1,0:T(8,128)(2,1)} async-done(((bf16[336,8,128]{2,1,0:T(8,128)(2,1)}), bf16[336,8,128]{2,1,0:T(8,128)(2,1)}, u32[]{:S(2)}, u32[]{:S(2)}) %all-to-all-start.1) | async-done | bytes 688160 | tf_op jit(solution)/shard_map/all_to_all | solution.py:274
  69.8 2.7 %terms.1 = f32[448,128]{1,0:T(8,128)S(1)} custom-call(bf16[10,512,128]{2,1,0:T(8,128)(2,1)S(1)} %turn.1.turned, bf16[336,8,128]{2,1,0:T(8,128)(2,1)} %all-to-all-done.1.arrived), custom_call_target="tpu_custom_call" | custom-call | flops 1006632960 | bytes 1310720 | tf_op jit(solution)/shard_map/terms/pallas_call | solution.py:374
  72.5 0.0 copy-start.1
  72.6 17.1 %all_to_all.25 = f32[448,1,128]{2,1,0:T(1,128)S(1)} all-to-all(f32[448,1,128]{2,1,0:T(1,128)S(1)} %bitcast.15), channel_id=1, replica_groups=mesh['y'=8,'x'=4,'z'=8,'c'=2] {'x','z','c'}, dimensions={0} | all-to-all | bytes 458752 | tf_op jit(solution)/shard_map/all_to_all | solution.py:274
  89.7 13.6 %all_to_all.26.parts = f32[8,8,128]{2,1,0:T(8,128)S(1)} all-to-all(f32[8,8,128]{2,1,0:T(8,128)S(1)} %near_sum.1), channel_id=1, replica_groups=mesh['y'=8,'x'=4,'z'=8,'c'=2] {'y'}, dimensions={0} | all-to-all | bytes 65536 | tf_op jit(solution)/shard_map/all_to_all | solution.py:274
  103.3 18.5 %all_to_all.27 = f32[448,1,128]{2,1,0:T(1,128)S(1)} all-to-all(f32[448,1,128]{2,1,0:T(1,128)S(1)} %bitcast.14), channel_id=1, replica_groups=mesh['y'=8,'x'=4,'z'=8,'c'=2] {'x','z','c'}, dimensions={0} | all-to-all | bytes 458752 | tf_op jit(solution)/shard_map/all_to_all | solution.py:274
  121.8 0.0 copy-done.1
  121.8 43.6 %solve.1 = bf16[3072,256]{1,0:T(8,128)(2,1)} custom-call(f32[448,128]{1,0:T(8,128)S(1)} %bitcast.12, f32[256,256]{1,0:T(8,128)S(1)} %copy-done.1, bf16[3072,256]{1,0:T(8,128)(2,1)} %bitcast.11), custom_call_target="tpu_custom_call" | custom-call | tf_op jit(solution)/shard_map/solve/pallas_call | solution.py:388
  (5 shorter events, 0.1 us)
Async XLA Ops:
  0.0 12.0 %copy-start.3 = (s32[1,5,40]{2,0,1:T(1,128)S(1)}, s32[1,5,40]{2,0,1:T(1,128)}, u32[]{:S(2)}) copy-start(s32[1,5,40]{2,0,1:T(1,128)} %param.15) | copy-start | bytes 2404
  0.0 12.1 %copy-start = (bf16[384,8,256]{2,1,0:T(8,128)(2,1)S(1)}, bf16[384,8,256]{2,1,0:T(8,128)(2,1)}, u32[]{:S(2)}) copy-start(bf16[384,8,256]{2,1,0:T(8,128)(2,1)} %ensemble.1) | copy-start | bytes 4718596
  0.0 45.2 %all-to-all-start = ((bf16[160,32,128]{2,1,0:T(8,128)(2,1)}), bf16[160,32,128]{2,1,0:T(8,128)(2,1)S(1)}, u32[]{:S(2)}, u32[]{:S(2)}) async-start(bf16[160,32,128]{2,1,0:T(8,128)(2,1)} %param.10), calls=%async_computation | async-start | bytes 2621440 | tf_op jit(solution)/shard_map/all_to_all | solution.py:274
  12.0 17.8 %copy-start.4 = (f32[512]{0:T(512)S(1)}, f32[512]{0:T(512)}, u32[]{:S(2)}) copy-start(f32[512]{0:T(512)} %param.13) | copy-start | bytes 6148
  12.0 25.4 %copy-start.2 = (s32[160]{0:T(256)S(1)}, s32[160]{0:T(256)}, u32[]{:S(2)}) copy-start(s32[160]{0:T(256)} %slot.1) | copy-start | bytes 1924
  13.7 18.9 %collective-permute-start = (bf16[40,8,256]{2,1,0:T(8,128)(2,1)}, bf16[40,8,256]{2,1,0:T(8,128)(2,1)S(1)}, u32[]{:S(2)}, u32[]{:S(2)}) collective-permute-start(bf16[40,8,256]{2,1,0:T(8,128)(2,1)} %get-tuple-element.12), channel_id=1, source_target_pairs={{0,480},{16,496},{32,0},{48,16},{64,32},{80,48},{96,64},{112,80},{... | collective-permute-start | bytes 491528 | tf_op jit(solution)/shard_map/ppermute | solution.py:270
  21.3 11.4 %collective-permute-start.1 = (bf16[40,8,256]{2,1,0:T(8,128)(2,1)S(1)}, bf16[40,8,256]{2,1,0:T(8,128)(2,1)S(1)}, u32[]{:S(2)}, u32[]{:S(2)}) collective-permute-start(bf16[40,8,256]{2,1,0:T(8,128)(2,1)S(1)} %get-tuple-element.13), channel_id=1, source_target_pairs={{0,496},{16,0},{32,16},{48,32},{64,48},{80,64},{96,80},{112,96},{1... | collective-permute-start | bytes 491528 | tf_op jit(solution)/shard_map/ppermute | solution.py:270
  24.0 10.3 %collective-permute-start.2 = (bf16[40,8,256]{2,1,0:T(8,128)(2,1)S(1)}, bf16[40,8,256]{2,1,0:T(8,128)(2,1)S(1)}, u32[]{:S(2)}, u32[]{:S(2)}) collective-permute-start(bf16[40,8,256]{2,1,0:T(8,128)(2,1)S(1)} %get-tuple-element.15), channel_id=1, source_target_pairs={{0,16},{16,32},{32,48},{48,64},{64,80},{80,96},{96,112},{112,128},... | collective-permute-start | bytes 491528 | tf_op jit(solution)/shard_map/ppermute | solution.py:270
  26.6 10.8 %collective-permute-start.3 = (bf16[40,8,256]{2,1,0:T(8,128)(2,1)S(1)}, bf16[40,8,256]{2,1,0:T(8,128)(2,1)S(1)}, u32[]{:S(2)}, u32[]{:S(2)}) collective-permute-start(bf16[40,8,256]{2,1,0:T(8,128)(2,1)S(1)} %get-tuple-element.16), channel_id=1, source_target_pairs={{0,32},{16,48},{32,64},{48,80},{64,96},{80,112},{96,128},{112,144}... | collective-permute-start | bytes 491528 | tf_op jit(solution)/shard_map/ppermute | solution.py:270
  45.2 24.6 %all-to-all-start.1 = ((bf16[336,8,128]{2,1,0:T(8,128)(2,1)}), bf16[336,8,128]{2,1,0:T(8,128)(2,1)}, u32[]{:S(2)}, u32[]{:S(2)}) async-start(bf16[336,8,128]{2,1,0:T(8,128)(2,1)} %slots.1), calls=%async_computation.1 | async-start | bytes 1376256 | tf_op jit(solution)/shard_map/all_to_all | solution.py:274
  72.5 49.3 %copy-start.1 = (f32[256,256]{1,0:T(8,128)S(1)}, f32[256,256]{1,0:T(8,128)}, u32[]{:S(2)}) copy-start(f32[256,256]{1,0:T(8,128)} %basis.1) | copy-start | bytes 786436

commit v11 on v10

--- a/solution.py
+++ b/solution.py
@@ -11,7 +11,7 @@
 NEAR = ("x", "z", "c")
 FAR = "y"
 MEM = 256
-CHUNK = 7
+CHUNK = 5
 HI = lax.Precision.HIGHEST
 F32 = jnp.float32
 BF16 = jnp.bfloat16
@@ -148,11 +148,15 @@
         gram = gram + nt(jnp.concatenate(lefts, axis=1), jnp.concatenate(rights, axis=1))
     pull = gram[MEM : MEM + 16, :]
     total = jnp.sum(pull, axis=0, keepdims=True)
-    out[0:128, :] = gram[0:128, 0:128]
+    row, col = iota2(128, 128, 0), iota2(128, 128, 1)
+    other = gram[128:256, 128:256]
+    out[0:128, :] = jnp.where(row >= col, gram[0:128, 0:128], other)
     out[128:256, :] = gram[128:256, 0:128]
-    out[256:384, :] = gram[128:256, 128:256]
-    unused = jnp.zeros((out.shape[0] - 386, 128), F32)
-    out[384:, :] = jnp.concatenate([total[:, 0:128], total[:, 128:256], unused], axis=0)
+    diagonal = jnp.sum(jnp.where(row == col, other, 0.0), axis=0, keepdims=True)
+    unused = jnp.zeros((out.shape[0] - 259, 128), F32)
+    out[256:, :] = jnp.concatenate(
+        [diagonal, total[:, 0:128], total[:, 128:256], unused], axis=0
+    )
 
 
 def near_sum_kernel(parts, out):
@@ -201,9 +205,13 @@
     load = pltpu.make_async_copy(ensemble_far, ensemble, load_sem)
     load.start()
     eye = (iota2(MEM, MEM, 0) == iota2(MEM, MEM, 1)).astype(F32)
-    g00 = summed[0:128, :]
+    row, col = iota2(128, 128, 0), iota2(128, 128, 1)
+    shared = summed[0:128, :]
+    below = jnp.where(row > col, shared, 0.0)
+    above = jnp.where(row < col, shared, 0.0)
+    g00 = below + below.T + jnp.where(row == col, shared, 0.0)
+    g11 = above + above.T + jnp.where(row == col, summed[256:257, :], 0.0)
     g10 = summed[128:256, :]
-    g11 = summed[256:384, :]
     a = jnp.concatenate(
         [jnp.concatenate([g00, g10.T], axis=1), jnp.concatenate([g10, g11], axis=1)], axis=0
     ) + (MEM - 1.0) * eye
@@ -248,7 +256,7 @@
         inverse[...] = rows[:, MEM : 2 * MEM]
 
     x = inverse[...]
-    pull = jnp.concatenate([summed[384:385, :], summed[385:386, :]], axis=1)
+    pull = jnp.concatenate([summed[257:258, :], summed[258:259, :]], axis=1)
     halfway = jnp.sum(x * pull, axis=1, keepdims=True)
     target = (MEM - 1.0) ** 0.5 * basis[...] + halfway
     transform = nn3(x.T, target).astype(BF16)

time: 166 us -> 164 us (0.988)
  blocking collectives: 49.2 us -> 47.1 us
    all_to_all x3, blocking collectives: 49.2 us -> 47.1 us  [swap(): return lax.all_to_all(x, axis, 0, 0, tiled=True)]
where the time goes in v11:
time: 164 us; the launch traced here: 163 us
  Pallas kernels  52.9 us (32%)
  blocking collectives  47.1 us (29%)
  starting transfers between devices  31.5 us (19%)
  waiting for transfers between devices  28.9 us (18%)
  local copies, waits for them, and re-layouts  2.01 us (1%)
    all_to_all x3, blocking collectives, swap(): return lax.all_to_all(x, axis, 0, 0, tiled=True)  47.1 us
    pallas_call x1, Pallas kernels, local(): pl.pallas_call(solve_kernel, out_shape=jax.ShapeDtypeStruct(flat_rows.sha...  43.7 us
    all_to_all x2, waiting for transfers between devices, swap(): return lax.all_to_all(x, axis, 0, 0, tiled=True)  24.2 us
    all_to_all x2, starting transfers between devices, swap(): return lax.all_to_all(x, axis, 0, 0, tiled=True)  16.1 us
    ppermute x4, starting transfers between devices, send_by(): lax.ppermute(value, axis, [(s, (s + steps) % count) for s in range(count)])  15.4 us
    ppermute x4, waiting for transfers between devices, send_by(): lax.ppermute(value, axis, [(s, (s + steps) % count) for s in range(count)])  4.72 us
  transfers between devices with their start and end apart: 6, of which 4 were waited for; matrix products, arithmetic and copies ran while one was open for 1% of the time, Pallas kernels for 4%

profile of v11, /device:TPU:1, one launch (start us, length us, event | category | flops | bytes accessed | tf_op | source)
XLA Modules:
  0.0 163.4 jit_solution(5903829689609073266)
XLA Ops:
  0.0 0.0 copy-start.3
  0.0 0.0 copy-start
  0.0 12.0 %all-to-all-start = ((bf16[160,32,128]{2,1,0:T(8,128)(2,1)}), bf16[160,32,128]{2,1,0:T(8,128)(2,1)S(1)}, u32[]{:S(2)}, u32[]{:S(2)}) async-start(bf16[160,32,128]{2,1,0:T(8,128)(2,1)} %param.10), calls=%async_computation | async-start | bytes 2621440 | tf_op jit(solution)/shard_map/all_to_all | solution.py:282
  12.0 0.0 copy-done.3
  12.0 0.0 copy-start.4
  12.0 0.0 copy-start.2
  12.0 0.1 reshape.28.pick
  12.1 0.0 copy-done
  12.1 1.6 pick.1
  13.7 7.6 %collective-permute-start = (bf16[40,8,256]{2,1,0:T(8,128)(2,1)}, bf16[40,8,256]{2,1,0:T(8,128)(2,1)S(1)}, u32[]{:S(2)}, u32[]{:S(2)}) collective-permute-start(bf16[40,8,256]{2,1,0:T(8,128)(2,1)} %get-tuple-element.12), channel_id=1, source_target_pairs={{0,480},{16,496},{32,0},{48,16},{64,32},{80,48},{96,64},{112,80},{... | collective-permute-start | bytes 491528 | tf_op jit(solution)/shard_map/ppermute | solution.py:278
  21.3 2.8 %collective-permute-start.1 = (bf16[40,8,256]{2,1,0:T(8,128)(2,1)S(1)}, bf16[40,8,256]{2,1,0:T(8,128)(2,1)S(1)}, u32[]{:S(2)}, u32[]{:S(2)}) collective-permute-start(bf16[40,8,256]{2,1,0:T(8,128)(2,1)S(1)} %get-tuple-element.13), channel_id=1, source_target_pairs={{0,496},{16,0},{32,16},{48,32},{64,48},{80,64},{96,80},{112,96},{1... | collective-permute-start | bytes 491528 | tf_op jit(solution)/shard_map/ppermute | solution.py:278
  24.0 2.5 %collective-permute-start.2 = (bf16[40,8,256]{2,1,0:T(8,128)(2,1)S(1)}, bf16[40,8,256]{2,1,0:T(8,128)(2,1)S(1)}, u32[]{:S(2)}, u32[]{:S(2)}) collective-permute-start(bf16[40,8,256]{2,1,0:T(8,128)(2,1)S(1)} %get-tuple-element.15), channel_id=1, source_target_pairs={{0,16},{16,32},{32,48},{48,64},{64,80},{80,96},{96,112},{112,128},... | collective-permute-start | bytes 491528 | tf_op jit(solution)/shard_map/ppermute | solution.py:278
  26.6 2.6 %collective-permute-start.3 = (bf16[40,8,256]{2,1,0:T(8,128)(2,1)S(1)}, bf16[40,8,256]{2,1,0:T(8,128)(2,1)S(1)}, u32[]{:S(2)}, u32[]{:S(2)}) collective-permute-start(bf16[40,8,256]{2,1,0:T(8,128)(2,1)S(1)} %get-tuple-element.16), channel_id=1, source_target_pairs={{0,32},{16,48},{32,64},{48,80},{64,96},{80,112},{96,128},{112,144}... | collective-permute-start | bytes 491528 | tf_op jit(solution)/shard_map/ppermute | solution.py:278
  29.8 0.0 copy-done.4
  29.8 0.1 reshape.29.scales
  29.9 0.9 copy.13.innovation
  30.7 0.1 pad_add_fusion.place
  30.8 1.0 copy.15.vectors
  31.8 0.8 misfit.1.misfits
  32.6 0.0 collective-permute-done.a0
  32.6 0.0 collective-permute-done.1.a1
  32.6 1.7 %collective-permute-done.2.a3 = bf16[40,8,256]{2,1,0:T(8,128)(2,1)S(1)} collective-permute-done((bf16[40,8,256]{2,1,0:T(8,128)(2,1)S(1)}, bf16[40,8,256]{2,1,0:T(8,128)(2,1)S(1)}, u32[]{:S(2)}, u32[]{:S(2)}) %collective-permute-start.2) | collective-permute-done | bytes 163872 | tf_op jit(solution)/shard_map/ppermute | solution.py:278
  34.4 3.0 %collective-permute-done.3.a4 = bf16[40,8,256]{2,1,0:T(8,128)(2,1)S(1)} collective-permute-done((bf16[40,8,256]{2,1,0:T(8,128)(2,1)S(1)}, bf16[40,8,256]{2,1,0:T(8,128)(2,1)S(1)}, u32[]{:S(2)}, u32[]{:S(2)}) %collective-permute-start.3) | collective-permute-done | bytes 163872 | tf_op jit(solution)/shard_map/ppermute | solution.py:278
  37.4 0.0 copy-done.2
  37.4 1.7 %slots.1 = bf16[336,8,128]{2,1,0:T(8,128)(2,1)} custom-call(s32[160]{0:T(256)S(1)} %copy-done.2, bf16[40,8,256]{2,1,0:T(8,128)(2,1)S(1)} %collective-permute-done.a0, bf16[40,8,256]{2,1,0:T(8,128)(2,1)S(1)} %collective-permute-done.1.a1, bf16[40,8,256]{2,1,0:T(8,128)(2,1)S(1)} %get-tuple-element.14.a2, bf16[40,8,256]{2,1,0:T(8,128)(2,1)S(1)} %collective-permute-done.2.a3, ...), custom_call_target="tpu_custom_call" | custom-call | bytes 1310720 | tf_op jit(solution)/shard_map/slots/pallas_call | solution.py:359
  39.1 6.1 %all-to-all-done.jacobian = bf16[160,32,128]{2,1,0:T(8,128)(2,1)S(1)} async-done(((bf16[160,32,128]{2,1,0:T(8,128)(2,1)}), bf16[160,32,128]{2,1,0:T(8,128)(2,1)S(1)}, u32[]{:S(2)}, u32[]{:S(2)}) %all-to-all-start) | async-done | bytes 1310752 | tf_op jit(solution)/shard_map/all_to_all | solution.py:282
  45.2 4.2 %all-to-all-start.1 = ((bf16[336,8,128]{2,1,0:T(8,128)(2,1)}), bf16[336,8,128]{2,1,0:T(8,128)(2,1)}, u32[]{:S(2)}, u32[]{:S(2)}) async-start(bf16[336,8,128]{2,1,0:T(8,128)(2,1)} %slots.1), calls=%async_computation.1 | async-start | bytes 1376256 | tf_op jit(solution)/shard_map/all_to_all | solution.py:282
  49.4 2.3 %turn.1.turned = bf16[10,512,128]{2,1,0:T(8,128)(2,1)S(1)} custom-call(s32[2]{0:T(128)S(1)} %pad_add_fusion.place, f32[512,32]{1,0:T(8,128)S(1)} %copy.15.vectors, f32[2,256]{1,0:T(2,128)S(1)} %reshape.27.scales, bf16[160,32,128]{2,1,0:T(8,128)(2,1)S(1)} %all-to-all-done.jacobian), custom_call_target="tpu_custom_call" | custom-call | flops 671088640 | bytes 2621440 | tf_op jit(solution)/shard_map/turn/pallas_call | solution.py:372
  51.7 0.0 copy-start.1
  51.7 18.1 %all-to-all-done.1.arrived = bf16[336,8,128]{2,1,0:T(8,128)(2,1)} async-done(((bf16[336,8,128]{2,1,0:T(8,128)(2,1)}), bf16[336,8,128]{2,1,0:T(8,128)(2,1)}, u32[]{:S(2)}, u32[]{:S(2)}) %all-to-all-start.1) | async-done | bytes 688160 | tf_op jit(solution)/shard_map/all_to_all | solution.py:282
  69.8 2.7 %terms.1 = f32[320,128]{1,0:T(8,128)S(1)} custom-call(bf16[10,512,128]{2,1,0:T(8,128)(2,1)S(1)} %turn.1.turned, bf16[336,8,128]{2,1,0:T(8,128)(2,1)} %all-to-all-done.1.arrived), custom_call_target="tpu_custom_call" | custom-call | flops 1006632960 | bytes 1310720 | tf_op jit(solution)/shard_map/terms/pallas_call | solution.py:382
  72.5 16.5 %all_to_all.25 = f32[320,1,128]{2,1,0:T(1,128)S(1)} all-to-all(f32[320,1,128]{2,1,0:T(1,128)S(1)} %bitcast.15), channel_id=1, replica_groups=mesh['y'=8,'x'=4,'z'=8,'c'=2] {'x','z','c'}, dimensions={0} | all-to-all | bytes 327680 | tf_op jit(solution)/shard_map/all_to_all | solution.py:282
  89.0 13.6 %all_to_all.26.parts = f32[8,8,128]{2,1,0:T(8,128)S(1)} all-to-all(f32[8,8,128]{2,1,0:T(8,128)S(1)} %near_sum.1), channel_id=1, replica_groups=mesh['y'=8,'x'=4,'z'=8,'c'=2] {'y'}, dimensions={0} | all-to-all | bytes 65536 | tf_op jit(solution)/shard_map/all_to_all | solution.py:282
  102.6 17.1 %all_to_all.27 = f32[320,1,128]{2,1,0:T(1,128)S(1)} all-to-all(f32[320,1,128]{2,1,0:T(1,128)S(1)} %bitcast.14), channel_id=1, replica_groups=mesh['y'=8,'x'=4,'z'=8,'c'=2] {'x','z','c'}, dimensions={0} | all-to-all | bytes 327680 | tf_op jit(solution)/shard_map/all_to_all | solution.py:282
  119.7 0.0 copy-done.1
  119.7 43.7 %solve.1 = bf16[3072,256]{1,0:T(8,128)(2,1)} custom-call(f32[320,128]{1,0:T(8,128)S(1)} %bitcast.12, f32[256,256]{1,0:T(8,128)S(1)} %copy-done.1, bf16[3072,256]{1,0:T(8,128)(2,1)} %bitcast.11), custom_call_target="tpu_custom_call" | custom-call | tf_op jit(solution)/shard_map/solve/pallas_call | solution.py:396
  (5 shorter events, 0.1 us)
Async XLA Ops:
  0.0 12.0 %copy-start.3 = (s32[1,5,40]{2,0,1:T(1,128)S(1)}, s32[1,5,40]{2,0,1:T(1,128)}, u32[]{:S(2)}) copy-start(s32[1,5,40]{2,0,1:T(1,128)} %param.15) | copy-start | bytes 2404
  0.0 12.1 %copy-start = (bf16[384,8,256]{2,1,0:T(8,128)(2,1)S(1)}, bf16[384,8,256]{2,1,0:T(8,128)(2,1)}, u32[]{:S(2)}) copy-start(bf16[384,8,256]{2,1,0:T(8,128)(2,1)} %ensemble.1) | copy-start | bytes 4718596
  0.0 45.2 %all-to-all-start = ((bf16[160,32,128]{2,1,0:T(8,128)(2,1)}), bf16[160,32,128]{2,1,0:T(8,128)(2,1)S(1)}, u32[]{:S(2)}, u32[]{:S(2)}) async-start(bf16[160,32,128]{2,1,0:T(8,128)(2,1)} %param.10), calls=%async_computation | async-start | bytes 2621440 | tf_op jit(solution)/shard_map/all_to_all | solution.py:282
  12.0 17.8 %copy-start.4 = (f32[512]{0:T(512)S(1)}, f32[512]{0:T(512)}, u32[]{:S(2)}) copy-start(f32[512]{0:T(512)} %param.13) | copy-start | bytes 6148
  12.0 25.4 %copy-start.2 = (s32[160]{0:T(256)S(1)}, s32[160]{0:T(256)}, u32[]{:S(2)}) copy-start(s32[160]{0:T(256)} %slot.1) | copy-start | bytes 1924
  13.7 18.9 %collective-permute-start = (bf16[40,8,256]{2,1,0:T(8,128)(2,1)}, bf16[40,8,256]{2,1,0:T(8,128)(2,1)S(1)}, u32[]{:S(2)}, u32[]{:S(2)}) collective-permute-start(bf16[40,8,256]{2,1,0:T(8,128)(2,1)} %get-tuple-element.12), channel_id=1, source_target_pairs={{0,480},{16,496},{32,0},{48,16},{64,32},{80,48},{96,64},{112,80},{... | collective-permute-start | bytes 491528 | tf_op jit(solution)/shard_map/ppermute | solution.py:278
  21.3 11.4 %collective-permute-start.1 = (bf16[40,8,256]{2,1,0:T(8,128)(2,1)S(1)}, bf16[40,8,256]{2,1,0:T(8,128)(2,1)S(1)}, u32[]{:S(2)}, u32[]{:S(2)}) collective-permute-start(bf16[40,8,256]{2,1,0:T(8,128)(2,1)S(1)} %get-tuple-element.13), channel_id=1, source_target_pairs={{0,496},{16,0},{32,16},{48,32},{64,48},{80,64},{96,80},{112,96},{1... | collective-permute-start | bytes 491528 | tf_op jit(solution)/shard_map/ppermute | solution.py:278
  24.0 10.3 %collective-permute-start.2 = (bf16[40,8,256]{2,1,0:T(8,128)(2,1)S(1)}, bf16[40,8,256]{2,1,0:T(8,128)(2,1)S(1)}, u32[]{:S(2)}, u32[]{:S(2)}) collective-permute-start(bf16[40,8,256]{2,1,0:T(8,128)(2,1)S(1)} %get-tuple-element.15), channel_id=1, source_target_pairs={{0,16},{16,32},{32,48},{48,64},{64,80},{80,96},{96,112},{112,128},... | collective-permute-start | bytes 491528 | tf_op jit(solution)/shard_map/ppermute | solution.py:278
  26.6 10.8 %collective-permute-start.3 = (bf16[40,8,256]{2,1,0:T(8,128)(2,1)S(1)}, bf16[40,8,256]{2,1,0:T(8,128)(2,1)S(1)}, u32[]{:S(2)}, u32[]{:S(2)}) collective-permute-start(bf16[40,8,256]{2,1,0:T(8,128)(2,1)S(1)} %get-tuple-element.16), channel_id=1, source_target_pairs={{0,32},{16,48},{32,64},{48,80},{64,96},{80,112},{96,128},{112,144}... | collective-permute-start | bytes 491528 | tf_op jit(solution)/shard_map/ppermute | solution.py:278
  45.2 24.6 %all-to-all-start.1 = ((bf16[336,8,128]{2,1,0:T(8,128)(2,1)}), bf16[336,8,128]{2,1,0:T(8,128)(2,1)}, u32[]{:S(2)}, u32[]{:S(2)}) async-start(bf16[336,8,128]{2,1,0:T(8,128)(2,1)} %slots.1), calls=%async_computation.1 | async-start | bytes 1376256 | tf_op jit(solution)/shard_map/all_to_all | solution.py:282
  51.7 68.0 %copy-start.1 = (f32[256,256]{1,0:T(8,128)S(1)}, f32[256,256]{1,0:T(8,128)}, u32[]{:S(2)}) copy-start(f32[256,256]{1,0:T(8,128)} %basis.1) | copy-start | bytes 786436

commit v12 on v11

--- a/solution.py
+++ b/solution.py
@@ -167,13 +167,13 @@
     y = x[0:CHUNK, :]
     for k in range(1, 8):
         y = y + x[k * CHUNK : (k + 1) * CHUNK, :]
-    tile = jnp.concatenate([y, jnp.zeros((8 - CHUNK, 128), F32)], axis=0)
-    for k in range(out.shape[0]):
-        out[k] = tile
+    out[...] = jnp.concatenate([y] * (out.shape[0] // CHUNK), axis=0)
 
 
 def far_sum_kernel(parts, out):
-    y = jnp.sum(parts[...], axis=0)[0:CHUNK, :]
+    y = parts[0:CHUNK, :]
+    for k in range(1, parts.shape[0] // CHUNK):
+        y = y + parts[k * CHUNK : (k + 1) * CHUNK, :]
     x = jnp.concatenate([y] * 8, axis=0)
     span = 8 * CHUNK
     for k in range(out.shape[0] // span):
@@ -290,7 +290,7 @@
     far = lax.axis_size(FAR)
     mine = pl.pallas_call(
         near_sum_kernel,
-        out_shape=jax.ShapeDtypeStruct((far, 8, 128), F32),
+        out_shape=jax.ShapeDtypeStruct((far * CHUNK, 128), F32),
         in_specs=[VM],
         out_specs=VM,
         compiler_params=grant(20),
@@ -303,7 +303,7 @@
         out_specs=VM,
         compiler_params=grant(20),
         name="far_sum",
-    )(swap(mine, FAR))
+    )(swap_rows(mine, FAR))
     return swap_rows(mine, NEAR)
 
 

time: 164 us -> 164 us (level)
  no operation moved by 1% of the time
where the time goes in v12:
time: 164 us; the launch traced here: 163 us
  Pallas kernels  52.9 us (32%)
  blocking collectives  46.9 us (29%)
  starting transfers between devices  31.5 us (19%)
  waiting for transfers between devices  28.9 us (18%)
  local copies, waits for them, and re-layouts  2.01 us (1%)
    all_to_all x3, blocking collectives, swap(): return lax.all_to_all(x, axis, 0, 0, tiled=True)  46.9 us
    pallas_call x1, Pallas kernels, local(): pl.pallas_call(solve_kernel, out_shape=jax.ShapeDtypeStruct(flat_rows.sha...  43.7 us
    all_to_all x2, waiting for transfers between devices, swap(): return lax.all_to_all(x, axis, 0, 0, tiled=True)  24.2 us
    all_to_all x2, starting transfers between devices, swap(): return lax.all_to_all(x, axis, 0, 0, tiled=True)  16.1 us
    ppermute x4, starting transfers between devices, send_by(): lax.ppermute(value, axis, [(s, (s + steps) % count) for s in range(count)])  15.4 us
    ppermute x4, waiting for transfers between devices, send_by(): lax.ppermute(value, axis, [(s, (s + steps) % count) for s in range(count)])  4.72 us
  transfers between devices with their start and end apart: 6, of which 4 were waited for; matrix products, arithmetic and copies ran while one was open for 1% of the time, Pallas kernels for 4%

profile of v12, /device:TPU:1, one launch (start us, length us, event | category | flops | bytes accessed | tf_op | source)
XLA Modules:
  0.0 163.1 jit_solution(11900027224777998015)
XLA Ops:
  0.0 0.0 copy-start.3
  0.0 0.0 copy-start
  0.0 12.0 %all-to-all-start = ((bf16[160,32,128]{2,1,0:T(8,128)(2,1)}), bf16[160,32,128]{2,1,0:T(8,128)(2,1)S(1)}, u32[]{:S(2)}, u32[]{:S(2)}) async-start(bf16[160,32,128]{2,1,0:T(8,128)(2,1)} %param.10), calls=%async_computation | async-start | bytes 2621440 | tf_op jit(solution)/shard_map/all_to_all | solution.py:282
  12.0 0.0 copy-done.3
  12.0 0.0 copy-start.4
  12.0 0.0 copy-start.2
  12.0 0.1 reshape.34.pick
  12.1 0.0 copy-done
  12.1 1.6 pick.1
  13.7 7.6 %collective-permute-start = (bf16[40,8,256]{2,1,0:T(8,128)(2,1)}, bf16[40,8,256]{2,1,0:T(8,128)(2,1)S(1)}, u32[]{:S(2)}, u32[]{:S(2)}) collective-permute-start(bf16[40,8,256]{2,1,0:T(8,128)(2,1)} %get-tuple-element.12), channel_id=1, source_target_pairs={{0,480},{16,496},{32,0},{48,16},{64,32},{80,48},{96,64},{112,80},{... | collective-permute-start | bytes 491528 | tf_op jit(solution)/shard_map/ppermute | solution.py:278
  21.3 2.8 %collective-permute-start.1 = (bf16[40,8,256]{2,1,0:T(8,128)(2,1)S(1)}, bf16[40,8,256]{2,1,0:T(8,128)(2,1)S(1)}, u32[]{:S(2)}, u32[]{:S(2)}) collective-permute-start(bf16[40,8,256]{2,1,0:T(8,128)(2,1)S(1)} %get-tuple-element.13), channel_id=1, source_target_pairs={{0,496},{16,0},{32,16},{48,32},{64,48},{80,64},{96,80},{112,96},{1... | collective-permute-start | bytes 491528 | tf_op jit(solution)/shard_map/ppermute | solution.py:278
  24.0 2.5 %collective-permute-start.2 = (bf16[40,8,256]{2,1,0:T(8,128)(2,1)S(1)}, bf16[40,8,256]{2,1,0:T(8,128)(2,1)S(1)}, u32[]{:S(2)}, u32[]{:S(2)}) collective-permute-start(bf16[40,8,256]{2,1,0:T(8,128)(2,1)S(1)} %get-tuple-element.15), channel_id=1, source_target_pairs={{0,16},{16,32},{32,48},{48,64},{64,80},{80,96},{96,112},{112,128},... | collective-permute-start | bytes 491528 | tf_op jit(solution)/shard_map/ppermute | solution.py:278
  26.6 2.6 %collective-permute-start.3 = (bf16[40,8,256]{2,1,0:T(8,128)(2,1)S(1)}, bf16[40,8,256]{2,1,0:T(8,128)(2,1)S(1)}, u32[]{:S(2)}, u32[]{:S(2)}) collective-permute-start(bf16[40,8,256]{2,1,0:T(8,128)(2,1)S(1)} %get-tuple-element.16), channel_id=1, source_target_pairs={{0,32},{16,48},{32,64},{48,80},{64,96},{80,112},{96,128},{112,144}... | collective-permute-start | bytes 491528 | tf_op jit(solution)/shard_map/ppermute | solution.py:278
  29.8 0.0 copy-done.4
  29.8 0.1 reshape.35.scales
  29.9 0.9 copy.13.innovation
  30.7 0.1 pad_add_fusion.place
  30.8 1.0 copy.15.vectors
  31.8 0.8 misfit.1.misfits
  32.6 0.0 collective-permute-done.a0
  32.6 0.0 collective-permute-done.1.a1
  32.6 1.7 %collective-permute-done.2.a3 = bf16[40,8,256]{2,1,0:T(8,128)(2,1)S(1)} collective-permute-done((bf16[40,8,256]{2,1,0:T(8,128)(2,1)S(1)}, bf16[40,8,256]{2,1,0:T(8,128)(2,1)S(1)}, u32[]{:S(2)}, u32[]{:S(2)}) %collective-permute-start.2) | collective-permute-done | bytes 163872 | tf_op jit(solution)/shard_map/ppermute | solution.py:278
  34.4 3.0 %collective-permute-done.3.a4 = bf16[40,8,256]{2,1,0:T(8,128)(2,1)S(1)} collective-permute-done((bf16[40,8,256]{2,1,0:T(8,128)(2,1)S(1)}, bf16[40,8,256]{2,1,0:T(8,128)(2,1)S(1)}, u32[]{:S(2)}, u32[]{:S(2)}) %collective-permute-start.3) | collective-permute-done | bytes 163872 | tf_op jit(solution)/shard_map/ppermute | solution.py:278
  37.4 0.0 copy-done.2
  37.4 1.7 %slots.1 = bf16[336,8,128]{2,1,0:T(8,128)(2,1)} custom-call(s32[160]{0:T(256)S(1)} %copy-done.2, bf16[40,8,256]{2,1,0:T(8,128)(2,1)S(1)} %collective-permute-done.a0, bf16[40,8,256]{2,1,0:T(8,128)(2,1)S(1)} %collective-permute-done.1.a1, bf16[40,8,256]{2,1,0:T(8,128)(2,1)S(1)} %get-tuple-element.14.a2, bf16[40,8,256]{2,1,0:T(8,128)(2,1)S(1)} %collective-permute-done.2.a3, ...), custom_call_target="tpu_custom_call" | custom-call | bytes 1310720 | tf_op jit(solution)/shard_map/slots/pallas_call | solution.py:359
  39.1 6.1 %all-to-all-done.jacobian = bf16[160,32,128]{2,1,0:T(8,128)(2,1)S(1)} async-done(((bf16[160,32,128]{2,1,0:T(8,128)(2,1)}), bf16[160,32,128]{2,1,0:T(8,128)(2,1)S(1)}, u32[]{:S(2)}, u32[]{:S(2)}) %all-to-all-start) | async-done | bytes 1310752 | tf_op jit(solution)/shard_map/all_to_all | solution.py:282
  45.2 4.2 %all-to-all-start.1 = ((bf16[336,8,128]{2,1,0:T(8,128)(2,1)}), bf16[336,8,128]{2,1,0:T(8,128)(2,1)}, u32[]{:S(2)}, u32[]{:S(2)}) async-start(bf16[336,8,128]{2,1,0:T(8,128)(2,1)} %slots.1), calls=%async_computation.1 | async-start | bytes 1376256 | tf_op jit(solution)/shard_map/all_to_all | solution.py:282
  49.4 2.3 %turn.1.turned = bf16[10,512,128]{2,1,0:T(8,128)(2,1)S(1)} custom-call(s32[2]{0:T(128)S(1)} %pad_add_fusion.place, f32[512,32]{1,0:T(8,128)S(1)} %copy.15.vectors, f32[2,256]{1,0:T(2,128)S(1)} %reshape.33.scales, bf16[160,32,128]{2,1,0:T(8,128)(2,1)S(1)} %all-to-all-done.jacobian), custom_call_target="tpu_custom_call" | custom-call | flops 671088640 | bytes 2621440 | tf_op jit(solution)/shard_map/turn/pallas_call | solution.py:372
  51.7 0.0 copy-start.1
  51.7 18.1 %all-to-all-done.1.arrived = bf16[336,8,128]{2,1,0:T(8,128)(2,1)} async-done(((bf16[336,8,128]{2,1,0:T(8,128)(2,1)}), bf16[336,8,128]{2,1,0:T(8,128)(2,1)}, u32[]{:S(2)}, u32[]{:S(2)}) %all-to-all-start.1) | async-done | bytes 688160 | tf_op jit(solution)/shard_map/all_to_all | solution.py:282
  69.8 2.7 %terms.1 = f32[320,128]{1,0:T(8,128)S(1)} custom-call(bf16[10,512,128]{2,1,0:T(8,128)(2,1)S(1)} %turn.1.turned, bf16[336,8,128]{2,1,0:T(8,128)(2,1)} %all-to-all-done.1.arrived), custom_call_target="tpu_custom_call" | custom-call | flops 1006632960 | bytes 1310720 | tf_op jit(solution)/shard_map/terms/pallas_call | solution.py:382
  72.5 16.5 %all_to_all.25 = f32[320,1,128]{2,1,0:T(1,128)S(1)} all-to-all(f32[320,1,128]{2,1,0:T(1,128)S(1)} %bitcast.19), channel_id=1, replica_groups=mesh['y'=8,'x'=4,'z'=8,'c'=2] {'x','z','c'}, dimensions={0} | all-to-all | bytes 327680 | tf_op jit(solution)/shard_map/all_to_all | solution.py:282
  89.0 13.3 %all_to_all.26 = f32[40,1,128]{2,1,0:T(1,128)S(1)} all-to-all(f32[40,1,128]{2,1,0:T(1,128)S(1)} %bitcast.20), channel_id=1, replica_groups=mesh['y'=8,'x'=4,'z'=8,'c'=2] {'y'}, dimensions={0} | all-to-all | bytes 40960 | tf_op jit(solution)/shard_map/all_to_all | solution.py:282
  102.3 17.2 %all_to_all.27 = f32[320,1,128]{2,1,0:T(1,128)S(1)} all-to-all(f32[320,1,128]{2,1,0:T(1,128)S(1)} %bitcast.18), channel_id=1, replica_groups=mesh['y'=8,'x'=4,'z'=8,'c'=2] {'x','z','c'}, dimensions={0} | all-to-all | bytes 327680 | tf_op jit(solution)/shard_map/all_to_all | solution.py:282
  119.5 0.0 copy-done.1
  119.5 43.7 %solve.1 = bf16[3072,256]{1,0:T(8,128)(2,1)} custom-call(f32[320,128]{1,0:T(8,128)S(1)} %bitcast.16, f32[256,256]{1,0:T(8,128)S(1)} %copy-done.1, bf16[3072,256]{1,0:T(8,128)(2,1)} %bitcast.15), custom_call_target="tpu_custom_call" | custom-call | tf_op jit(solution)/shard_map/solve/pallas_call | solution.py:396
  (5 shorter events, 0.1 us)
Async XLA Ops:
  0.0 12.0 %copy-start.3 = (s32[1,5,40]{2,0,1:T(1,128)S(1)}, s32[1,5,40]{2,0,1:T(1,128)}, u32[]{:S(2)}) copy-start(s32[1,5,40]{2,0,1:T(1,128)} %param.15) | copy-start | bytes 2404
  0.0 12.1 %copy-start = (bf16[384,8,256]{2,1,0:T(8,128)(2,1)S(1)}, bf16[384,8,256]{2,1,0:T(8,128)(2,1)}, u32[]{:S(2)}) copy-start(bf16[384,8,256]{2,1,0:T(8,128)(2,1)} %ensemble.1) | copy-start | bytes 4718596
  0.0 45.2 %all-to-all-start = ((bf16[160,32,128]{2,1,0:T(8,128)(2,1)}), bf16[160,32,128]{2,1,0:T(8,128)(2,1)S(1)}, u32[]{:S(2)}, u32[]{:S(2)}) async-start(bf16[160,32,128]{2,1,0:T(8,128)(2,1)} %param.10), calls=%async_computation | async-start | bytes 2621440 | tf_op jit(solution)/shard_map/all_to_all | solution.py:282
  12.0 17.8 %copy-start.4 = (f32[512]{0:T(512)S(1)}, f32[512]{0:T(512)}, u32[]{:S(2)}) copy-start(f32[512]{0:T(512)} %param.13) | copy-start | bytes 6148
  12.0 25.4 %copy-start.2 = (s32[160]{0:T(256)S(1)}, s32[160]{0:T(256)}, u32[]{:S(2)}) copy-start(s32[160]{0:T(256)} %slot.1) | copy-start | bytes 1924
  13.7 18.9 %collective-permute-start = (bf16[40,8,256]{2,1,0:T(8,128)(2,1)}, bf16[40,8,256]{2,1,0:T(8,128)(2,1)S(1)}, u32[]{:S(2)}, u32[]{:S(2)}) collective-permute-start(bf16[40,8,256]{2,1,0:T(8,128)(2,1)} %get-tuple-element.12), channel_id=1, source_target_pairs={{0,480},{16,496},{32,0},{48,16},{64,32},{80,48},{96,64},{112,80},{... | collective-permute-start | bytes 491528 | tf_op jit(solution)/shard_map/ppermute | solution.py:278
  21.3 11.4 %collective-permute-start.1 = (bf16[40,8,256]{2,1,0:T(8,128)(2,1)S(1)}, bf16[40,8,256]{2,1,0:T(8,128)(2,1)S(1)}, u32[]{:S(2)}, u32[]{:S(2)}) collective-permute-start(bf16[40,8,256]{2,1,0:T(8,128)(2,1)S(1)} %get-tuple-element.13), channel_id=1, source_target_pairs={{0,496},{16,0},{32,16},{48,32},{64,48},{80,64},{96,80},{112,96},{1... | collective-permute-start | bytes 491528 | tf_op jit(solution)/shard_map/ppermute | solution.py:278
  24.0 10.3 %collective-permute-start.2 = (bf16[40,8,256]{2,1,0:T(8,128)(2,1)S(1)}, bf16[40,8,256]{2,1,0:T(8,128)(2,1)S(1)}, u32[]{:S(2)}, u32[]{:S(2)}) collective-permute-start(bf16[40,8,256]{2,1,0:T(8,128)(2,1)S(1)} %get-tuple-element.15), channel_id=1, source_target_pairs={{0,16},{16,32},{32,48},{48,64},{64,80},{80,96},{96,112},{112,128},... | collective-permute-start | bytes 491528 | tf_op jit(solution)/shard_map/ppermute | solution.py:278
  26.6 10.8 %collective-permute-start.3 = (bf16[40,8,256]{2,1,0:T(8,128)(2,1)S(1)}, bf16[40,8,256]{2,1,0:T(8,128)(2,1)S(1)}, u32[]{:S(2)}, u32[]{:S(2)}) collective-permute-start(bf16[40,8,256]{2,1,0:T(8,128)(2,1)S(1)} %get-tuple-element.16), channel_id=1, source_target_pairs={{0,32},{16,48},{32,64},{48,80},{64,96},{80,112},{96,128},{112,144}... | collective-permute-start | bytes 491528 | tf_op jit(solution)/shard_map/ppermute | solution.py:278
  45.2 24.6 %all-to-all-start.1 = ((bf16[336,8,128]{2,1,0:T(8,128)(2,1)}), bf16[336,8,128]{2,1,0:T(8,128)(2,1)}, u32[]{:S(2)}, u32[]{:S(2)}) async-start(bf16[336,8,128]{2,1,0:T(8,128)(2,1)} %slots.1), calls=%async_computation.1 | async-start | bytes 1376256 | tf_op jit(solution)/shard_map/all_to_all | solution.py:282
  51.7 67.8 %copy-start.1 = (f32[256,256]{1,0:T(8,128)S(1)}, f32[256,256]{1,0:T(8,128)}, u32[]{:S(2)}) copy-start(f32[256,256]{1,0:T(8,128)} %basis.1) | copy-start | bytes 786436
